TPU v7x, 32 devices: a whole 2x2x4 slice. The times are simulated.
32 devices in a mesh: sec: 2 (over core), dom: 8 (over z, y), lev: 2 (over x).
Axes of the slice: x: 2, y: 2, z: 4, core: 2. Of those that a mesh axis runs over, the one named last changes fastest.
Arguments:
- sections: float32 [2, 12, 90, 2048], P('sec', None, 'lev', 'dom'), may hold values from -6 to 6
- neighbours: int32 [3, 2048], P(None, 'dom'), may hold values from 0 to 767, as said below
- edge_weight: float32 [3, 2048], P(None, 'dom'), may hold values from 0.05 to 0.3
- field_diff: float32 [12], replicated, may hold values from 0.3 to 1
- vert_coef: float32 [90, 2048], P('lev', 'dom'), may hold values from 1 to 300
- relax_rate: float32 [12], replicated, may hold values from 0.05 to 0.5
- precip_mask: int32 [2, 2048], P(None, 'dom'), may hold values from 0 to 1, as said below
Outputs:
- final: float32 [2, 12, 90, 2048], P('sec', None, 'lev', 'dom')
Inputs may be any that keep to these rules, and one draw needn't show every extreme that they name: neighbours[j, c] is a position p in the block of 256 cells holding c, extended by the last 256 cells of the block before and the first 256 of the block after (the cell order closes around the sphere); p names the cell given by cell_neighbour and differs from the position of c by 1 to 256. `precip_mask`: for every step and every block b below 4, the blocks of 256 cells numbered b and b + 4 hold together at most 256 precipitating columns; in every step one block precipitates in all its columns.
All inputs are finite; a program needn't handle non-finite values.
Results may differ from a plain program's by a relative error of at most 0.0031.
Values may be sent and summed in bfloat16 or wider, within the bound.
No kernel may reach another device: no remote copies, remote signals or barrier semaphores. Data moves between devices by JAX's collectives and lax.ppermute only.
A program may use at most 64 MiB of HBM per device.

v0:
```python
import jax
import jax.numpy as jnp
from jax import lax
from jax.sharding import PartitionSpec as P

HALO = 256
STEPS = 2


def from_partner(array, axis, stride):
    return lax.ppermute(array, axis, [(i, i ^ 1 << stride) for i in range(lax.axis_size(axis))])


def padded(cells, sides, width):
    for axis, dim in sides:
        count = lax.axis_size(axis)
        head = lax.slice_in_dim(cells, 0, width, axis=dim)
        tail = lax.slice_in_dim(cells, cells.shape[dim] - width, cells.shape[dim], axis=dim)
        cells = jnp.concatenate(
            [
                lax.ppermute(tail, axis, [(i, (i + 1) % count) for i in range(count)]),
                cells,
                lax.ppermute(head, axis, [((i + 1) % count, i) for i in range(count)]),
            ],
            axis=dim,
        )
    return cells


def shortened(array):
    return jax.tree.map(lambda a: a.astype(jnp.bfloat16) if a.dtype == jnp.float32 else a, array)


def column_coefficients(kappa):
    zero_row = jnp.zeros((1, kappa.shape[1]), jnp.float32)
    above = jnp.concatenate([zero_row, kappa[:-1]], axis=0)
    lower = -above
    diagonal = 1.0 + above + kappa
    upper = jnp.concatenate([-kappa[:-1], zero_row], axis=0)
    return (lower, diagonal, upper)


def thomas_fields(lower, diagonal, upper, rights):
    count = len(rights)
    depth = lower.shape[0]
    prev_ratio = jnp.zeros(lower.shape[1:], jnp.float32)
    prev_values = [jnp.zeros(lower.shape[1:], jnp.float32) for index in range(count)]
    ratios = []
    values = [[] for index in range(count)]
    for level in range(depth):
        lower_k = lower[level]
        denom = diagonal[level] - lower_k * prev_ratio
        prev_ratio = upper[level] / denom
        ratios.append(prev_ratio)
        for index in range(count):
            prev_values[index] = (rights[index][level] - lower_k * prev_values[index]) / denom
            values[index].append(prev_values[index])
    solutions = []
    for index in range(count):
        after = jnp.zeros(lower.shape[1:], jnp.float32)
        rows = [None] * depth
        for level in range(depth - 1, -1, -1):
            after = values[index][level] - ratios[level] * after
            rows[level] = after
        solutions.append(jnp.stack(rows))
    return tuple(solutions)


def microphysics(moist):
    theta, vapour, cloud, rain = (moist[0], moist[1], moist[2], moist[3])
    saturation = 0.6 * jnp.exp(0.25 * theta)
    condense = 0.5 * jnp.tanh(vapour - saturation)
    autoconv = 0.4 * cloud * cloud / (1.0 + cloud * cloud)
    evaporate = 0.3 * rain * rain / (1.0 + rain * rain) * jax.nn.sigmoid(saturation - vapour)
    return jnp.stack(
        [
            2.5 * (condense - evaporate),
            evaporate - condense,
            condense - autoconv,
            autoconv - evaporate,
        ]
    )


def skip_micro(moist):
    return jnp.zeros(moist.shape, jnp.float32)


def run_micro(moist):
    return microphysics(moist.astype(jnp.float32))


def shards(sections, neighbours, edge_weight, field_diff, vert_coef, relax_rate, precip_mask):
    is_dyn = lax.axis_index("sec") == 0
    lev_rank = lax.axis_index("lev")
    mine = sections[0]
    levels = mine.shape[1]

    def run_horizontal(operand):
        extended, own = operand
        total = jnp.zeros_like(own)
        for edge in range(3):
            total = total + edge_weight[edge][None, None] * (
                jnp.take(extended, neighbours[edge], axis=2) - own
            )
        return own + field_diff[:, None, None] * total

    def skip_horizontal(operand):
        return jnp.zeros_like(operand[1])

    for step_index in range(STEPS):
        sent = lax.optimization_barrier(mine.astype(jnp.bfloat16))
        received = from_partner(sent, "sec", 0)
        physics_in = jnp.where(is_dyn, sent, received)
        extended = padded(mine, (("dom", 2),), HALO)
        smoothed = lax.cond(is_dyn, run_horizontal, skip_horizontal, (extended, mine))
        whole_right, whole_kappa = (
            lax.all_gather(shortened(smoothed[0:2]), "lev", axis=1, tiled=True),
            lax.all_gather(vert_coef.astype(jnp.bfloat16), "lev", axis=0, tiled=True).astype(
                vert_coef.dtype
            ),
        )

        def whole_solve(operand):
            right_pair, kappa_whole = operand
            lower_w, diag_w, upper_w = column_coefficients(kappa_whole)
            first_sol, second_sol = thomas_fields(
                lower_w, diag_w, upper_w, (right_pair[0], right_pair[1])
            )
            return jnp.stack([first_sol, second_sol])

        def skip_whole(operand):
            return jnp.zeros(operand[0].shape, jnp.float32)

        solved = lax.cond(is_dyn, whole_solve, skip_whole, (whole_right, whole_kappa))
        own_rows = jnp.where(lev_rank == 0, solved[:, :levels], solved[:, levels:])
        new_state = jnp.concatenate([own_rows, smoothed[2:]], axis=0) + received.astype(jnp.float32)
        mask_now = precip_mask[step_index]
        moist_in = physics_in[1:5]
        clear = -relax_rate[:, None, None] * physics_in.astype(jnp.float32)
        micro_full = lax.cond(is_dyn, skip_micro, run_micro, moist_in)
        moist_tend = jnp.where(mask_now[None, None] == 1, clear[1:5] + micro_full, clear[1:5])
        tendency = jnp.concatenate([clear[0:1], moist_tend, clear[5:]], axis=0)
        mine = jnp.where(is_dyn, new_state, tendency)
    return mine[None]


def solution(mesh):
    return jax.shard_map(
        shards,
        mesh=mesh,
        in_specs=(
            P("sec", None, "lev", "dom"),
            P(None, "dom"),
            P(None, "dom"),
            P(),
            P("lev", "dom"),
            P(),
            P(None, "dom"),
        ),
        out_specs=P("sec", None, "lev", "dom"),
        check_vma=False,
    )
```

profile of v0, /device:TPU:0, one launch (start us, length us, event | category | flops | bytes accessed | tf_op | source)
XLA Modules:
  0.0 150.4 jit_solution(2954051595688005377)
XLA Ops:
  0.0 1.1 copy.46
  1.1 3.0 %collective-permute-start = (f32[12,45,256]{2,1,0:T(8,128)S(1)}, f32[12,45,256]{2,1,0:T(8,128)S(1)}, u32[]{:S(2)}, u32[]{:S(2)}) collective-permute-start(f32[12,45,256]{2,1,0:T(8,128)S(1)} %bitcast.3674), channel_id=1, source_target_pairs={{0,2},{2,4},{4,6},{6,8},{8,10},{10,12},{12,14},{14,0},{1,3},{3,5},... | collective-permute-start | bytes 1658888 | tf_op jit(solution)/shard_map/ppermute | solution.py:21
  4.1 3.1 %collective-permute-start.1 = (f32[12,45,256]{2,1,0:T(8,128)S(1)}, f32[12,45,256]{2,1,0:T(8,128)}, u32[]{:S(2)}, u32[]{:S(2)}) collective-permute-start(f32[12,45,256]{2,1,0:T(8,128)S(1)} %bitcast.3675), channel_id=1, source_target_pairs={{2,0},{4,2},{6,4},{8,6},{10,8},{12,10},{14,12},{0,14},{3,1},{5,3},... | collective-permute-start | bytes 1658888 | tf_op jit(solution)/shard_map/ppermute | solution.py:23
  7.2 1.1 copy.47
  8.4 0.8 convert_bitcast_fusion
  9.2 0.8 compare_reduce_fusion
  10.0 4.5 %all-gather = bf16[2,45,256]{2,1,0:T(8,128)(2,1)S(1)} all-gather(bf16[1,45,256]{2,1,0:T(8,128)(2,1)S(1)} %convert_bitcast_fusion), channel_id=1, replica_groups=mesh['sec'=2,'dom'=8,'lev'=2] {'lev'}, dimensions={0}, use_global_device_ids=true | all-gather | bytes 69120 | tf_op jit(solution)/shard_map/all_gather | solution.py:119
  14.7 0.8 slice.5411
  15.5 13.8 %collective-permute-done = f32[12,45,256]{2,1,0:T(8,128)S(1)} collective-permute-done((f32[12,45,256]{2,1,0:T(8,128)S(1)}, f32[12,45,256]{2,1,0:T(8,128)S(1)}, u32[]{:S(2)}, u32[]{:S(2)}) %collective-permute-start) | collective-permute-done | bytes 552992 | tf_op jit(solution)/shard_map/ppermute | solution.py:21
  29.4 0.8 copy-done.6
  30.2 1.5 collective-permute-done.1
  31.7 1.4 pad_maximum_fusion.4
  33.1 31.0 %conditional.6 = (f32[12,45,256]{2,1,0:T(8,128)}, f32[10,45,256]{2,1,0:T(8,128)S(1)}) conditional(s32[]{:T(128)} %convert_element_type.12282, () %tuple.61, (f32[12]{0:T(128)S(1)}, f32[3,256]{1,0:T(4,128)S(1)}, s32[3,256]{1,0:T(4,128)S(1)}, f32[12,45,768]{2,1,0:T(8,128)S(1)}, f32[12,45,256]{2,1,0:T(8,128)S(1)}) %tuple.2097), branch_computations={%region_0.1_spmd, %region_1.3_spmd} | conditional | flops 1807104 | bytes 12578368 | solution.py:116
  33.2 5.0 %copy.26 = f32[12,45,768]{1,0,2:T(8,128)} copy(f32[12,45,768]{2,1,0:T(8,128)S(1)} %get-tuple-element.117) | data formatting | bytes 3317760 | tf_op jit(solution)/shard_map
  38.2 4.9 %gather_fusion = f32[256,12,45]{2,1,0:T(8,128)} fusion(f32[12,45,768]{1,0,2:T(8,128)} %copy.26, s32[1024]{0:T(1024)S(1)} %pad_clamp_fusion.2), kind=kCustom, calls=%fused_computation.clone | custom fusion | bytes 1106944 | tf_op jit(solution)/shard_map/cond/branch_1_fun/jit(_take)/gather | solution.py:104
  43.1 4.8 %gather_fusion.1 = f32[256,12,45]{2,1,0:T(8,128)} fusion(f32[12,45,768]{1,0,2:T(8,128)} %copy.26, s32[1024]{0:T(1024)S(1)} %pad_clamp_fusion.1), kind=kCustom, calls=%fused_computation.1.clone | custom fusion | bytes 1106944 | tf_op jit(solution)/shard_map/cond/branch_1_fun/jit(_take)/gather | solution.py:104
  48.0 4.9 %gather_fusion.2 = f32[256,12,45]{2,1,0:T(8,128)} fusion(f32[12,45,768]{1,0,2:T(8,128)} %copy.26, s32[1024]{0:T(1024)S(1)} %pad_clamp_fusion), kind=kCustom, calls=%fused_computation.2.clone | custom fusion | bytes 1106944 | tf_op jit(solution)/shard_map/cond/branch_1_fun/jit(_take)/gather | solution.py:104
  52.9 2.5 %copy.27 = f32[12,45,256]{1,0,2:T(8,128)} copy(f32[12,45,256]{2,1,0:T(8,128)S(1)} %get-tuple-element.118) | data formatting | bytes 1105920 | tf_op jit(solution)/shard_map
  55.4 5.9 %fusion.411 = f32[12,45,256]{1,0,2:T(8,128)S(1)} fusion(f32[12,45,256]{1,0,2:T(8,128)} %copy.27, f32[256,12,45]{2,1,0:T(8,128)} %gather_fusion.2, f32[256,12,45]{2,1,0:T(8,128)} %gather_fusion.1, f32[256,12,45]{2,1,0:T(8,128)} %gather_fusion, f32[256]{0:T(256)S(1)} %bitcast.5194, f32[256]{0:T(256)S(1)} %bitcast.5193, f32[256]{0:T(256)S(1)} %bitcast.5192, ...), kind=kLoop, calls=%fused_computation.2546 | loop fusion | flops 1797120 | bytes 2768688 | tf_op jit(solution)/shard_map/cond/branch_1_fun/add | solution.py:106
  61.3 1.7 %copy.39 = f32[12,45,256]{2,1,0:T(8,128)} copy(f32[12,45,256]{1,0,2:T(8,128)S(1)} %fusion.411) | data formatting | bytes 1105920 | tf_op jit(solution)/shard_map/cond | solution.py:116
  63.0 1.1 slice.5406
  64.1 0.9 slice.10097
  65.0 4.7 %all_gather.10 = bf16[2,90,256]{2,0,1:T(2,128)(2,1)S(1)} all-gather(bf16[2,45,256]{2,0,1:T(2,128)(2,1)S(1)} %copy.29), channel_id=1, replica_groups=mesh['sec'=2,'dom'=8,'lev'=2] {'lev'}, dimensions={1}, use_global_device_ids=true | all-gather | bytes 138240 | tf_op jit(solution)/shard_map/all_gather | solution.py:118
  69.8 5.8 %conditional.7 = (f32[2,45,256]{2,1,0:T(8,128)S(1)}, f32[2,45,256]{2,1,0:T(8,128)S(1)}) conditional(s32[]{:T(128)} %convert_element_type.12282, () %tuple.60, (bf16[2,90,256]{2,0,1:T(2,128)(2,1)S(1)}, f32[90,256]{1,0:T(8,128)S(1)}) %tuple.63), branch_computations={%region_2.0_spmd, %region_3.5_spmd} | conditional | flops 927232 | bytes 5335056 | solution.py:135
  70.4 0.6 multiply_subtract_fusion
  72.3 0.9 multiply_subtract_fusion.269
  75.8 1.0 collective-permute-start.3
  76.9 3.7 %collective-permute-start.4 = (f32[12,45,256]{2,1,0:T(8,128)S(1)}, f32[12,45,256]{2,1,0:T(8,128)}, u32[]{:S(2)}, u32[]{:S(2)}) collective-permute-start(f32[12,45,256]{2,1,0:T(8,128)S(1)} %get-tuple-element.1291), channel_id=1, source_target_pairs={{2,0},{4,2},{6,4},{8,6},{10,8},{12,10},{14,12},{0,14},{3,1},{5,3},... | collective-permute-start | bytes 1658888 | tf_op jit(solution)/shard_map/ppermute | solution.py:23
  80.7 0.8 slice.5415
  81.5 21.2 %collective-permute-done.3 = f32[12,45,256]{2,1,0:T(8,128)S(1)} collective-permute-done((f32[12,45,256]{2,1,0:T(8,128)S(1)}, f32[12,45,256]{2,1,0:T(8,128)S(1)}, u32[]{:S(2)}, u32[]{:S(2)}) %collective-permute-start.3) | collective-permute-done | bytes 552992 | tf_op jit(solution)/shard_map/ppermute | solution.py:21
  102.7 0.8 copy-done.7
  103.5 1.5 collective-permute-done.4
  105.0 1.4 pad_maximum_fusion.5
  106.4 31.1 %conditional.9 = (f32[12,45,256]{2,1,0:T(8,128)}, f32[10,45,256]{2,1,0:T(8,128)S(1)}) conditional(s32[]{:T(128)} %convert_element_type.12282, () %tuple.59, (f32[12]{0:T(128)S(1)}, f32[3,256]{1,0:T(4,128)S(1)}, s32[3,256]{1,0:T(4,128)S(1)}, f32[12,45,768]{2,1,0:T(8,128)S(1)}, f32[12,45,256]{2,1,0:T(8,128)S(1)}) %tuple.2098), branch_computations={%region_6.8_spmd, %region_7.9_spmd} | conditional | flops 1807104 | bytes 12578368 | solution.py:116
  106.7 5.0 %copy.32 = f32[12,45,768]{1,0,2:T(8,128)} copy(f32[12,45,768]{2,1,0:T(8,128)S(1)} %get-tuple-element.124) | data formatting | bytes 3317760 | tf_op jit(solution)/shard_map
  111.7 4.8 %gather_fusion.4 = f32[256,12,45]{2,1,0:T(8,128)} fusion(f32[12,45,768]{1,0,2:T(8,128)} %copy.32, s32[1024]{0:T(1024)S(1)} %pad_clamp_fusion.4), kind=kCustom, calls=%fused_computation.4.clone | custom fusion | bytes 1106944 | tf_op jit(solution)/shard_map/cond/branch_1_fun/jit(_take)/gather | solution.py:104
  116.5 4.9 %gather_fusion.5 = f32[256,12,45]{2,1,0:T(8,128)} fusion(f32[12,45,768]{1,0,2:T(8,128)} %copy.32, s32[1024]{0:T(1024)S(1)} %pad_clamp_fusion.3), kind=kCustom, calls=%fused_computation.5.clone | custom fusion | bytes 1106944 | tf_op jit(solution)/shard_map/cond/branch_1_fun/jit(_take)/gather | solution.py:104
  121.5 4.9 %gather_fusion.3 = f32[256,12,45]{2,1,0:T(8,128)} fusion(f32[12,45,768]{1,0,2:T(8,128)} %copy.32, s32[1024]{0:T(1024)S(1)} %pad_clamp_fusion.5), kind=kCustom, calls=%fused_computation.3.clone | custom fusion | bytes 1106944 | tf_op jit(solution)/shard_map/cond/branch_1_fun/jit(_take)/gather | solution.py:104
  126.4 2.5 %copy.33 = f32[12,45,256]{1,0,2:T(8,128)} copy(f32[12,45,256]{2,1,0:T(8,128)S(1)} %get-tuple-element.125) | data formatting | bytes 1105920 | tf_op jit(solution)/shard_map
  128.9 5.9 %fusion.418 = f32[12,45,256]{1,0,2:T(8,128)S(1)} fusion(f32[12,45,256]{1,0,2:T(8,128)} %copy.33, f32[256,12,45]{2,1,0:T(8,128)} %gather_fusion.5, f32[256,12,45]{2,1,0:T(8,128)} %gather_fusion.4, f32[256,12,45]{2,1,0:T(8,128)} %gather_fusion.3, f32[256]{0:T(256)S(1)} %bitcast.5197, f32[256]{0:T(256)S(1)} %bitcast.5196, f32[256]{0:T(256)S(1)} %bitcast.5195, ...), kind=kLoop, calls=%fused_computation.2565 | loop fusion | flops 1797120 | bytes 2768688 | tf_op jit(solution)/shard_map/cond/branch_1_fun/add | solution.py:106
  134.8 1.7 %copy.41 = f32[12,45,256]{2,1,0:T(8,128)} copy(f32[12,45,256]{1,0,2:T(8,128)S(1)} %fusion.418) | data formatting | bytes 1105920 | tf_op jit(solution)/shard_map/cond | solution.py:116
  136.5 1.1 slice.5407
  137.5 0.9 slice.10096
  138.5 4.7 %all_gather.12 = bf16[2,90,256]{2,0,1:T(2,128)(2,1)S(1)} all-gather(bf16[2,45,256]{2,0,1:T(2,128)(2,1)S(1)} %copy.35), channel_id=1, replica_groups=mesh['sec'=2,'dom'=8,'lev'=2] {'lev'}, dimensions={1}, use_global_device_ids=true | all-gather | bytes 138240 | tf_op jit(solution)/shard_map/all_gather | solution.py:118
  143.2 5.8 %conditional.10 = (f32[2,45,256]{2,1,0:T(8,128)S(1)}, f32[2,45,256]{2,1,0:T(8,128)S(1)}) conditional(s32[]{:T(128)} %convert_element_type.12282, () %tuple.58, (bf16[2,90,256]{2,0,1:T(2,128)(2,1)S(1)}, f32[90,256]{1,0:T(8,128)S(1)}) %tuple.66), branch_computations={%region_8.10_spmd, %region_9.11_spmd} | conditional | flops 927232 | bytes 5335056 | solution.py:135
  143.9 0.6 multiply_subtract_fusion.356
  145.8 0.9 multiply_subtract_fusion.625
  149.2 1.2 broadcast_in_dim.31
  (144 shorter events, 9.1 us)
Async XLA Ops:
  0.0 14.5 %copy-start.11 = (f32[12]{0:T(128)S(1)}, f32[12]{0:T(128)}, u32[]{:S(2)}) copy-start(f32[12]{0:T(128)} %param.26) | copy-start | bytes 148
  1.1 28.2 %collective-permute-start = (f32[12,45,256]{2,1,0:T(8,128)S(1)}, f32[12,45,256]{2,1,0:T(8,128)S(1)}, u32[]{:S(2)}, u32[]{:S(2)}) collective-permute-start(f32[12,45,256]{2,1,0:T(8,128)S(1)} %bitcast.3674), channel_id=1, source_target_pairs={{0,2},{2,4},{4,6},{6,8},{8,10},{10,12},{12,14},{14,0},{1,3},{3,5},... | collective-permute-start | bytes 1658888 | tf_op jit(solution)/shard_map/ppermute | solution.py:21
  4.1 27.5 %collective-permute-start.1 = (f32[12,45,256]{2,1,0:T(8,128)S(1)}, f32[12,45,256]{2,1,0:T(8,128)}, u32[]{:S(2)}, u32[]{:S(2)}) collective-permute-start(f32[12,45,256]{2,1,0:T(8,128)S(1)} %bitcast.3675), channel_id=1, source_target_pairs={{2,0},{4,2},{6,4},{8,6},{10,8},{12,10},{14,12},{0,14},{3,1},{5,3},... | collective-permute-start | bytes 1658888 | tf_op jit(solution)/shard_map/ppermute | solution.py:23
  8.3 6.2 %collective-permute-start.2 = (bf16[12,45,256]{2,1,0:T(8,128)(2,1)S(1)}, bf16[12,45,256]{2,1,0:T(8,128)(2,1)S(1)}, u32[]{:S(2)}, u32[]{:S(2)}) collective-permute-start(bf16[12,45,256]{2,1,0:T(8,128)(2,1)S(1)} %bitcast.3678), channel_id=1, source_target_pairs={{0,16},{16,0},{1,17},{17,1},{2,18},{18,2},{3,19},{19,3},{4,20},{20... | collective-permute-start | bytes 829448 | tf_op jit(solution)/shard_map/ppermute | solution.py:11
  14.6 0.9 copy-start.2
  15.5 17.6 %copy-start.8 = (f32[3,256]{1,0:T(4,128)S(1)}, f32[3,256]{1,0:T(4,128)}, u32[]{:S(2)}) copy-start(f32[3,256]{1,0:T(4,128)} %param.23) | copy-start | bytes 9220
  15.5 17.6 %copy-start.9 = (s32[3,256]{1,0:T(4,128)S(1)}, s32[3,256]{1,0:T(4,128)}, u32[]{:S(2)}) copy-start(s32[3,256]{1,0:T(4,128)} %param.22) | copy-start | bytes 9220
  15.5 17.6 %copy-start.10 = (f32[12]{0:T(128)S(1)}, f32[12]{0:T(128)}, u32[]{:S(2)}) copy-start(f32[12]{0:T(128)} %param.24) | copy-start | bytes 148
  29.4 0.8 copy-start.6
  69.7 5.8 %copy-start = (f32[7,45,256]{2,1,0:T(8,128)S(1)}, f32[7,45,256]{2,1,0:T(8,128)}, u32[]{:S(2)}) copy-start(f32[7,45,256]{2,1,0:T(8,128)} %slice.5411) | copy-start | bytes 967684
  69.7 5.9 %copy-start.3 = (bf16[12,45,256]{2,1,0:T(8,128)(2,1)S(1)}, bf16[12,45,256]{2,1,0:T(8,128)(2,1)}, u32[]{:S(2)}) copy-start(bf16[12,45,256]{2,1,0:T(8,128)(2,1)} %copy-done.2) | copy-start | bytes 829444
  75.7 4.9 %collective-permute-start.5 = (bf16[12,45,256]{2,1,0:T(8,128)(2,1)S(1)}, bf16[12,45,256]{2,1,0:T(8,128)(2,1)S(1)}, u32[]{:S(2)}, u32[]{:S(2)}) collective-permute-start(bf16[12,45,256]{2,1,0:T(8,128)(2,1)S(1)} %get-tuple-element.1290), channel_id=1, source_target_pairs={{0,16},{16,0},{1,17},{17,1},{2,18},{18,2},{3,19},{19,3},{4,20},{20... | collective-permute-start | bytes 829448 | tf_op jit(solution)/shard_map/ppermute | solution.py:11
  75.8 26.9 %collective-permute-start.3 = (f32[12,45,256]{2,1,0:T(8,128)S(1)}, f32[12,45,256]{2,1,0:T(8,128)S(1)}, u32[]{:S(2)}, u32[]{:S(2)}) collective-permute-start(f32[12,45,256]{2,1,0:T(8,128)S(1)} %get-tuple-element.1291), channel_id=1, source_target_pairs={{0,2},{2,4},{4,6},{6,8},{8,10},{10,12},{12,14},{14,0},{1,3},{3,5},... | collective-permute-start | bytes 1658888 | tf_op jit(solution)/shard_map/ppermute | solution.py:21
  76.9 28.1 %collective-permute-start.4 = (f32[12,45,256]{2,1,0:T(8,128)S(1)}, f32[12,45,256]{2,1,0:T(8,128)}, u32[]{:S(2)}, u32[]{:S(2)}) collective-permute-start(f32[12,45,256]{2,1,0:T(8,128)S(1)} %get-tuple-element.1291), channel_id=1, source_target_pairs={{2,0},{4,2},{6,4},{8,6},{10,8},{12,10},{14,12},{0,14},{3,1},{5,3},... | collective-permute-start | bytes 1658888 | tf_op jit(solution)/shard_map/ppermute | solution.py:23
  80.6 0.9 copy-start.4
  102.7 0.8 copy-start.7
  143.2 5.8 %copy-start.1 = (f32[7,45,256]{2,1,0:T(8,128)S(1)}, f32[7,45,256]{2,1,0:T(8,128)}, u32[]{:S(2)}) copy-start(f32[7,45,256]{2,1,0:T(8,128)} %slice.5415) | copy-start | bytes 967684
  143.2 5.9 %copy-start.5 = (bf16[12,45,256]{2,1,0:T(8,128)(2,1)S(1)}, bf16[12,45,256]{2,1,0:T(8,128)(2,1)}, u32[]{:S(2)}) copy-start(bf16[12,45,256]{2,1,0:T(8,128)(2,1)} %copy-done.4) | copy-start | bytes 829444
where the time goes:
time: 151 us; the launch traced here: 150 us
  local copies, waits for them, and re-layouts  59.9 us (40%)
  waiting for transfers between devices  38 us (25%)
  other arithmetic  26.4 us (17%)
  blocking collectives  14 us (9%)
  starting transfers between devices  11 us (7%)
    ppermute x2, waiting for transfers between devices, padded(): lax.ppermute(tail, axis, [(i, (i + 1) % count) for i in range(count)])  35 us
    gather x6, local copies, waits for them, and re-layouts, run_horizontal(): jnp.take(extended, neighbours[edge], axis=2) - own  29.4 us
    another operation x8, local copies, waits for them, and re-layouts  15 us
    add x2, other arithmetic, run_horizontal(): return own + field_diff[:, None, None] * total  11.9 us
    all_gather x2, blocking collectives, shards(): lax.all_gather(shortened(smoothed[0:2]), 'lev', axis=1, tiled=True)  9.47 us
    ppermute x2, starting transfers between devices, padded(): lax.ppermute(head, axis, [((i + 1) % count, i) for i in range(count)])  6.83 us
    all_gather x1, blocking collectives, shards(): lax.all_gather(vert_coef.astype(jnp.bfloat16), 'lev', axis=0, tiled=True)  4.5 us
    ppermute x2, starting transfers between devices, padded(): lax.ppermute(tail, axis, [(i, (i + 1) % count) for i in range(count)])  4.07 us
  transfers between devices with their start and end apart: 6, of which 4 were waited for; matrix products, arithmetic and copies ran while one was open for 3% of the time, Pallas kernels for 0%

commit v1 on v0

v1 whole, which is shorter than its diff:
```python
import functools
import jax
import jax.numpy as jnp
from jax import lax
from jax.experimental import pallas as pl
from jax.experimental.pallas import tpu as pltpu
from jax.sharding import PartitionSpec as P

AXES = ("sec", "dom", "lev")
SOLVED = 2
EDGES = 3
LANES8 = 8
LANES = 128
VMEM = pl.BlockSpec(memory_space=pltpu.VMEM)
SMEM = pl.BlockSpec(memory_space=pltpu.SMEM)
F32 = jnp.float32
BF16 = jnp.bfloat16


def up(count, unit):
    return -(-count // unit) * unit


def route(array, dom_step, swap_lev, pairs):
    doms, levs = lax.axis_size("dom"), lax.axis_size("lev")
    place = lambda s, d, v: (s * doms + d) * levs + v
    table = [
        (place(a, d, v), place(b, (d + step) % doms, v ^ flip))
        for a, b, step, flip in [(a, b, dom_step, swap_lev) for a, b in pairs]
        for d in range(doms)
        for v in range(levs)
    ]
    return lax.ppermute(array, AXES, table)


def tendency_into(out_ref, state, mask, relax_ref):
    fields = out_ref.shape[0]
    rounded = lambda f: state(f).astype(BF16).astype(F32)
    theta, vapour, cloud, rain = rounded(1), rounded(2), rounded(3), rounded(4)
    saturation = 0.6 * jnp.exp(0.25 * theta)
    condense = 0.5 * jnp.tanh(vapour - saturation)
    autoconv = 0.4 * cloud * cloud / (1.0 + cloud * cloud)
    evaporate = 0.3 * rain * rain / (1.0 + rain * rain) * jax.nn.sigmoid(saturation - vapour)
    micro = {
        1: 2.5 * (condense - evaporate),
        2: evaporate - condense,
        3: condense - autoconv,
        4: autoconv - evaporate,
    }
    for f in range(fields):
        clear = -relax_ref[f] * rounded(f)
        if f in micro:
            clear = jnp.where(mask == 1, clear + micro[f], clear)
        out_ref[f] = clear.astype(out_ref.dtype)


def prepare_kernel(mine_ref, nbr_ref, weight_ref, mask_ref, relax_ref, gather_ref, lagged_ref):
    width = nbr_ref.shape[1]
    reach = gather_ref.shape[0]
    rows = 64
    for start in range(0, reach, rows):
        place = lax.broadcasted_iota(jnp.int32, (rows, width), 0) + start
        total = jnp.zeros((rows, width), F32)
        for edge in range(EDGES):
            total = total + jnp.where(place == nbr_ref[edge : edge + 1, :], weight_ref[edge : edge + 1, :], 0.0)
        high = total.astype(BF16)
        gather_ref[start : start + rows, 0:width] = high
        gather_ref[start : start + rows, width : 2 * width] = (total - high.astype(F32)).astype(BF16)

    @pl.when(lax.axis_index("sec") == 0)
    def _():
        tendency_into(lagged_ref, lambda f: mine_ref[0, f], mask_ref[0:1, :], relax_ref)


def shift(values, by):
    return pltpu.roll(values, by % LANES8, 0)


def put(ref, start, value):
    for h in range(ref.shape[0]):
        ref[h, start : start + value.shape[0], :] = value[:, h * LANES : (h + 1) * LANES]


def get(ref, start, count):
    return jnp.concatenate([ref[h, start : start + count, :] for h in range(ref.shape[0])], axis=1)


def get_strided(ref, start, steps):
    rows = pl.ds(start, LANES8, stride=steps)
    return jnp.concatenate([ref[h, rows, :] for h in range(ref.shape[0])], axis=1)


def put_strided(ref, start, steps, value):
    for h in range(ref.shape[0]):
        ref[h, pl.ds(start, LANES8, stride=steps), :] = value[:, h * LANES : (h + 1) * LANES]


def factor_kernel(own_ref, other_ref, low_ref, fore_ref, inv_ref, high_ref, back_ref, scan_ref, kappa, ratio, inverse):
    half, width = own_ref.shape
    depth = 2 * half
    steps = low_ref.shape[0]
    level = lax.axis_index("lev")
    ratio[...] = jnp.zeros(ratio.shape, F32)
    inverse[...] = jnp.zeros(inverse.shape, F32)

    @pl.when(level == 0)
    def _():
        kappa[0:half, :] = own_ref[...]
        kappa[half:depth, :] = other_ref[...].astype(F32)

    @pl.when(level == 1)
    def _():
        kappa[0:half, :] = other_ref[...].astype(F32)
        kappa[half:depth, :] = own_ref[...]

    excess = jnp.ones((1, width), F32)
    for k in range(depth):
        here = kappa[k : k + 1, :]
        inv = 1.0 / (excess + here)
        down = here * inv
        put(inverse, k, inv)
        if k < depth - 1:
            put(ratio, LANES8 + k, down)
        excess = 1.0 + down * excess

    index = lax.broadcasted_iota(jnp.int32, (LANES8, width), 0)
    running = None
    for t in range(steps):
        low = get_strided(ratio, LANES8 - 1 + t, steps)
        low_ref[t] = low
        running = low if running is None else running * low
        fore_ref[t] = running
        inv_ref[t] = get_strided(inverse, t, steps)
    one = jnp.where(index >= 1, running, 0.0)
    two = jnp.where(index >= 2, running * shift(running, 1), 0.0)
    four = jnp.where(index >= 4, two * shift(two, 2), 0.0)
    scan_ref[0], scan_ref[1], scan_ref[2] = one, two, four
    running = None
    for t in range(steps - 1, -1, -1):
        high = get_strided(ratio, LANES8 + t, steps)
        high_ref[t] = high
        running = high if running is None else running * high
        back_ref[t] = running
    one = jnp.where(index < LANES8 - 1, running, 0.0)
    two = jnp.where(index < LANES8 - 2, running * shift(running, -1), 0.0)
    four = jnp.where(index < LANES8 - 4, two * shift(two, -2), 0.0)
    scan_ref[3], scan_ref[4], scan_ref[5] = one, two, four


def solve(right, factors):
    low_ref, fore_ref, inv_ref, high_ref, back_ref, scan_ref = factors
    steps, _, width = low_ref.shape
    index = lax.broadcasted_iota(jnp.int32, (LANES8, width), 0)
    rows = []
    for t in range(steps):
        row = get_strided(right, t, steps)
        if t:
            row = row + low_ref[t] * rows[-1]
        rows.append(row)
    carry = rows[-1]
    for i, by in enumerate((1, 2, 4)):
        carry = carry + scan_ref[i] * shift(carry, by)
    carry = jnp.where(index >= 1, shift(carry, 1), 0.0)
    rows = [(rows[t] + fore_ref[t] * carry) * inv_ref[t] for t in range(steps)]
    for t in range(steps - 2, -1, -1):
        rows[t] = rows[t] + high_ref[t] * rows[t + 1]
    carry = rows[0]
    for i, by in enumerate((1, 2, 4)):
        carry = carry + scan_ref[3 + i] * shift(carry, -by)
    carry = jnp.where(index < LANES8 - 1, shift(carry, -1), 0.0)
    for t in range(steps):
        put_strided(right, t, steps, rows[t] + back_ref[t] * carry)


def dynamics(own, left, right, weight_ref, diff_ref, gather_ref, factors, wide, flux, columns, emit, half, fields):
    slots = fields + SOLVED
    stride = wide.shape[0] // slots
    width = weight_ref.shape[1]
    for f in range(slots):
        at = slice(f * stride, f * stride + half)
        mid = own(f)
        high = mid.astype(BF16)
        wide[at, 0:width] = left(f)
        wide[at, width : 2 * width] = high
        wide[at, 2 * width : 3 * width] = right(f)
        wide[at, 3 * width :] = (mid - high.astype(F32)).astype(BF16)
    both = jnp.dot(wide[:, 0 : 3 * width], gather_ref[...], preferred_element_type=F32)
    rest = jnp.dot(wide[:, 3 * width :], gather_ref[width : 2 * width, 0:width], preferred_element_type=F32)
    flux[...] = both[:, :width] + both[:, width:] + rest
    total = weight_ref[0:1, :] + weight_ref[1:2, :] + weight_ref[2:3, :]

    def smoothed(f):
        scale = diff_ref[f if f < fields else f - fields]
        mid = own(f)
        return mid + scale * (flux[f * stride : f * stride + half, :] - total * mid)

    level = lax.axis_index("lev")
    depth = 2 * half
    for f in range(SOLVED):
        put(columns.at[f], depth, jnp.zeros((columns.shape[2] - depth, width), F32))
        mine, theirs = smoothed(f), smoothed(fields + f)

        @pl.when(level == 0)
        def _():
            put(columns.at[f], 0, mine)
            put(columns.at[f], half, theirs)

        @pl.when(level == 1)
        def _():
            put(columns.at[f], 0, theirs)
            put(columns.at[f], half, mine)

    for f in range(SOLVED):
        solve(columns.at[f], factors)
    for f in range(SOLVED, fields):
        emit(f, smoothed(f))

    @pl.when(level == 0)
    def _():
        for f in range(SOLVED):
            emit(f, get(columns.at[f], 0, half))
            emit(fields + f, get(columns.at[f], half, half))

    @pl.when(level == 1)
    def _():
        for f in range(SOLVED):
            emit(f, get(columns.at[f], half, half))
            emit(fields + f, get(columns.at[f], 0, half))


def first_kernel(
    state_ref, left_ref, right_ref, dleft_ref, dright_ref, across_ref, mine_ref, lag_ref, weight_ref, diff_ref, gather_ref,
    *rest,
):
    factors, (full_ref, short_ref, wide, flux, columns) = rest[:6], rest[6:]
    fields, half = state_ref.shape[1], state_ref.shape[2]

    def emit(f, value):
        lagged = mine_ref[f] if f < fields else lag_ref[f - fields]
        value = value + lagged.astype(F32)
        full_ref[f] = value
        short_ref[f] = value.astype(BF16)

    @pl.when(lax.axis_index("sec") == 1)
    def _():
        dynamics(
            lambda f: state_ref[0, f] if f < fields else across_ref[f - fields].astype(F32),
            lambda f: left_ref[f] if f < fields else dleft_ref[f - fields],
            lambda f: right_ref[f] if f < fields else dright_ref[f - fields],
            weight_ref, diff_ref, gather_ref, factors, wide, flux, columns, emit, half, fields,
        )


def last_kernel(
    state_ref, left_ref, right_ref, full_ref, lagged_ref, mask_ref, relax_ref, weight_ref, diff_ref, gather_ref, *rest
):
    factors, (out_ref, wide, flux, columns) = rest[:6], rest[6:]
    fields, half = out_ref.shape[1], out_ref.shape[2]

    def emit(f, value):
        if f < fields:
            out_ref[0, f] = value + lagged_ref[f].astype(F32)

    @pl.when(lax.axis_index("sec") == 0)
    def _():
        dynamics(
            lambda f: state_ref[f], lambda f: left_ref[f], lambda f: right_ref[f],
            weight_ref, diff_ref, gather_ref, factors, wide, flux, columns, emit, half, fields,
        )

    @pl.when(lax.axis_index("sec") == 1)
    def _():
        tendency_into(out_ref.at[0], lambda f: full_ref[f], mask_ref[1:2, :], relax_ref)


def params(mib):
    return pltpu.CompilerParams(vmem_limit_bytes=mib << 20)


def shards(sections, neighbours, edge_weight, field_diff, vert_coef, relax_rate, precip_mask):
    _, fields, half, width = sections.shape
    shape = jax.ShapeDtypeStruct
    steps = up(up(2 * half, LANES8) // LANES8, 4)
    depth = steps * LANES8
    slots = fields + SOLVED
    reach = 3 * width

    short = sections[0].astype(BF16)
    solved_short = short[0:SOLVED]
    left = route(short, 1, 0, [(0, 1)])
    right = route(short, -1, 0, [(0, 1)])
    pack = jnp.concatenate([solved_short, vert_coef.astype(BF16)[None]], axis=0)
    across = route(pack, 0, 1, [(0, 1), (1, 0)])
    lag = route(solved_short, 0, 1, [(0, 0), (1, 1)])
    dleft = route(solved_short, 1, 1, [(0, 1)])
    dright = route(solved_short, -1, 1, [(0, 1)])
    state = route(sections, 0, 0, [(0, 1), (1, 0)])

    gather, lagged = pl.pallas_call(
        prepare_kernel,
        out_shape=[shape((reach, 2 * width), BF16), shape((fields, half, width), BF16)],
        in_specs=[VMEM] * 4 + [SMEM],
        out_specs=[VMEM] * 2,
        compiler_params=params(16),
    )(sections, neighbours, edge_weight, precip_mask, relax_rate)

    chunk = shape((steps, LANES8, width), F32)
    factors = pl.pallas_call(
        factor_kernel,
        out_shape=[chunk] * 5 + [shape((6, LANES8, width), F32)],
        in_specs=[VMEM] * 2,
        out_specs=[VMEM] * 6,
        scratch_shapes=[
            pltpu.VMEM((2 * half, width), F32),
            pltpu.VMEM((width // LANES, depth + 2 * LANES8, LANES), F32),
            pltpu.VMEM((width // LANES, depth, LANES), F32),
        ],
        compiler_params=params(16),
    )(vert_coef, across[SOLVED])

    scratch = [
        pltpu.VMEM((slots * up(half, 16), 4 * width), BF16),
        pltpu.VMEM((slots * up(half, 16), width), F32),
        pltpu.VMEM((SOLVED, width // LANES, depth, LANES), F32),
    ]
    full, brief = pl.pallas_call(
        first_kernel,
        out_shape=[shape((slots, half, width), F32), shape((slots, half, width), BF16)],
        in_specs=[VMEM] * 9 + [SMEM] + [VMEM] * 7,
        out_specs=[VMEM] * 2,
        scratch_shapes=scratch,
        compiler_params=params(32),
    )(state, left, right, dleft, dright, across, short, lag, edge_weight, field_diff, gather, *factors)

    left = route(brief, 1, 0, [(1, 0)])
    right = route(brief, -1, 0, [(1, 0)])
    state = route(full, 0, 0, [(1, 0), (0, 1)])
    return pl.pallas_call(
        last_kernel,
        out_shape=shape(sections.shape, F32),
        in_specs=[VMEM] * 6 + [SMEM, VMEM, SMEM] + [VMEM] * 7,
        out_specs=VMEM,
        scratch_shapes=scratch,
        compiler_params=params(32),
    )(state, left, right, full, lagged, precip_mask, relax_rate, edge_weight, field_diff, gather, *factors)


def solution(mesh):
    return jax.shard_map(
        shards,
        mesh=mesh,
        in_specs=(
            P("sec", None, "lev", "dom"),
            P(None, "dom"),
            P(None, "dom"),
            P(),
            P("lev", "dom"),
            P(),
            P(None, "dom"),
        ),
        out_specs=P("sec", None, "lev", "dom"),
        check_vma=False,
    )
```

time: 151 us -> 37.8 us (0.25)
  local copies, waits for them, and re-layouts: 59.9 us -> 3.3 us
  waiting for transfers between devices: 38 us -> 10.7 us
  other arithmetic: 26.4 us -> 0.02 us
  blocking collectives: 14 us -> 0 us
  starting transfers between devices: 11 us -> 19.2 us
  Pallas kernels: 0 us -> 4.08 us
    gather x6 -> x0, local copies, waits for them, and re-layouts: 29.4 us -> none  [run_horizontal(): jnp.take(extended, neighbours[edge], axis=2) - own]
    ppermute x6 -> x10, waiting for transfers between devices: 38 us -> 10.7 us  [route(): return lax.ppermute(array, AXES, table)]
    another operation x12 -> x0, local copies, waits for them, and re-layouts: 16.3 us -> none
    all_gather x3 -> x0, blocking collectives: 14 us -> none  [the longest x2 9.47 us: shards(): lax.all_gather(shortened(smoothed[0:2]), 'lev', axis=1, tiled=True)]
    add x4 -> x0, other arithmetic: 11.9 us -> none  [the longest x2 11.9 us: run_horizontal(): return own + field_diff[:, None, None] * total]
    ppermute x6 -> x10, starting transfers between devices: 11 us -> 19.2 us  [route(): return lax.ppermute(array, AXES, table)]
    slice x34 -> x1, local copies, waits for them, and re-layouts: 5.89 us -> 0.01 us  [shards(): solved_short = short[0:SOLVED]]
    sub x10 -> x0, other arithmetic: 5.57 us -> none  [the longest x8 3.82 us: thomas_fields(): after = values[index][level] - ratios[level] * after]
  transfers between devices with their start and end apart: 6 -> 10, of which waited for: 4 -> 3; matrix products, arithmetic and copies ran while one was open for 3% -> 3% of each run, Pallas kernels for 0% -> 5%
where the time goes in v1:
time: 37.8 us; the launch traced here: 37.5 us
  starting transfers between devices  19.2 us (51%)
  waiting for transfers between devices  10.7 us (28%)
  Pallas kernels  4.08 us (11%)
  local copies, waits for them, and re-layouts  3.3 us (9%)
    ppermute x10, starting transfers between devices, route(): return lax.ppermute(array, AXES, table)  19.2 us
    ppermute x10, waiting for transfers between devices, route(): return lax.ppermute(array, AXES, table)  10.7 us
    unnamed x17, local copies, waits for them, and re-layouts  1.87 us
    pallas_call x1, Pallas kernels, shards(): pl.pallas_call(last_kernel, out_shape=shape(sections.shape, F32), in_spec...  1.6 us
    pallas_call x1, local copies, waits for them, and re-layouts, shards(): pl.pallas_call(last_kernel, out_shape=shape(sections.shape, F32), in_spec...  1.37 us
    pallas_call x1, Pallas kernels, shards(): pl.pallas_call(prepare_kernel, out_shape=[shape((reach, 2 * width), BF16)...  0.98 us
    pallas_call x1, Pallas kernels, shards(): pl.pallas_call(factor_kernel, out_shape=[chunk] * 5 + [shape((6, LANES8,...  0.95 us
  transfers between devices with their start and end apart: 10, of which 3 were waited for; matrix products, arithmetic and copies ran while one was open for 3% of the time, Pallas kernels for 5%

profile of v1, /device:TPU:0, one launch (start us, length us, event | category | flops | bytes accessed | tf_op | source)
XLA Modules:
  0.0 37.5 jit_solution(11703869625930085903)
XLA Ops:
  0.0 0.0 copy-start.6
  0.0 0.0 copy-start
  0.0 0.5 %collective-permute-start = (f32[1,12,45,256]{3,0,2,1:T(1,128)}, f32[1,12,45,256]{3,0,2,1:T(1,128)S(1)}, u32[]{:S(2)}, u32[]{:S(2)}) collective-permute-start(f32[1,12,45,256]{3,0,2,1:T(1,128)} %param.7), channel_id=1, source_target_pairs={{0,16},{1,17},{2,18},{3,19},{4,20},{5,21},{6,22},{7,23},{8,24},{9,... | collective-permute-start | bytes 1658888 | tf_op jit(solution)/shard_map/ppermute | solution.py:33
  0.5 1.1 %copy.17 = bf16[1,12,45,256]{3,2,1,0:T(8,128)(2,1)S(1)} copy(f32[1,12,45,256]{3,0,2,1:T(1,128)} %param.7) | data formatting | bytes 829440 | tf_op args[0]
  1.6 0.0 copy-done
  1.6 2.7 %collective-permute-start.5 = (bf16[3,45,256]{2,1,0:T(8,128)(2,1)S(1)}, bf16[3,45,256]{2,1,0:T(8,128)(2,1)S(1)}, u32[]{:S(2)}, u32[]{:S(2)}) collective-permute-start(bf16[3,45,256]{2,1,0:T(8,128)(2,1)S(1)} %pad_maximum_fusion), channel_id=1, source_target_pairs={{0,17},{1,16},{2,19},{3,18},{4,21},{5,20},{6,23},{7,22},{8,25},{9,... | collective-permute-start | bytes 207368 | tf_op jit(solution)/shard_map/ppermute | solution.py:33
  4.3 0.0 copy-done.6
  4.3 0.0 copy-start.1
  4.3 0.0 copy-start.2
  4.4 0.0 copy-start.3
  4.4 0.0 copy-start.5
  4.4 6.3 %collective-permute-start.2 = (bf16[12,45,256]{2,1,0:T(8,128)(2,1)S(1)}, bf16[12,45,256]{2,1,0:T(8,128)(2,1)S(1)}, u32[]{:S(2)}, u32[]{:S(2)}) collective-permute-start(bf16[12,45,256]{2,1,0:T(8,128)(2,1)S(1)} %bitcast.9), channel_id=1, source_target_pairs={{0,30},{1,31},{2,16},{3,17},{4,18},{5,19},{6,20},{7,21},{8,22},{9,... | collective-permute-start | bytes 829448 | tf_op jit(solution)/shard_map/ppermute | solution.py:33
  10.7 1.3 %collective-permute-start.1 = (bf16[12,45,256]{2,1,0:T(8,128)(2,1)S(1)}, bf16[12,45,256]{2,1,0:T(8,128)(2,1)S(1)}, u32[]{:S(2)}, u32[]{:S(2)}) collective-permute-start(bf16[12,45,256]{2,1,0:T(8,128)(2,1)S(1)} %bitcast.10), channel_id=1, source_target_pairs={{0,18},{1,19},{2,20},{3,21},{4,22},{5,23},{6,24},{7,25},{8,26},{9,... | collective-permute-start | bytes 829448 | tf_op jit(solution)/shard_map/ppermute | solution.py:33
  12.0 0.6 %collective-permute-start.6 = (bf16[2,45,256]{2,1,0:T(8,128)(2,1)S(1)}, bf16[2,45,256]{2,1,0:T(8,128)(2,1)S(1)}, u32[]{:S(2)}, u32[]{:S(2)}) collective-permute-start(bf16[2,45,256]{2,1,0:T(8,128)(2,1)S(1)} %slice_bitcast_fusion), channel_id=1, source_target_pairs={{0,1},{1,0},{2,3},{3,2},{4,5},{5,4},{6,7},{7,6},{8,9},{9,8},{10,11... | collective-permute-start | bytes 138248 | tf_op jit(solution)/shard_map/ppermute | solution.py:33
  12.6 0.0 copy-done.1
  12.7 0.0 copy-done.2
  12.7 0.0 copy-done.3
  12.7 0.0 copy-done.5
  12.7 1.0 %shard_map.73 = (bf16[768,512]{1,0:T(8,128)(2,1)S(1)}, bf16[12,45,256]{2,1,0:T(8,128)(2,1)S(1)}) custom-call(f32[1,12,45,256]{3,2,1,0:T(8,128)S(1)} %copy.12.mine_ref, s32[3,256]{1,0:T(4,128)S(1)} %copy-done.3, f32[3,256]{1,0:T(4,128)S(1)} %copy-done.1, s32[2,256]{1,0:T(2,128)S(1)} %copy-done.2, f32[12]{0:T(128)S(1)} %copy-done.5), custom_call_target="tpu_custom_call" | custom-call | tf_op jit(solution)/shard_map/pallas_call | solution.py:299
  13.7 0.0 collective-permute-done.5.across_ref
  13.7 1.8 %collective-permute-start.4 = (bf16[2,45,256]{2,1,0:T(8,128)(2,1)S(1)}, bf16[2,45,256]{2,1,0:T(8,128)(2,1)S(1)}, u32[]{:S(2)}, u32[]{:S(2)}) collective-permute-start(bf16[2,45,256]{2,1,0:T(8,128)(2,1)S(1)} %slice_bitcast_fusion), channel_id=1, source_target_pairs={{0,31},{1,30},{2,17},{3,16},{4,19},{5,18},{6,21},{7,20},{8,23},{9,... | collective-permute-start | bytes 138248 | tf_op jit(solution)/shard_map/ppermute | solution.py:33
  15.5 0.0 collective-permute-done
  15.5 1.3 %collective-permute-start.3 = (bf16[2,45,256]{2,1,0:T(8,128)(2,1)S(1)}, bf16[2,45,256]{2,1,0:T(8,128)(2,1)S(1)}, u32[]{:S(2)}, u32[]{:S(2)}) collective-permute-start(bf16[2,45,256]{2,1,0:T(8,128)(2,1)S(1)} %slice_bitcast_fusion), channel_id=1, source_target_pairs={{0,19},{1,18},{2,21},{3,20},{4,23},{5,22},{6,25},{7,24},{8,27},{9,... | collective-permute-start | bytes 138248 | tf_op jit(solution)/shard_map/ppermute | solution.py:33
  16.8 0.9 %shard_map.74 = (f32[12,8,256]{2,1,0:T(8,128)S(1)}, f32[12,8,256]{2,1,0:T(8,128)S(1)}, f32[12,8,256]{2,1,0:T(8,128)S(1)}, f32[12,8,256]{2,1,0:T(8,128)S(1)}, f32...) custom-call(f32[45,256]{1,0:T(8,128)S(1)} %copy-done, bf16[45,256]{1,0:T(8,128)(2,1)S(1)} %slice_bitcast_fusion.1.other_ref), custom_call_target="tpu_custom_call" | custom-call | tf_op jit(solution)/shard_map/pallas_call | solution.py:308
  17.7 0.1 copy.14.state_ref
  17.8 0.0 collective-permute-done.6.lag_ref
  17.8 0.0 collective-permute-done.4.dright_ref
  17.8 0.7 %collective-permute-done.3.dleft_ref = bf16[2,45,256]{2,1,0:T(8,128)(2,1)S(1)} collective-permute-done((bf16[2,45,256]{2,1,0:T(8,128)(2,1)S(1)}, bf16[2,45,256]{2,1,0:T(8,128)(2,1)S(1)}, u32[]{:S(2)}, u32[]{:S(2)}) %collective-permute-start.3) | collective-permute-done | bytes 46112 | tf_op jit(solution)/shard_map/ppermute | solution.py:33
  18.5 0.0 collective-permute-done.2.right_ref
  18.5 0.0 collective-permute-done.1.left_ref
  18.5 0.0 copy-start.4
  18.5 0.7 %copy-done.4 = f32[12]{0:T(128)S(1)} copy-done((f32[12]{0:T(128)S(1)}, f32[12]{0:T(128)}, u32[]{:S(2)}) %copy-start.4) | copy-done | bytes 72
  19.2 0.6 %shard_map.75 = (f32[14,45,256]{2,1,0:T(8,128)S(1)}, bf16[14,45,256]{2,1,0:T(8,128)(2,1)S(1)}) custom-call(f32[1,12,45,256]{3,2,1,0:T(8,128)S(1)} %copy.14.state_ref, bf16[12,45,256]{2,1,0:T(8,128)(2,1)S(1)} %collective-permute-done.1.left_ref, bf16[12,45,256]{2,1,0:T(8,128)(2,1)S(1)} %collective-permute-done.2.right_ref, ...), custom_call_target="tpu_custom_call" | custom-call | tf_op jit(solution)/shard_map/pallas_call | solution.py:326
  19.7 2.2 %collective-permute-start.7 = (f32[14,45,256]{2,1,0:T(8,128)S(1)}, f32[14,45,256]{2,1,0:T(8,128)S(1)}, u32[]{:S(2)}, u32[]{:S(2)}) collective-permute-start(f32[14,45,256]{2,1,0:T(8,128)S(1)} %get-tuple-element.22.full_ref), channel_id=1, source_target_pairs={{16,0},{17,1},{18,2},{19,3},{20,4},{21,5},{22,6},{23,7},{24,8},{25... | collective-permute-start | bytes 1935368 | tf_op jit(solution)/shard_map/ppermute | solution.py:33
  22.0 1.3 %collective-permute-start.9 = (bf16[14,45,256]{2,1,0:T(8,128)(2,1)S(1)}, bf16[14,45,256]{2,1,0:T(8,128)(2,1)S(1)}, u32[]{:S(2)}, u32[]{:S(2)}) collective-permute-start(bf16[14,45,256]{2,1,0:T(8,128)(2,1)S(1)} %get-tuple-element.23), channel_id=1, source_target_pairs={{16,14},{17,15},{18,0},{19,1},{20,2},{21,3},{22,4},{23,5},{24,6},{... | collective-permute-start | bytes 967688 | tf_op jit(solution)/shard_map/ppermute | solution.py:33
  23.3 1.3 %collective-permute-start.8 = (bf16[14,45,256]{2,1,0:T(8,128)(2,1)S(1)}, bf16[14,45,256]{2,1,0:T(8,128)(2,1)S(1)}, u32[]{:S(2)}, u32[]{:S(2)}) collective-permute-start(bf16[14,45,256]{2,1,0:T(8,128)(2,1)S(1)} %get-tuple-element.23), channel_id=1, source_target_pairs={{16,2},{17,3},{18,4},{19,5},{20,6},{21,7},{22,8},{23,9},{24,10},{2... | collective-permute-start | bytes 967688 | tf_op jit(solution)/shard_map/ppermute | solution.py:33
  24.6 6.0 %collective-permute-done.9.right_ref = bf16[14,45,256]{2,1,0:T(8,128)(2,1)S(1)} collective-permute-done((bf16[14,45,256]{2,1,0:T(8,128)(2,1)S(1)}, bf16[14,45,256]{2,1,0:T(8,128)(2,1)S(1)}, u32[]{:S(2)}, u32[]{:S(2)}) %collective-permute-start.9) | collective-permute-done | bytes 322592 | tf_op jit(solution)/shard_map/ppermute | solution.py:33
  30.5 4.0 %collective-permute-done.8.left_ref = bf16[14,45,256]{2,1,0:T(8,128)(2,1)S(1)} collective-permute-done((bf16[14,45,256]{2,1,0:T(8,128)(2,1)S(1)}, bf16[14,45,256]{2,1,0:T(8,128)(2,1)S(1)}, u32[]{:S(2)}, u32[]{:S(2)}) %collective-permute-start.8) | collective-permute-done | bytes 322592 | tf_op jit(solution)/shard_map/ppermute | solution.py:33
  34.5 0.0 collective-permute-done.7.state_ref
  34.5 1.6 %shard_map.76 = f32[1,12,45,256]{3,2,1,0:T(8,128)S(1)} custom-call(f32[14,45,256]{2,1,0:T(8,128)S(1)} %collective-permute-done.7.state_ref, bf16[14,45,256]{2,1,0:T(8,128)(2,1)S(1)} %collective-permute-done.8.left_ref, bf16[14,45,256]{2,1,0:T(8,128)(2,1)S(1)} %collective-permute-done.9.right_ref, f32[14,45,256]{2,1,0:T(8,128)S(1)} %get-tuple-element.22.full_ref, ...), custom_call_target="tpu_custom_call" | custom-call | tf_op jit(solution)/shard_map/pallas_call | solution.py:338
  36.1 1.4 %copy.15 = f32[1,12,45,256]{3,0,2,1:T(1,128)} copy(f32[1,12,45,256]{3,2,1,0:T(8,128)S(1)} %shard_map.76) | data formatting | bytes 1105920 | tf_op jit(solution)/shard_map/pallas_call | solution.py:338
  (6 shorter events, 0.1 us)
Async XLA Ops:
  0.0 4.3 %copy-start.6 = (f32[1,12,45,256]{3,0,2,1:T(1,128)S(1)}, f32[1,12,45,256]{3,0,2,1:T(1,128)}, u32[]{:S(2)}) copy-start(f32[1,12,45,256]{3,0,2,1:T(1,128)} %param.7) | copy-start | bytes 1658884
  0.0 1.6 %copy-start = (f32[45,256]{1,0:T(8,128)S(1)}, f32[45,256]{1,0:T(8,128)}, u32[]{:S(2)}) copy-start(f32[45,256]{1,0:T(8,128)} %own_ref.1) | copy-start | bytes 138244
  0.0 15.5 %collective-permute-start = (f32[1,12,45,256]{3,0,2,1:T(1,128)}, f32[1,12,45,256]{3,0,2,1:T(1,128)S(1)}, u32[]{:S(2)}, u32[]{:S(2)}) collective-permute-start(f32[1,12,45,256]{3,0,2,1:T(1,128)} %param.7), channel_id=1, source_target_pairs={{0,16},{1,17},{2,18},{3,19},{4,20},{5,21},{6,22},{7,23},{8,24},{9,... | collective-permute-start | bytes 1658888 | tf_op jit(solution)/shard_map/ppermute | solution.py:33
  1.6 12.1 %collective-permute-start.5 = (bf16[3,45,256]{2,1,0:T(8,128)(2,1)S(1)}, bf16[3,45,256]{2,1,0:T(8,128)(2,1)S(1)}, u32[]{:S(2)}, u32[]{:S(2)}) collective-permute-start(bf16[3,45,256]{2,1,0:T(8,128)(2,1)S(1)} %pad_maximum_fusion), channel_id=1, source_target_pairs={{0,17},{1,16},{2,19},{3,18},{4,21},{5,20},{6,23},{7,22},{8,25},{9,... | collective-permute-start | bytes 207368 | tf_op jit(solution)/shard_map/ppermute | solution.py:33
  4.3 8.3 %copy-start.1 = (f32[3,256]{1,0:T(4,128)S(1)}, f32[3,256]{1,0:T(4,128)}, u32[]{:S(2)}) copy-start(f32[3,256]{1,0:T(4,128)} %weight_ref.5) | copy-start | bytes 9220
  4.3 8.3 %copy-start.2 = (s32[2,256]{1,0:T(2,128)S(1)}, s32[2,256]{1,0:T(2,128)}, u32[]{:S(2)}) copy-start(s32[2,256]{1,0:T(2,128)} %mask_ref.3) | copy-start | bytes 6148
  4.4 8.3 %copy-start.3 = (s32[3,256]{1,0:T(4,128)S(1)}, s32[3,256]{1,0:T(4,128)}, u32[]{:S(2)}) copy-start(s32[3,256]{1,0:T(4,128)} %nbr_ref.1) | copy-start | bytes 9220
  4.4 8.3 %copy-start.5 = (f32[12]{0:T(128)S(1)}, f32[12]{0:T(128)}, u32[]{:S(2)}) copy-start(f32[12]{0:T(128)} %relax_ref.3) | copy-start | bytes 148
  4.4 14.1 %collective-permute-start.2 = (bf16[12,45,256]{2,1,0:T(8,128)(2,1)S(1)}, bf16[12,45,256]{2,1,0:T(8,128)(2,1)S(1)}, u32[]{:S(2)}, u32[]{:S(2)}) collective-permute-start(bf16[12,45,256]{2,1,0:T(8,128)(2,1)S(1)} %bitcast.9), channel_id=1, source_target_pairs={{0,30},{1,31},{2,16},{3,17},{4,18},{5,19},{6,20},{7,21},{8,22},{9,... | collective-permute-start | bytes 829448 | tf_op jit(solution)/shard_map/ppermute | solution.py:33
  10.7 7.8 %collective-permute-start.1 = (bf16[12,45,256]{2,1,0:T(8,128)(2,1)S(1)}, bf16[12,45,256]{2,1,0:T(8,128)(2,1)S(1)}, u32[]{:S(2)}, u32[]{:S(2)}) collective-permute-start(bf16[12,45,256]{2,1,0:T(8,128)(2,1)S(1)} %bitcast.10), channel_id=1, source_target_pairs={{0,18},{1,19},{2,20},{3,21},{4,22},{5,23},{6,24},{7,25},{8,26},{9,... | collective-permute-start | bytes 829448 | tf_op jit(solution)/shard_map/ppermute | solution.py:33
  12.0 5.8 %collective-permute-start.6 = (bf16[2,45,256]{2,1,0:T(8,128)(2,1)S(1)}, bf16[2,45,256]{2,1,0:T(8,128)(2,1)S(1)}, u32[]{:S(2)}, u32[]{:S(2)}) collective-permute-start(bf16[2,45,256]{2,1,0:T(8,128)(2,1)S(1)} %slice_bitcast_fusion), channel_id=1, source_target_pairs={{0,1},{1,0},{2,3},{3,2},{4,5},{5,4},{6,7},{7,6},{8,9},{9,8},{10,11... | collective-permute-start | bytes 138248 | tf_op jit(solution)/shard_map/ppermute | solution.py:33
  13.7 4.1 %collective-permute-start.4 = (bf16[2,45,256]{2,1,0:T(8,128)(2,1)S(1)}, bf16[2,45,256]{2,1,0:T(8,128)(2,1)S(1)}, u32[]{:S(2)}, u32[]{:S(2)}) collective-permute-start(bf16[2,45,256]{2,1,0:T(8,128)(2,1)S(1)} %slice_bitcast_fusion), channel_id=1, source_target_pairs={{0,31},{1,30},{2,17},{3,16},{4,19},{5,18},{6,21},{7,20},{8,23},{9,... | collective-permute-start | bytes 138248 | tf_op jit(solution)/shard_map/ppermute | solution.py:33
  15.5 3.0 %collective-permute-start.3 = (bf16[2,45,256]{2,1,0:T(8,128)(2,1)S(1)}, bf16[2,45,256]{2,1,0:T(8,128)(2,1)S(1)}, u32[]{:S(2)}, u32[]{:S(2)}) collective-permute-start(bf16[2,45,256]{2,1,0:T(8,128)(2,1)S(1)} %slice_bitcast_fusion), channel_id=1, source_target_pairs={{0,19},{1,18},{2,21},{3,20},{4,23},{5,22},{6,25},{7,24},{8,27},{9,... | collective-permute-start | bytes 138248 | tf_op jit(solution)/shard_map/ppermute | solution.py:33
  18.5 0.7 %copy-start.4 = (f32[12]{0:T(128)S(1)}, f32[12]{0:T(128)}, u32[]{:S(2)}) copy-start(f32[12]{0:T(128)} %diff_ref.3) | copy-start | bytes 148
  19.7 14.8 %collective-permute-start.7 = (f32[14,45,256]{2,1,0:T(8,128)S(1)}, f32[14,45,256]{2,1,0:T(8,128)S(1)}, u32[]{:S(2)}, u32[]{:S(2)}) collective-permute-start(f32[14,45,256]{2,1,0:T(8,128)S(1)} %get-tuple-element.22.full_ref), channel_id=1, source_target_pairs={{16,0},{17,1},{18,2},{19,3},{20,4},{21,5},{22,6},{23,7},{24,8},{25... | collective-permute-start | bytes 1935368 | tf_op jit(solution)/shard_map/ppermute | solution.py:33
  22.0 8.6 %collective-permute-start.9 = (bf16[14,45,256]{2,1,0:T(8,128)(2,1)S(1)}, bf16[14,45,256]{2,1,0:T(8,128)(2,1)S(1)}, u32[]{:S(2)}, u32[]{:S(2)}) collective-permute-start(bf16[14,45,256]{2,1,0:T(8,128)(2,1)S(1)} %get-tuple-element.23), channel_id=1, source_target_pairs={{16,14},{17,15},{18,0},{19,1},{20,2},{21,3},{22,4},{23,5},{24,6},{... | collective-permute-start | bytes 967688 | tf_op jit(solution)/shard_map/ppermute | solution.py:33
  23.3 11.3 %collective-permute-start.8 = (bf16[14,45,256]{2,1,0:T(8,128)(2,1)S(1)}, bf16[14,45,256]{2,1,0:T(8,128)(2,1)S(1)}, u32[]{:S(2)}, u32[]{:S(2)}) collective-permute-start(bf16[14,45,256]{2,1,0:T(8,128)(2,1)S(1)} %get-tuple-element.23), channel_id=1, source_target_pairs={{16,2},{17,3},{18,4},{19,5},{20,6},{21,7},{22,8},{23,9},{24,10},{2... | collective-permute-start | bytes 967688 | tf_op jit(solution)/shard_map/ppermute | solution.py:33

commit v2 on v1

--- a/solution.py
+++ b/solution.py
@@ -8,11 +8,13 @@
 
 AXES = ("sec", "dom", "lev")
 SOLVED = 2
+PART = 5
 EDGES = 3
 LANES8 = 8
 LANES = 128
 VMEM = pl.BlockSpec(memory_space=pltpu.VMEM)
 SMEM = pl.BlockSpec(memory_space=pltpu.SMEM)
+ANY = pl.BlockSpec(memory_space=pl.ANY)
 F32 = jnp.float32
 BF16 = jnp.bfloat16
 
@@ -21,20 +23,33 @@
     return -(-count // unit) * unit
 
 
-def route(array, dom_step, swap_lev, pairs):
+def route(array, *moves):
     doms, levs = lax.axis_size("dom"), lax.axis_size("lev")
     place = lambda s, d, v: (s * doms + d) * levs + v
     table = [
-        (place(a, d, v), place(b, (d + step) % doms, v ^ flip))
-        for a, b, step, flip in [(a, b, dom_step, swap_lev) for a, b in pairs]
+        (place(a, d, v), place(b, (d + blocks) % doms, v ^ flip))
+        for a, b, blocks, flip in moves
         for d in range(doms)
         for v in range(levs)
     ]
     return lax.ppermute(array, AXES, table)
 
 
-def tendency_into(out_ref, state, mask, relax_ref):
-    fields = out_ref.shape[0]
+def strips(array):
+    return array.reshape(-1, LANES)
+
+
+def get_field(ref, f, half, parts):
+    rows = [pl.ds(f * half * parts + h, half, stride=parts) for h in range(parts)]
+    return jnp.concatenate([ref[r, :] for r in rows], axis=1)
+
+
+def put_field(ref, f, half, parts, value):
+    for h in range(parts):
+        ref[pl.ds(f * half * parts + h, half, stride=parts), :] = value[:, h * LANES : (h + 1) * LANES]
+
+
+def tendency(state, fields, mask, relax, emit):
     rounded = lambda f: state(f).astype(BF16).astype(F32)
     theta, vapour, cloud, rain = rounded(1), rounded(2), rounded(3), rounded(4)
     saturation = 0.6 * jnp.exp(0.25 * theta)
@@ -48,13 +63,13 @@
         4: autoconv - evaporate,
     }
     for f in range(fields):
-        clear = -relax_ref[f] * rounded(f)
+        clear = -relax(f) * rounded(f)
         if f in micro:
             clear = jnp.where(mask == 1, clear + micro[f], clear)
-        out_ref[f] = clear.astype(out_ref.dtype)
-
-
-def prepare_kernel(mine_ref, nbr_ref, weight_ref, mask_ref, relax_ref, gather_ref, lagged_ref):
+        emit(f, clear)
+
+
+def edge_matrix(gather_ref, nbr_ref, weight_ref):
     width = nbr_ref.shape[1]
     reach = gather_ref.shape[0]
     rows = 64
@@ -67,9 +82,27 @@
         gather_ref[start : start + rows, 0:width] = high
         gather_ref[start : start + rows, width : 2 * width] = (total - high.astype(F32)).astype(BF16)
 
+
+def prepare_kernel(
+    mine_ref, short_ref, kappa_ref, nbr_ref, weight_ref, mask_ref, relax_ref, diff_ref, after_ref,
+    gather_ref, lagged_ref, rates_ref, pack_ref,
+):
+    fields, half, width = lagged_ref.shape
+    for f in range(SOLVED):
+        pack_ref[f] = short_ref[f]
+    pack_ref[SOLVED] = kappa_ref[...].astype(BF16)
+    edge_matrix(gather_ref, nbr_ref, weight_ref)
+    for f in range(fields):
+        rates_ref[f : f + 1, :] = jnp.full((1, width), diff_ref[f], F32)
+        rates_ref[fields + f : fields + f + 1, :] = jnp.full((1, width), relax_ref[f], F32)
+
     @pl.when(lax.axis_index("sec") == 0)
     def _():
-        tendency_into(lagged_ref, lambda f: mine_ref[0, f], mask_ref[0:1, :], relax_ref)
+        def emit(f, value):
+            lagged_ref[f] = value.astype(BF16)
+
+        state = lambda f: get_field(mine_ref, f, half, width // LANES)
+        tendency(state, fields, mask_ref[0:1, :], lambda f: relax_ref[f], emit)
 
 
 def shift(values, by):
@@ -95,7 +128,7 @@
         ref[h, pl.ds(start, LANES8, stride=steps), :] = value[:, h * LANES : (h + 1) * LANES]
 
 
-def factor_kernel(own_ref, other_ref, low_ref, fore_ref, inv_ref, high_ref, back_ref, scan_ref, kappa, ratio, inverse):
+def factor_kernel(own_ref, pack_ref, low_ref, fore_ref, inv_ref, high_ref, back_ref, scan_ref, kappa, ratio, inverse):
     half, width = own_ref.shape
     depth = 2 * half
     steps = low_ref.shape[0]
@@ -106,11 +139,11 @@
     @pl.when(level == 0)
     def _():
         kappa[0:half, :] = own_ref[...]
-        kappa[half:depth, :] = other_ref[...].astype(F32)
+        kappa[half:depth, :] = pack_ref[SOLVED].astype(F32)
 
     @pl.when(level == 1)
     def _():
-        kappa[0:half, :] = other_ref[...].astype(F32)
+        kappa[0:half, :] = pack_ref[SOLVED].astype(F32)
         kappa[half:depth, :] = own_ref[...]
 
     excess = jnp.ones((1, width), F32)
@@ -172,7 +205,7 @@
         put_strided(right, t, steps, rows[t] + back_ref[t] * carry)
 
 
-def dynamics(own, left, right, weight_ref, diff_ref, gather_ref, factors, wide, flux, columns, emit, half, fields):
+def dynamics(own, left, right, weight_ref, rates_ref, gather_ref, factors, wide, flux, columns, emit, half, fields):
     slots = fields + SOLVED
     stride = wide.shape[0] // slots
     width = weight_ref.shape[1]
@@ -190,7 +223,8 @@
     total = weight_ref[0:1, :] + weight_ref[1:2, :] + weight_ref[2:3, :]
 
     def smoothed(f):
-        scale = diff_ref[f if f < fields else f - fields]
+        at = f % fields
+        scale = rates_ref[at : at + 1, :]
         mid = own(f)
         return mid + scale * (flux[f * stride : f * stride + half, :] - total * mid)
 
@@ -229,48 +263,69 @@
 
 
 def first_kernel(
-    state_ref, left_ref, right_ref, dleft_ref, dright_ref, across_ref, mine_ref, lag_ref, weight_ref, diff_ref, gather_ref,
-    *rest,
+    state_ref, left_ref, right_ref, dleft_ref, dright_ref, across_ref, pack_ref, mine_ref, weight_ref, rates_ref, gather_ref, *rest
 ):
-    factors, (full_ref, short_ref, wide, flux, columns) = rest[:6], rest[6:]
-    fields, half = state_ref.shape[1], state_ref.shape[2]
+    factors, (*full_refs, short_ref, wide, flux, columns) = rest[:6], rest[6:]
+    fields, half, width = mine_ref.shape
 
     def emit(f, value):
-        lagged = mine_ref[f] if f < fields else lag_ref[f - fields]
+        lagged = mine_ref[f] if f < fields else pack_ref[f - fields]
         value = value + lagged.astype(F32)
-        full_ref[f] = value
+        full_refs[f // PART][f % PART] = value
         short_ref[f] = value.astype(BF16)
 
     @pl.when(lax.axis_index("sec") == 1)
     def _():
         dynamics(
-            lambda f: state_ref[0, f] if f < fields else across_ref[f - fields].astype(F32),
+            lambda f: get_field(state_ref, f, half, width // LANES) if f < fields else across_ref[f - fields].astype(F32),
             lambda f: left_ref[f] if f < fields else dleft_ref[f - fields],
             lambda f: right_ref[f] if f < fields else dright_ref[f - fields],
-            weight_ref, diff_ref, gather_ref, factors, wide, flux, columns, emit, half, fields,
+            weight_ref, rates_ref, gather_ref, factors, wide, flux, columns, emit, half, fields,
         )
 
 
 def last_kernel(
-    state_ref, left_ref, right_ref, full_ref, lagged_ref, mask_ref, relax_ref, weight_ref, diff_ref, gather_ref, *rest
+    left_ref, right_ref, brief_ref, lagged_ref, mask_ref, weight_ref, rates_ref, gather_ref, *rest
 ):
-    factors, (out_ref, wide, flux, columns) = rest[:6], rest[6:]
-    fields, half = out_ref.shape[1], out_ref.shape[2]
+    count = -(-left_ref.shape[0] // PART)
+    states, rest = rest[:count], rest[count:]
+    factors, (out_ref, wide, flux, columns, held, sems) = rest[:6], rest[6:]
+    fields, half, width = lagged_ref.shape
+    parts = width // LANES
+
+    def send(low, high, sem):
+        rows = pl.ds(low * half * parts, (high - low) * half * parts)
+        return pltpu.make_async_copy(held.at[rows], out_ref.at[rows], sems.at[sem])
 
     def emit(f, value):
         if f < fields:
-            out_ref[0, f] = value + lagged_ref[f].astype(F32)
+            put_field(held, f, half, parts, value + lagged_ref[f].astype(F32))
+            if f == fields - 1:
+                send(SOLVED, fields, 0).start()
 
     @pl.when(lax.axis_index("sec") == 0)
     def _():
         dynamics(
-            lambda f: state_ref[f], lambda f: left_ref[f], lambda f: right_ref[f],
-            weight_ref, diff_ref, gather_ref, factors, wide, flux, columns, emit, half, fields,
+            lambda f: states[f // PART][f % PART], lambda f: left_ref[f], lambda f: right_ref[f],
+            weight_ref, rates_ref, gather_ref, factors, wide, flux, columns, emit, half, fields,
         )
 
     @pl.when(lax.axis_index("sec") == 1)
     def _():
-        tendency_into(out_ref.at[0], lambda f: full_ref[f], mask_ref[1:2, :], relax_ref)
+        def keep(f, value):
+            put_field(held, f, half, parts, value)
+
+        relax = lambda f: rates_ref[fields + f : fields + f + 1, :]
+        tendency(lambda f: brief_ref[f].astype(F32), fields, mask_ref[1:2, :], relax, keep)
+        send(SOLVED, fields, 0).start()
+
+    send(0, SOLVED, 1).start()
+    send(SOLVED, fields, 0).wait()
+    send(0, SOLVED, 1).wait()
+
+
+def cost(us):
+    return pl.CostEstimate(flops=0, transcendentals=0, bytes_accessed=int(us * 3e6))
 
 
 def params(mib):
@@ -285,24 +340,31 @@
     slots = fields + SOLVED
     reach = 3 * width
 
+    mine = strips(sections)
     short = sections[0].astype(BF16)
-    solved_short = short[0:SOLVED]
-    left = route(short, 1, 0, [(0, 1)])
-    right = route(short, -1, 0, [(0, 1)])
-    pack = jnp.concatenate([solved_short, vert_coef.astype(BF16)[None]], axis=0)
-    across = route(pack, 0, 1, [(0, 1), (1, 0)])
-    lag = route(solved_short, 0, 1, [(0, 0), (1, 1)])
-    dleft = route(solved_short, 1, 1, [(0, 1)])
-    dright = route(solved_short, -1, 1, [(0, 1)])
-    state = route(sections, 0, 0, [(0, 1), (1, 0)])
-
-    gather, lagged = pl.pallas_call(
+    head = short[0:SOLVED]
+    back = (1, 0, 0, 0)
+    state = route(mine, (0, 1, 0, 0), (1, 0, 0, 0))
+    left = route(short, (0, 1, 1, 0), back)
+    right = route(short, (0, 1, -1, 0), back)
+    dleft = route(head, (0, 1, 1, 1), back)
+    dright = route(head, (0, 1, -1, 1), back)
+
+    gather, lagged, rates, pack = pl.pallas_call(
         prepare_kernel,
-        out_shape=[shape((reach, 2 * width), BF16), shape((fields, half, width), BF16)],
-        in_specs=[VMEM] * 4 + [SMEM],
-        out_specs=[VMEM] * 2,
-        compiler_params=params(16),
-    )(sections, neighbours, edge_weight, precip_mask, relax_rate)
+        out_shape=[
+            shape((reach, 2 * width), BF16),
+            shape((fields, half, width), BF16),
+            shape((2 * fields, width), F32),
+            shape((SOLVED + 1, half, width), BF16),
+        ],
+        in_specs=[VMEM] * 6 + [SMEM] * 2 + [ANY],
+        out_specs=[VMEM] * 4,
+        compiler_params=params(8),
+        cost_estimate=cost(0.01),
+    )(mine, short, vert_coef, neighbours, edge_weight, precip_mask, relax_rate, field_diff, state)
+    pack = route(pack, (0, 0, 0, 1), (1, 1, 0, 1))
+    across = route(pack, (0, 1, 0, 0), (1, 0, 0, 0))
 
     chunk = shape((steps, LANES8, width), F32)
     factors = pl.pallas_call(
@@ -315,34 +377,37 @@
             pltpu.VMEM((width // LANES, depth + 2 * LANES8, LANES), F32),
             pltpu.VMEM((width // LANES, depth, LANES), F32),
         ],
-        compiler_params=params(16),
-    )(vert_coef, across[SOLVED])
+        compiler_params=params(8),
+        cost_estimate=cost(0.01),
+    )(vert_coef, pack)
 
     scratch = [
         pltpu.VMEM((slots * up(half, 16), 4 * width), BF16),
         pltpu.VMEM((slots * up(half, 16), width), F32),
         pltpu.VMEM((SOLVED, width // LANES, depth, LANES), F32),
     ]
-    full, brief = pl.pallas_call(
+    *full, brief = pl.pallas_call(
         first_kernel,
-        out_shape=[shape((slots, half, width), F32), shape((slots, half, width), BF16)],
-        in_specs=[VMEM] * 9 + [SMEM] + [VMEM] * 7,
-        out_specs=[VMEM] * 2,
+        out_shape=[shape((min(PART, slots - f), half, width), F32) for f in range(0, slots, PART)]
+        + [shape((slots, half, width), BF16)],
+        in_specs=[VMEM] * 17,
+        out_specs=[VMEM] * (1 + -(-slots // PART)),
         scratch_shapes=scratch,
         compiler_params=params(32),
-    )(state, left, right, dleft, dright, across, short, lag, edge_weight, field_diff, gather, *factors)
-
-    left = route(brief, 1, 0, [(1, 0)])
-    right = route(brief, -1, 0, [(1, 0)])
-    state = route(full, 0, 0, [(1, 0), (0, 1)])
-    return pl.pallas_call(
+    )(state, left, right, dleft, dright, across, pack, short, edge_weight, rates, gather, *factors)
+
+    left = route(brief, (1, 0, 1, 0), (0, 1, 0, 0))
+    right = route(brief, (1, 0, -1, 0))
+    states = [route(part, (1, 0, 0, 0), (0, 1, 0, 0)) for part in full]
+    out = pl.pallas_call(
         last_kernel,
-        out_shape=shape(sections.shape, F32),
-        in_specs=[VMEM] * 6 + [SMEM, VMEM, SMEM] + [VMEM] * 7,
-        out_specs=VMEM,
-        scratch_shapes=scratch,
+        out_shape=shape(mine.shape, F32),
+        in_specs=[VMEM] * (14 + len(states)),
+        out_specs=ANY,
+        scratch_shapes=scratch + [pltpu.VMEM(mine.shape, F32), pltpu.SemaphoreType.DMA((2,))],
         compiler_params=params(32),
-    )(state, left, right, full, lagged, precip_mask, relax_rate, edge_weight, field_diff, gather, *factors)
+    )(left, right, brief, lagged, precip_mask, edge_weight, rates, gather, *states, *factors)
+    return out.reshape(sections.shape)
 
 
 def solution(mesh):

time: 37.8 us -> 31.3 us (0.83)
  local copies, waits for them, and re-layouts: 3.3 us -> 1.2 us
  starting transfers between devices: 19.2 us -> 17.2 us
  waiting for transfers between devices: 10.7 us -> 8.84 us
  Pallas kernels: 4.08 us -> 3.7 us
    ppermute x10 -> x12, starting transfers between devices: 19.2 us -> 17.2 us  [route(): return lax.ppermute(array, AXES, table)]
    ppermute x10 -> x12, waiting for transfers between devices: 10.7 us -> 8.84 us  [route(): return lax.ppermute(array, AXES, table)]
    pallas_call x1 -> x0, local copies, waits for them, and re-layouts: 1.37 us -> none  [shards(): pl.pallas_call(last_kernel, out_shape=shape(sections.shape, F32), in_spec...]
    unnamed x17 -> x16, local copies, waits for them, and re-layouts: 1.87 us -> 1.2 us
    pallas_call x2, Pallas kernels: 2.15 us -> 1.76 us  [the longest x1 1.74 us: shards(): pl.pallas_call(last_kernel, out_shape=shape(mine.shape, F32), in_specs=[V...]
  transfers between devices with their start and end apart: 10 -> 12, of which waited for: 3 -> 4; matrix products, arithmetic and copies ran while one was open for 3% -> 4% of each run, Pallas kernels for 5% -> 3%
where the time goes in v2:
time: 31.3 us; the launch traced here: 31.1 us
  starting transfers between devices  17.2 us (55%)
  waiting for transfers between devices  8.84 us (28%)
  Pallas kernels  3.7 us (12%)
  local copies, waits for them, and re-layouts  1.2 us (4%)
    ppermute x12, starting transfers between devices, route(): return lax.ppermute(array, AXES, table)  17.2 us
    ppermute x12, waiting for transfers between devices, route(): return lax.ppermute(array, AXES, table)  8.84 us
    pallas_call x1, Pallas kernels, shards(): pl.pallas_call(last_kernel, out_shape=shape(mine.shape, F32), in_specs=[V...  1.74 us
    unnamed x16, local copies, waits for them, and re-layouts  1.2 us
    pallas_call x1, Pallas kernels, shards(): pl.pallas_call(prepare_kernel, out_shape=[shape((reach, 2 * width), BF16)...  1 us
    pallas_call x1, Pallas kernels, shards(): pl.pallas_call(factor_kernel, out_shape=[chunk] * 5 + [shape((6, LANES8,...  0.94 us
  transfers between devices with their start and end apart: 12, of which 4 were waited for; matrix products, arithmetic and copies ran while one was open for 4% of the time, Pallas kernels for 3%

profile of v2, /device:TPU:0, one launch (start us, length us, event | category | flops | bytes accessed | tf_op | source)
XLA Modules:
  0.0 31.1 jit_solution(17055064203691072519)
XLA Ops:
  0.0 0.0 copy-start
  0.0 0.0 copy-start.1
  0.0 0.5 %collective-permute-start = (f32[1080,128]{1,0:T(8,128)}, f32[1080,128]{1,0:T(8,128)S(1)}, u32[]{:S(2)}, u32[]{:S(2)}) collective-permute-start(f32[1080,128]{1,0:T(8,128)} %bitcast.7), channel_id=1, source_target_pairs={{0,16},{1,17},{2,18},{3,19},{4,20},{5,21},{6,22},{7,23},{8,24},{9,... | collective-permute-start | bytes 1658888 | tf_op jit(solution)/shard_map/ppermute | solution.py:35
  0.5 0.0 copy-start.2
  0.5 0.0 copy-start.3
  0.5 0.0 copy-start.4
  0.5 1.1 %copy.15 = bf16[1,12,45,256]{3,2,1,0:T(8,128)(2,1)S(1)} copy(f32[1,12,45,256]{3,0,2,1:T(1,128)} %param.7) | data formatting | bytes 829440 | tf_op args[0]
  1.6 0.0 copy-start.5
  1.6 0.0 copy-start.6
  1.6 0.6 %collective-permute-done.after_ref.state_ref = f32[1080,128]{1,0:T(8,128)S(1)} collective-permute-done((f32[1080,128]{1,0:T(8,128)}, f32[1080,128]{1,0:T(8,128)S(1)}, u32[]{:S(2)}, u32[]{:S(2)}) %collective-permute-start) | collective-permute-done | bytes 552992 | tf_op jit(solution)/shard_map/ppermute | solution.py:35
  2.2 0.0 copy-done
  2.2 0.0 copy-done.1
  2.3 0.0 copy-done.2
  2.3 0.0 copy-done.3
  2.3 0.0 copy-done.4
  2.3 0.0 copy-done.5
  2.3 0.0 copy-done.6
  2.3 1.0 %shard_map.73 = (bf16[768,512]{1,0:T(8,128)(2,1)S(1)}, bf16[12,45,256]{2,1,0:T(8,128)(2,1)S(1)}, f32[24,256]{1,0:T(8,128)S(1)}, bf16[3,45,256]{2,1,0:T(8,128)(2,1)S(1)}) custom-call(f32[1080,128]{1,0:T(8,128)S(1)} %bitcast.8, bf16[12,45,256]{2,1,0:T(8,128)(2,1)S(1)} %bitcast.9, f32[45,256]{1,0:T(8,128)S(1)} %copy-done.1, s32[3,256]{1,0:T(4,128)S(1)} %copy-done.4, ...), custom_call_target="tpu_custom_call" | custom-call | bytes 30000 | tf_op jit(solution)/shard_map/pallas_call | solution.py:353
  3.3 2.9 %collective-permute-start.5 = (bf16[3,45,256]{2,1,0:T(8,128)(2,1)S(1)}, bf16[3,45,256]{2,1,0:T(8,128)(2,1)S(1)}, u32[]{:S(2)}, u32[]{:S(2)}) collective-permute-start(bf16[3,45,256]{2,1,0:T(8,128)(2,1)S(1)} %get-tuple-element.19), channel_id=1, source_target_pairs={{0,1},{1,0},{2,3},{3,2},{4,5},{5,4},{6,7},{7,6},{8,9},{9,8},{10,11... | collective-permute-start | bytes 207368 | tf_op jit(solution)/shard_map/ppermute | solution.py:35
  6.2 3.9 %collective-permute-start.2 = (bf16[12,45,256]{2,1,0:T(8,128)(2,1)S(1)}, bf16[12,45,256]{2,1,0:T(8,128)(2,1)S(1)}, u32[]{:S(2)}, u32[]{:S(2)}) collective-permute-start(bf16[12,45,256]{2,1,0:T(8,128)(2,1)S(1)} %bitcast.10), channel_id=1, source_target_pairs={{0,30},{1,31},{2,16},{3,17},{4,18},{5,19},{6,20},{7,21},{8,22},{9,... | collective-permute-start | bytes 829448 | tf_op jit(solution)/shard_map/ppermute | solution.py:35
  10.1 0.0 collective-permute-start.1
  10.2 0.0 collective-permute-done.5.pack_ref
  10.2 0.6 %collective-permute-start.6 = (bf16[3,45,256]{2,1,0:T(8,128)(2,1)S(1)}, bf16[3,45,256]{2,1,0:T(8,128)(2,1)S(1)}, u32[]{:S(2)}, u32[]{:S(2)}) collective-permute-start(bf16[3,45,256]{2,1,0:T(8,128)(2,1)S(1)} %collective-permute-done.5.pack_ref), channel_id=1, source_target_pairs={{0,16},{1,17},{2,18},{3,19},{4,20},{5,21},{6,22},{7,23},{8,24},{9,... | collective-permute-start | bytes 207368 | tf_op jit(solution)/shard_map/ppermute | solution.py:35
  10.7 3.9 %collective-permute-start.4 = (bf16[2,45,256]{2,1,0:T(8,128)(2,1)S(1)}, bf16[2,45,256]{2,1,0:T(8,128)(2,1)S(1)}, u32[]{:S(2)}, u32[]{:S(2)}) collective-permute-start(bf16[2,45,256]{2,1,0:T(8,128)(2,1)S(1)} %slice_bitcast_fusion), channel_id=1, source_target_pairs={{0,31},{1,30},{2,17},{3,16},{4,19},{5,18},{6,21},{7,20},{8,23},{9,... | collective-permute-start | bytes 138248 | tf_op jit(solution)/shard_map/ppermute | solution.py:35
  14.7 0.0 collective-permute-start.3
  14.7 0.9 %shard_map.74 = (f32[12,8,256]{2,1,0:T(8,128)S(1)}, f32[12,8,256]{2,1,0:T(8,128)S(1)}, f32[12,8,256]{2,1,0:T(8,128)S(1)}, f32[12,8,256]{2,1,0:T(8,128)S(1)}, f32...) custom-call(f32[45,256]{1,0:T(8,128)S(1)} %copy-done.1, bf16[3,45,256]{2,1,0:T(8,128)(2,1)S(1)} %collective-permute-done.5.pack_ref), custom_call_target="tpu_custom_call" | custom-call | bytes 30000 | tf_op jit(solution)/shard_map/pallas_call | solution.py:370
  15.7 0.8 %collective-permute-done.4.dright_ref = bf16[2,45,256]{2,1,0:T(8,128)(2,1)S(1)} collective-permute-done((bf16[2,45,256]{2,1,0:T(8,128)(2,1)S(1)}, bf16[2,45,256]{2,1,0:T(8,128)(2,1)S(1)}, u32[]{:S(2)}, u32[]{:S(2)}) %collective-permute-start.4) | collective-permute-done | bytes 46112 | tf_op jit(solution)/shard_map/ppermute | solution.py:35
  16.4 0.0 collective-permute-done.3.dleft_ref
  16.5 0.0 collective-permute-done.2.right_ref
  16.5 0.0 collective-permute-done.1.left_ref
  16.5 0.0 collective-permute-done.6.across_ref
  16.5 1.3 %collective-permute-start.8 = (bf16[14,45,256]{2,1,0:T(8,128)(2,1)S(1)}, bf16[14,45,256]{2,1,0:T(8,128)(2,1)S(1)}, u32[]{:S(2)}, u32[]{:S(2)}) collective-permute-start(bf16[14,45,256]{2,1,0:T(8,128)(2,1)S(1)} %get-tuple-element.28.brief_ref), channel_id=1, source_target_pairs={{16,14},{17,15},{18,0},{19,1},{20,2},{21,3},{22,4},{23,5},{24,6},{... | collective-permute-start | bytes 967688 | tf_op jit(solution)/shard_map/ppermute | solution.py:35
  17.8 3.5 %collective-permute-start.7 = (bf16[14,45,256]{2,1,0:T(8,128)(2,1)S(1)}, bf16[14,45,256]{2,1,0:T(8,128)(2,1)S(1)}, u32[]{:S(2)}, u32[]{:S(2)}) collective-permute-start(bf16[14,45,256]{2,1,0:T(8,128)(2,1)S(1)} %get-tuple-element.28.brief_ref), channel_id=1, source_target_pairs={{16,2},{17,3},{18,4},{19,5},{20,6},{21,7},{22,8},{23,9},{24,10},{2... | collective-permute-start | bytes 967688 | tf_op jit(solution)/shard_map/ppermute | solution.py:35
  21.3 0.1 collective-permute-start.9
  21.4 0.4 %collective-permute-start.10 = (f32[5,45,256]{2,1,0:T(8,128)S(1)}, f32[5,45,256]{2,1,0:T(8,128)S(1)}, u32[]{:S(2)}, u32[]{:S(2)}) collective-permute-start(f32[5,45,256]{2,1,0:T(8,128)S(1)} %get-tuple-element.31), channel_id=1, source_target_pairs={{16,0},{17,1},{18,2},{19,3},{20,4},{21,5},{22,6},{23,7},{24,8},{25... | collective-permute-start | bytes 691208 | tf_op jit(solution)/shard_map/ppermute | solution.py:35
  21.9 0.1 collective-permute-start.11
  21.9 1.7 %collective-permute-done.11.rest_2_ = f32[4,45,256]{2,1,0:T(8,128)S(1)} collective-permute-done((f32[4,45,256]{2,1,0:T(8,128)S(1)}, f32[4,45,256]{2,1,0:T(8,128)S(1)}, u32[]{:S(2)}, u32[]{:S(2)}) %collective-permute-start.11) | collective-permute-done | bytes 184352 | tf_op jit(solution)/shard_map/ppermute | solution.py:35
  23.6 0.0 collective-permute-done.9.rest_0_
  23.6 0.0 collective-permute-done.10.rest_1_
  23.6 5.7 %collective-permute-done.8.right_ref = bf16[14,45,256]{2,1,0:T(8,128)(2,1)S(1)} collective-permute-done((bf16[14,45,256]{2,1,0:T(8,128)(2,1)S(1)}, bf16[14,45,256]{2,1,0:T(8,128)(2,1)S(1)}, u32[]{:S(2)}, u32[]{:S(2)}) %collective-permute-start.8) | collective-permute-done | bytes 322592 | tf_op jit(solution)/shard_map/ppermute | solution.py:35
  29.3 0.0 collective-permute-done.7.left_ref
  29.3 1.7 %shard_map.76 = f32[1080,128]{1,0:T(8,128)} custom-call(bf16[14,45,256]{2,1,0:T(8,128)(2,1)S(1)} %collective-permute-done.7.left_ref, bf16[14,45,256]{2,1,0:T(8,128)(2,1)S(1)} %collective-permute-done.8.right_ref, bf16[14,45,256]{2,1,0:T(8,128)(2,1)S(1)} %get-tuple-element.28.brief_ref, bf16[12,45,256]{2,1,0:T(8,128)(2,1)S(1)} %get-tuple-element.29.lagged_ref, ...), custom_call_target="tpu_custom_call" | custom-call | tf_op jit(solution)/shard_map/pallas_call | solution.py:402
  (3 shorter events, 0.1 us)
Async XLA Ops:
  0.0 2.2 %copy-start = (f32[1,12,45,256]{3,0,2,1:T(1,128)S(1)}, f32[1,12,45,256]{3,0,2,1:T(1,128)}, u32[]{:S(2)}) copy-start(f32[1,12,45,256]{3,0,2,1:T(1,128)} %param.7) | copy-start | bytes 1658884
  0.0 2.2 %copy-start.1 = (f32[45,256]{1,0:T(8,128)S(1)}, f32[45,256]{1,0:T(8,128)}, u32[]{:S(2)}) copy-start(f32[45,256]{1,0:T(8,128)} %own_ref.1) | copy-start | bytes 138244
  0.0 2.2 %collective-permute-start = (f32[1080,128]{1,0:T(8,128)}, f32[1080,128]{1,0:T(8,128)S(1)}, u32[]{:S(2)}, u32[]{:S(2)}) collective-permute-start(f32[1080,128]{1,0:T(8,128)} %bitcast.7), channel_id=1, source_target_pairs={{0,16},{1,17},{2,18},{3,19},{4,20},{5,21},{6,22},{7,23},{8,24},{9,... | collective-permute-start | bytes 1658888 | tf_op jit(solution)/shard_map/ppermute | solution.py:35
  0.5 1.8 %copy-start.2 = (f32[3,256]{1,0:T(4,128)S(1)}, f32[3,256]{1,0:T(4,128)}, u32[]{:S(2)}) copy-start(f32[3,256]{1,0:T(4,128)} %weight_ref.5) | copy-start | bytes 9220
  0.5 1.8 %copy-start.3 = (s32[2,256]{1,0:T(2,128)S(1)}, s32[2,256]{1,0:T(2,128)}, u32[]{:S(2)}) copy-start(s32[2,256]{1,0:T(2,128)} %mask_ref.3) | copy-start | bytes 6148
  0.5 1.8 %copy-start.4 = (s32[3,256]{1,0:T(4,128)S(1)}, s32[3,256]{1,0:T(4,128)}, u32[]{:S(2)}) copy-start(s32[3,256]{1,0:T(4,128)} %nbr_ref.1) | copy-start | bytes 9220
  1.6 0.7 %copy-start.5 = (f32[12]{0:T(128)S(1)}, f32[12]{0:T(128)}, u32[]{:S(2)}) copy-start(f32[12]{0:T(128)} %relax_ref.1) | copy-start | bytes 148
  1.6 0.7 %copy-start.6 = (f32[12]{0:T(128)S(1)}, f32[12]{0:T(128)}, u32[]{:S(2)}) copy-start(f32[12]{0:T(128)} %diff_ref.1) | copy-start | bytes 148
  3.3 6.9 %collective-permute-start.5 = (bf16[3,45,256]{2,1,0:T(8,128)(2,1)S(1)}, bf16[3,45,256]{2,1,0:T(8,128)(2,1)S(1)}, u32[]{:S(2)}, u32[]{:S(2)}) collective-permute-start(bf16[3,45,256]{2,1,0:T(8,128)(2,1)S(1)} %get-tuple-element.19), channel_id=1, source_target_pairs={{0,1},{1,0},{2,3},{3,2},{4,5},{5,4},{6,7},{7,6},{8,9},{9,8},{10,11... | collective-permute-start | bytes 207368 | tf_op jit(solution)/shard_map/ppermute | solution.py:35
  6.2 10.2 %collective-permute-start.2 = (bf16[12,45,256]{2,1,0:T(8,128)(2,1)S(1)}, bf16[12,45,256]{2,1,0:T(8,128)(2,1)S(1)}, u32[]{:S(2)}, u32[]{:S(2)}) collective-permute-start(bf16[12,45,256]{2,1,0:T(8,128)(2,1)S(1)} %bitcast.10), channel_id=1, source_target_pairs={{0,30},{1,31},{2,16},{3,17},{4,18},{5,19},{6,20},{7,21},{8,22},{9,... | collective-permute-start | bytes 829448 | tf_op jit(solution)/shard_map/ppermute | solution.py:35
  10.1 6.3 %collective-permute-start.1 = (bf16[12,45,256]{2,1,0:T(8,128)(2,1)S(1)}, bf16[12,45,256]{2,1,0:T(8,128)(2,1)S(1)}, u32[]{:S(2)}, u32[]{:S(2)}) collective-permute-start(bf16[12,45,256]{2,1,0:T(8,128)(2,1)S(1)} %bitcast.11), channel_id=1, source_target_pairs={{0,18},{1,19},{2,20},{3,21},{4,22},{5,23},{6,24},{7,25},{8,26},{9,... | collective-permute-start | bytes 829448 | tf_op jit(solution)/shard_map/ppermute | solution.py:35
  10.2 6.3 %collective-permute-start.6 = (bf16[3,45,256]{2,1,0:T(8,128)(2,1)S(1)}, bf16[3,45,256]{2,1,0:T(8,128)(2,1)S(1)}, u32[]{:S(2)}, u32[]{:S(2)}) collective-permute-start(bf16[3,45,256]{2,1,0:T(8,128)(2,1)S(1)} %collective-permute-done.5.pack_ref), channel_id=1, source_target_pairs={{0,16},{1,17},{2,18},{3,19},{4,20},{5,21},{6,22},{7,23},{8,24},{9,... | collective-permute-start | bytes 207368 | tf_op jit(solution)/shard_map/ppermute | solution.py:35
  10.7 5.7 %collective-permute-start.4 = (bf16[2,45,256]{2,1,0:T(8,128)(2,1)S(1)}, bf16[2,45,256]{2,1,0:T(8,128)(2,1)S(1)}, u32[]{:S(2)}, u32[]{:S(2)}) collective-permute-start(bf16[2,45,256]{2,1,0:T(8,128)(2,1)S(1)} %slice_bitcast_fusion), channel_id=1, source_target_pairs={{0,31},{1,30},{2,17},{3,16},{4,19},{5,18},{6,21},{7,20},{8,23},{9,... | collective-permute-start | bytes 138248 | tf_op jit(solution)/shard_map/ppermute | solution.py:35
  14.7 1.8 %collective-permute-start.3 = (bf16[2,45,256]{2,1,0:T(8,128)(2,1)S(1)}, bf16[2,45,256]{2,1,0:T(8,128)(2,1)S(1)}, u32[]{:S(2)}, u32[]{:S(2)}) collective-permute-start(bf16[2,45,256]{2,1,0:T(8,128)(2,1)S(1)} %slice_bitcast_fusion), channel_id=1, source_target_pairs={{0,19},{1,18},{2,21},{3,20},{4,23},{5,22},{6,25},{7,24},{8,27},{9,... | collective-permute-start | bytes 138248 | tf_op jit(solution)/shard_map/ppermute | solution.py:35
  16.5 12.8 %collective-permute-start.8 = (bf16[14,45,256]{2,1,0:T(8,128)(2,1)S(1)}, bf16[14,45,256]{2,1,0:T(8,128)(2,1)S(1)}, u32[]{:S(2)}, u32[]{:S(2)}) collective-permute-start(bf16[14,45,256]{2,1,0:T(8,128)(2,1)S(1)} %get-tuple-element.28.brief_ref), channel_id=1, source_target_pairs={{16,14},{17,15},{18,0},{19,1},{20,2},{21,3},{22,4},{23,5},{24,6},{... | collective-permute-start | bytes 967688 | tf_op jit(solution)/shard_map/ppermute | solution.py:35
  17.8 11.5 %collective-permute-start.7 = (bf16[14,45,256]{2,1,0:T(8,128)(2,1)S(1)}, bf16[14,45,256]{2,1,0:T(8,128)(2,1)S(1)}, u32[]{:S(2)}, u32[]{:S(2)}) collective-permute-start(bf16[14,45,256]{2,1,0:T(8,128)(2,1)S(1)} %get-tuple-element.28.brief_ref), channel_id=1, source_target_pairs={{16,2},{17,3},{18,4},{19,5},{20,6},{21,7},{22,8},{23,9},{24,10},{2... | collective-permute-start | bytes 967688 | tf_op jit(solution)/shard_map/ppermute | solution.py:35
  21.3 2.3 %collective-permute-start.9 = (f32[5,45,256]{2,1,0:T(8,128)S(1)}, f32[5,45,256]{2,1,0:T(8,128)S(1)}, u32[]{:S(2)}, u32[]{:S(2)}) collective-permute-start(f32[5,45,256]{2,1,0:T(8,128)S(1)} %get-tuple-element.30), channel_id=1, source_target_pairs={{16,0},{17,1},{18,2},{19,3},{20,4},{21,5},{22,6},{23,7},{24,8},{25... | collective-permute-start | bytes 691208 | tf_op jit(solution)/shard_map/ppermute | solution.py:35
  21.4 2.2 %collective-permute-start.10 = (f32[5,45,256]{2,1,0:T(8,128)S(1)}, f32[5,45,256]{2,1,0:T(8,128)S(1)}, u32[]{:S(2)}, u32[]{:S(2)}) collective-permute-start(f32[5,45,256]{2,1,0:T(8,128)S(1)} %get-tuple-element.31), channel_id=1, source_target_pairs={{16,0},{17,1},{18,2},{19,3},{20,4},{21,5},{22,6},{23,7},{24,8},{25... | collective-permute-start | bytes 691208 | tf_op jit(solution)/shard_map/ppermute | solution.py:35
  21.9 1.8 %collective-permute-start.11 = (f32[4,45,256]{2,1,0:T(8,128)S(1)}, f32[4,45,256]{2,1,0:T(8,128)S(1)}, u32[]{:S(2)}, u32[]{:S(2)}) collective-permute-start(f32[4,45,256]{2,1,0:T(8,128)S(1)} %get-tuple-element.32), channel_id=1, source_target_pairs={{16,0},{17,1},{18,2},{19,3},{20,4},{21,5},{22,6},{23,7},{24,8},{25... | collective-permute-start | bytes 552968 | tf_op jit(solution)/shard_map/ppermute | solution.py:35

commit v3 on v2

v3 whole, which is shorter than its diff:
```python
import jax
import jax.numpy as jnp
from jax import lax
from jax.experimental import pallas as pl
from jax.experimental.pallas import tpu as pltpu
from jax.sharding import PartitionSpec as P

AXES = ("sec", "dom", "lev")
SOLVED = 2
EDGES = 3
SUB = 8
LANES = 128
TILE = 16
CHUNK = 32
PIECES = 3
VMEM = pl.BlockSpec(memory_space=pltpu.VMEM)
SMEM = pl.BlockSpec(memory_space=pltpu.SMEM)
ANY = pl.BlockSpec(memory_space=pl.ANY)
F32 = jnp.float32
BF16 = jnp.bfloat16


def up(count, unit):
    return -(-count // unit) * unit


def spans(low, high, size):
    return [(r, min(r + size, high)) for r in range(low, high, size)]


def route(array, *moves):
    doms, levs = lax.axis_size("dom"), lax.axis_size("lev")
    place = lambda s, d, v: (s * doms + d) * levs + v
    table = [
        (place(a, d, v), place(b, (d + blocks) % doms, v ^ flip))
        for a, b, blocks, flip in moves
        for d in range(doms)
        for v in range(levs)
    ]
    return lax.ppermute(array, AXES, table)


def strips(array):
    return array.reshape(-1, LANES)


def get_rows(ref, low, high, parts):
    return jnp.concatenate([ref[pl.ds(low * parts + h, high - low, stride=parts), :] for h in range(parts)], axis=1)


def put_rows(ref, low, parts, value):
    for h in range(parts):
        ref[pl.ds(low * parts + h, value.shape[0], stride=parts), :] = value[:, h * LANES : (h + 1) * LANES]


def tendency(state, fields, mask, relax, emit):
    rounded = lambda f: state(f).astype(BF16).astype(F32)
    theta, vapour, cloud, rain = rounded(1), rounded(2), rounded(3), rounded(4)
    saturation = 0.6 * jnp.exp(0.25 * theta)
    condense = 0.5 * jnp.tanh(vapour - saturation)
    autoconv = 0.4 * cloud * cloud / (1.0 + cloud * cloud)
    evaporate = 0.3 * rain * rain / (1.0 + rain * rain) * jax.nn.sigmoid(saturation - vapour)
    micro = {
        1: 2.5 * (condense - evaporate),
        2: evaporate - condense,
        3: condense - autoconv,
        4: autoconv - evaporate,
    }
    for f in range(fields):
        clear = -relax(f) * rounded(f)
        if f in micro:
            clear = jnp.where(mask == 1, clear + micro[f], clear)
        emit(f, clear)


def shorten_kernel(mine_ref, short_ref, head_ref):
    own, width = short_ref.shape
    parts = width // LANES

    @pl.when(lax.axis_index("sec") == 0)
    def _():
        for low, high in spans(0, own, CHUNK):
            value = get_rows(mine_ref, low, high, parts).astype(BF16)
            short_ref[low:high, :] = value
            end = min(high, head_ref.shape[0])
            if low < end:
                head_ref[low:end, :] = value[: end - low]


def pack_kernel(head_ref, other_ref, kappa_ref, pack_ref):
    _, half, width = pack_ref.shape
    parts = width // LANES

    @pl.when(lax.axis_index("sec") == 0)
    def _():
        for f in range(SOLVED):
            pack_ref[f] = head_ref[f * half : (f + 1) * half, :]
            pack_ref[SOLVED + f] = get_rows(other_ref, f * half, (f + 1) * half, parts).astype(BF16)

    pack_ref[2 * SOLVED] = kappa_ref[...].astype(BF16)


def prepare_kernel(
    mine_ref, short_ref, nbr_ref, weight_ref, mask_ref, relax_ref, diff_ref, gather_ref, lagged_ref, rates_ref, keep_ref, take_ref, work,
    lagged,
):
    fields = rates_ref.shape[0]
    reach, width = gather_ref.shape[0], nbr_ref.shape[1]
    half = lagged_ref.shape[0] // fields
    base = up(fields * half, TILE)
    for low, high in spans(0, reach, 64):
        place = lax.broadcasted_iota(jnp.int32, (high - low, width), 0) + low
        total = jnp.zeros((high - low, width), F32)
        for edge in range(EDGES):
            total = total + jnp.where(place == nbr_ref[edge : edge + 1, :], weight_ref[edge : edge + 1, :], 0.0)
        first = total.astype(BF16)
        gather_ref[low:high, 0:width] = first
        gather_ref[low:high, width : 2 * width] = (total - first.astype(F32)).astype(BF16)
    total = weight_ref[0:1, :] + weight_ref[1:2, :] + weight_ref[2:3, :]
    keep_ref[...] = jnp.zeros(keep_ref.shape, F32)
    take_ref[...] = jnp.zeros(take_ref.shape, F32)
    for f in range(fields):
        rates_ref[f : f + 1, :] = jnp.full((1, width), relax_ref[f], F32)
    for f in range(fields + SOLVED):
        low = f * half if f < fields else base + (f - fields) * half
        scale = diff_ref[f % fields]
        keep_ref[low : low + half, :] = jnp.broadcast_to(1.0 - scale * total, (half, width))
        take_ref[low : low + half, :] = jnp.full((half, width), scale, F32)

    @pl.when(lax.axis_index("sec") == 0)
    def _():
        def emit(f, value):
            lagged[f * half : (f + 1) * half, :] = value

        for low, high in spans(0, fields * half, CHUNK):
            work[low:high, :] = short_ref[low:high, :].astype(F32)
        tendency(
            lambda f: work[f * half : (f + 1) * half, :], fields, mask_ref[0:1, :], lambda f: relax_ref[f], emit
        )
        for low, high in spans(0, fields * half, CHUNK):
            lagged_ref[low:high, :] = lagged[low:high, :].astype(BF16)

    @pl.when(lax.axis_index("sec") == 1)
    def _():
        for low, high in spans(0, fields * half, CHUNK):
            lagged_ref[low:high, :] = get_rows(mine_ref, low, high, width // LANES).astype(BF16)


def shift(values, by):
    return pltpu.roll(values, by % SUB, 0)


def put(ref, start, value):
    for h in range(ref.shape[0]):
        ref[h, start : start + value.shape[0], :] = value[:, h * LANES : (h + 1) * LANES]


def get(ref, start, count):
    return jnp.concatenate([ref[h, start : start + count, :] for h in range(ref.shape[0])], axis=1)


def get_strided(ref, start, steps):
    rows = pl.ds(start, SUB, stride=steps)
    return jnp.concatenate([ref[h, rows, :] for h in range(ref.shape[0])], axis=1)


def put_strided(ref, start, steps, value):
    for h in range(ref.shape[0]):
        ref[h, pl.ds(start, SUB, stride=steps), :] = value[:, h * LANES : (h + 1) * LANES]


def factor_kernel(own_ref, pack_ref, low_ref, fore_ref, inv_ref, high_ref, back_ref, scan_ref, kappa, ratio, inverse):
    half, width = own_ref.shape
    depth = 2 * half
    steps = low_ref.shape[0]
    level = lax.axis_index("lev")
    other = pack_ref[2 * SOLVED].astype(F32)
    ratio[...] = jnp.zeros(ratio.shape, F32)
    inverse[...] = jnp.zeros(inverse.shape, F32)

    @pl.when(level == 0)
    def _():
        kappa[0:half, :] = own_ref[...]
        kappa[half:depth, :] = other

    @pl.when(level == 1)
    def _():
        kappa[0:half, :] = other
        kappa[half:depth, :] = own_ref[...]

    excess = jnp.ones((1, width), F32)
    for k in range(depth):
        here = kappa[k : k + 1, :]
        inv = 1.0 / (excess + here)
        down = here * inv
        put(inverse, k, inv)
        if k < depth - 1:
            put(ratio, SUB + k, down)
        excess = 1.0 + down * excess

    index = lax.broadcasted_iota(jnp.int32, (SUB, width), 0)
    running = None
    for t in range(steps):
        low = get_strided(ratio, SUB - 1 + t, steps)
        low_ref[t] = low
        running = low if running is None else running * low
        fore_ref[t] = running
        inv_ref[t] = get_strided(inverse, t, steps)
    one = jnp.where(index >= 1, running, 0.0)
    two = jnp.where(index >= 2, running * shift(running, 1), 0.0)
    four = jnp.where(index >= 4, two * shift(two, 2), 0.0)
    scan_ref[0], scan_ref[1], scan_ref[2] = one, two, four
    running = None
    for t in range(steps - 1, -1, -1):
        high = get_strided(ratio, SUB + t, steps)
        high_ref[t] = high
        running = high if running is None else running * high
        back_ref[t] = running
    one = jnp.where(index < SUB - 1, running, 0.0)
    two = jnp.where(index < SUB - 2, running * shift(running, -1), 0.0)
    four = jnp.where(index < SUB - 4, two * shift(two, -2), 0.0)
    scan_ref[3], scan_ref[4], scan_ref[5] = one, two, four


def solve(right, factors):
    low_ref, fore_ref, inv_ref, high_ref, back_ref, scan_ref = factors
    steps, _, width = low_ref.shape
    index = lax.broadcasted_iota(jnp.int32, (SUB, width), 0)
    rows = []
    for t in range(steps):
        row = get_strided(right, t, steps)
        if t:
            row = row + low_ref[t] * rows[-1]
        rows.append(row)
    carry = rows[-1]
    for i, by in enumerate((1, 2, 4)):
        carry = carry + scan_ref[i] * shift(carry, by)
    carry = jnp.where(index >= 1, shift(carry, 1), 0.0)
    rows = [(rows[t] + fore_ref[t] * carry) * inv_ref[t] for t in range(steps)]
    for t in range(steps - 2, -1, -1):
        rows[t] = rows[t] + high_ref[t] * rows[t + 1]
    carry = rows[0]
    for i, by in enumerate((1, 2, 4)):
        carry = carry + scan_ref[3 + i] * shift(carry, -by)
    carry = jnp.where(index < SUB - 1, shift(carry, -1), 0.0)
    for t in range(steps):
        put_strided(right, t, steps, rows[t] + back_ref[t] * carry)


def gathered(left, middle, right, gather_ref):
    width = gather_ref.shape[1] // 2
    high = middle.astype(BF16)
    low = (middle - high.astype(F32)).astype(BF16)
    mul = lambda rows, side, cols: jnp.dot(
        rows, gather_ref[side * width : (side + 1) * width, cols], preferred_element_type=F32
    )
    both = mul(left, 0, slice(None)) + mul(high, 1, slice(None)) + mul(right, 2, slice(None))
    return both[:, :width] + both[:, width:] + mul(low, 1, slice(0, width))


def solve_rows(smooth, columns, factors, half, base):
    level = lax.axis_index("lev")
    depth = 2 * half
    width = smooth.shape[1]
    for f in range(SOLVED):
        put(columns.at[f], depth, jnp.zeros((columns.shape[2] - depth, width), F32))
        mine = smooth[f * half : (f + 1) * half, :]
        theirs = smooth[base + f * half : base + (f + 1) * half, :]

        @pl.when(level == 0)
        def _():
            put(columns.at[f], 0, mine)
            put(columns.at[f], half, theirs)

        @pl.when(level == 1)
        def _():
            put(columns.at[f], 0, theirs)
            put(columns.at[f], half, mine)

    for f in range(SOLVED):
        solve(columns.at[f], factors)


def first_kernel(
    state_ref, left_ref, right_ref, dleft_ref, dright_ref, pack_ref, lagged_ref, keep_ref, take_ref, gather_ref, *rest
):
    factors, (*full_refs, short_ref, smooth, columns) = rest[:6], rest[6:]
    _, half, width = pack_ref.shape
    own = lagged_ref.shape[0]
    total = short_ref.shape[0]
    base = up(own, TILE)
    parts = width // LANES
    piece = full_refs[0].shape[0]

    @pl.when(lax.axis_index("sec") == 1)
    def _():
        middle = get_rows(state_ref, 0, own, parts)
        smooth[0:own, :] = middle * keep_ref[0:own, :] + take_ref[0:own, :] * gathered(
            left_ref[...], middle, right_ref[...], gather_ref
        )
        for f in range(SOLVED):
            smooth[base + f * half : base + (f + 1) * half, :] = pack_ref[f].astype(F32)
        rows = slice(base, base + SOLVED * half)
        middle = smooth[rows, :]
        smooth[rows, :] = middle * keep_ref[rows, :] + take_ref[rows, :] * gathered(
            dleft_ref[...], middle, dright_ref[...], gather_ref
        )
        solve_rows(smooth, columns, factors, half, base)
        for f in range(SOLVED):
            lag = pack_ref[SOLVED + f].astype(F32)

            @pl.when(lax.axis_index("lev") == 0)
            def _():
                smooth[f * half : (f + 1) * half, :] = get(columns.at[f], 0, half)
                smooth[base + f * half : base + (f + 1) * half, :] = get(columns.at[f], half, half) + lag

            @pl.when(lax.axis_index("lev") == 1)
            def _():
                smooth[f * half : (f + 1) * half, :] = get(columns.at[f], half, half)
                smooth[base + f * half : base + (f + 1) * half, :] = get(columns.at[f], 0, half) + lag

        for low, high in spans(0, total, CHUNK):
            value = smooth[low:high, :]
            if low < own:
                stop = min(high, own)
                value = smooth[low:stop, :] + lagged_ref[low:stop, :].astype(F32)
                smooth[low:stop, :] = value
                value = smooth[low:high, :]
            short_ref[low:high, :] = value.astype(BF16)
            full_refs[low // piece][low % piece : low % piece + high - low, :] = value


def last_kernel(left_ref, right_ref, brief_ref, lagged_ref, mask_ref, rates_ref, keep_ref, take_ref, gather_ref, *rest):
    pieces, factors, (out_ref, smooth, columns, held, sems) = rest[:PIECES], rest[PIECES : PIECES + 6], rest[PIECES + 6 :]
    own, width = lagged_ref.shape
    fields = rates_ref.shape[0]
    half = own // fields
    base = up(own, TILE)
    total = left_ref.shape[0]
    parts = width // LANES
    first = up(SOLVED * half, CHUNK)
    piece = pieces[0].shape[0]

    def send(low, high, sem):
        rows = pl.ds(low * parts, (high - low) * parts)
        return pltpu.make_async_copy(held.at[rows], out_ref.at[rows], sems.at[sem])

    @pl.when(lax.axis_index("sec") == 0)
    def _():
        for i in range(PIECES):
            low, high = i * piece, min((i + 1) * piece, total)
            rows = slice(low, high)
            middle = pieces[i][...]
            smooth[rows, :] = middle * keep_ref[rows, :] + take_ref[rows, :] * gathered(
                left_ref[rows, :], middle, right_ref[rows, :], gather_ref
            )
        for low, high in spans(first, own, CHUNK):
            put_rows(held, low, parts, smooth[low:high, :] + lagged_ref[low:high, :].astype(F32))
        send(first, own, 0).start()
        solve_rows(smooth, columns, factors, half, base)
        for f in range(SOLVED):

            @pl.when(lax.axis_index("lev") == 0)
            def _():
                smooth[f * half : (f + 1) * half, :] = get(columns.at[f], 0, half)

            @pl.when(lax.axis_index("lev") == 1)
            def _():
                smooth[f * half : (f + 1) * half, :] = get(columns.at[f], half, half)

        for low, high in spans(0, first, CHUNK):
            put_rows(held, low, parts, smooth[low:high, :] + lagged_ref[low:high, :].astype(F32))

    @pl.when(lax.axis_index("sec") == 1)
    def _():
        for low, high in spans(0, base, CHUNK):
            smooth[low:high, :] = brief_ref[low:high, :].astype(F32)

        def keep(f, value):
            put_rows(held, f * half, parts, value)

        relax = lambda f: rates_ref[f : f + 1, :]
        tendency(lambda f: smooth[f * half : (f + 1) * half, :], fields, mask_ref[1:2, :], relax, keep)
        send(first, own, 0).start()

    send(0, first, 1).start()
    send(first, own, 0).wait()
    send(0, first, 1).wait()


def cost(us):
    return pl.CostEstimate(flops=0, transcendentals=0, bytes_accessed=int(us * 3e6))


def params(mib):
    return pltpu.CompilerParams(vmem_limit_bytes=mib << 20)


def shards(sections, neighbours, edge_weight, field_diff, vert_coef, relax_rate, precip_mask):
    _, fields, half, width = sections.shape
    shape = jax.ShapeDtypeStruct
    steps = up(up(2 * half, SUB) // SUB, 4)
    depth = steps * SUB
    own = fields * half
    total = up(own, TILE) + up(SOLVED * half, TILE)
    piece = up(-(-total // PIECES), CHUNK)

    mine = strips(sections)
    short, head = pl.pallas_call(
        shorten_kernel,
        out_shape=[shape((own, width), BF16), shape((SOLVED * half, width), BF16)],
        in_specs=[VMEM],
        out_specs=[VMEM] * 2,
        compiler_params=params(4),
        cost_estimate=cost(0.01),
    )(mine)
    back = (1, 0, 0, 0)
    state = route(mine, (0, 1, 0, 0), (1, 0, 0, 0))
    left = route(short, (0, 1, 1, 0), back)
    right = route(short, (0, 1, -1, 0), back)
    dleft = route(head, (0, 1, 1, 1), back)
    dright = route(head, (0, 1, -1, 1), back)

    pack = pl.pallas_call(
        pack_kernel,
        out_shape=shape((2 * SOLVED + 1, half, width), BF16),
        in_specs=[VMEM] * 3,
        out_specs=VMEM,
        compiler_params=params(4),
        cost_estimate=cost(0.01),
    )(head, state, vert_coef)
    pack = route(pack, (0, 1, 0, 1), (1, 0, 0, 1))

    gather, lagged, rates, keep, take = pl.pallas_call(
        prepare_kernel,
        out_shape=[
            shape((3 * width, 2 * width), BF16),
            shape((own, width), BF16),
            shape((fields, width), F32),
            shape((total, width), F32),
            shape((total, width), F32),
        ],
        in_specs=[VMEM] * 5 + [SMEM] * 2,
        out_specs=[VMEM] * 5,
        scratch_shapes=[pltpu.VMEM((own, width), F32)] * 2,
        compiler_params=params(8),
        cost_estimate=cost(0.01),
    )(mine, short, neighbours, edge_weight, precip_mask, relax_rate, field_diff)

    chunk = shape((steps, SUB, width), F32)
    factors = pl.pallas_call(
        factor_kernel,
        out_shape=[chunk] * 5 + [shape((6, SUB, width), F32)],
        in_specs=[VMEM] * 2,
        out_specs=[VMEM] * 6,
        scratch_shapes=[
            pltpu.VMEM((2 * half, width), F32),
            pltpu.VMEM((width // LANES, depth + 2 * SUB, LANES), F32),
            pltpu.VMEM((width // LANES, depth, LANES), F32),
        ],
        compiler_params=params(8),
        cost_estimate=cost(0.01),
    )(vert_coef, pack)

    scratch = [pltpu.VMEM((total, width), F32), pltpu.VMEM((SOLVED, width // LANES, depth, LANES), F32)]
    *full, brief = pl.pallas_call(
        first_kernel,
        out_shape=[shape((high - low, width), F32) for low, high in spans(0, total, piece)] + [shape((total, width), BF16)],
        in_specs=[VMEM] * 16,
        out_specs=[VMEM] * (PIECES + 1),
        scratch_shapes=scratch,
        compiler_params=params(24),
    )(state, left, right, dleft, dright, pack, lagged, keep, take, gather, *factors)

    left = route(brief, (1, 0, 1, 0), (0, 1, 0, 0))
    right = route(brief, (1, 0, -1, 0))
    pieces = [route(part, (1, 0, 0, 0), (0, 1, 0, 0)) for part in full]
    out = pl.pallas_call(
        last_kernel,
        out_shape=shape(mine.shape, F32),
        in_specs=[VMEM] * (15 + PIECES),
        out_specs=ANY,
        scratch_shapes=scratch + [pltpu.VMEM(mine.shape, F32), pltpu.SemaphoreType.DMA((2,))],
        compiler_params=params(24),
    )(left, right, brief, lagged, precip_mask, rates, keep, take, gather, *pieces, *factors)
    return out.reshape(sections.shape)


def solution(mesh):
    return jax.shard_map(
        shards,
        mesh=mesh,
        in_specs=(
            P("sec", None, "lev", "dom"),
            P(None, "dom"),
            P(None, "dom"),
            P(),
            P("lev", "dom"),
            P(),
            P(None, "dom"),
        ),
        out_specs=P("sec", None, "lev", "dom"),
        check_vma=False,
    )
```

time: 31.3 us -> 28.4 us (0.907)
  starting transfers between devices: 17.2 us -> 14.1 us
  local copies, waits for them, and re-layouts: 1.2 us -> 1.87 us
  waiting for transfers between devices: 8.84 us -> 8.22 us
    ppermute x12 -> x11, starting transfers between devices: 17.2 us -> 14.1 us  [route(): return lax.ppermute(array, AXES, table)]
    unnamed x16, local copies, waits for them, and re-layouts: 1.2 us -> 1.87 us
    ppermute x12 -> x11, waiting for transfers between devices: 8.84 us -> 8.22 us  [route(): return lax.ppermute(array, AXES, table)]
    pallas_call x3 -> x5, Pallas kernels: 1.97 us -> 2.22 us  [the longest x1 1.18 us: shards(): pl.pallas_call(prepare_kernel, out_shape=[shape((3 * width, 2 * width), B...]
  transfers between devices with their start and end apart: 12 -> 11, of which waited for: 4 -> 3; matrix products, arithmetic and copies ran while one was open for 4% -> 0% of each run, Pallas kernels for 3% -> 8%
where the time goes in v3:
time: 28.4 us; the launch traced here: 28.2 us
  starting transfers between devices  14.1 us (50%)
  waiting for transfers between devices  8.22 us (29%)
  Pallas kernels  3.85 us (14%)
  local copies, waits for them, and re-layouts  1.87 us (7%)
    ppermute x11, starting transfers between devices, route(): return lax.ppermute(array, AXES, table)  14.1 us
    ppermute x11, waiting for transfers between devices, route(): return lax.ppermute(array, AXES, table)  8.22 us
    unnamed x16, local copies, waits for them, and re-layouts  1.87 us
    pallas_call x1, Pallas kernels, shards(): pl.pallas_call(last_kernel, out_shape=shape(mine.shape, F32), in_specs=[V...  1.64 us
    pallas_call x1, Pallas kernels, shards(): pl.pallas_call(prepare_kernel, out_shape=[shape((3 * width, 2 * width), B...  1.18 us
    pallas_call x1, Pallas kernels, shards(): pl.pallas_call(factor_kernel, out_shape=[chunk] * 5 + [shape((6, SUB, wid...  0.94 us
  transfers between devices with their start and end apart: 11, of which 3 were waited for; matrix products, arithmetic and copies ran while one was open for 0% of the time, Pallas kernels for 8%

profile of v3, /device:TPU:0, one launch (start us, length us, event | category | flops | bytes accessed | tf_op | source)
XLA Modules:
  0.0 28.2 jit_solution(17886584696123700904)
XLA Ops:
  0.0 0.5 %collective-permute-start = (f32[1080,128]{1,0:T(8,128)}, f32[1080,128]{1,0:T(8,128)S(1)}, u32[]{:S(2)}, u32[]{:S(2)}) collective-permute-start(f32[1080,128]{1,0:T(8,128)} %bitcast.2), channel_id=1, source_target_pairs={{0,16},{1,17},{2,18},{3,19},{4,20},{5,21},{6,22},{7,23},{8,24},{9,... | collective-permute-start | bytes 1658888 | tf_op jit(solution)/shard_map/ppermute | solution.py:40
  0.5 0.0 copy-start
  0.5 1.0 %copy-done = f32[1,12,45,256]{3,0,2,1:T(1,128)S(1)} copy-done((f32[1,12,45,256]{3,0,2,1:T(1,128)S(1)}, f32[1,12,45,256]{3,0,2,1:T(1,128)}, u32[]{:S(2)}) %copy-start) | copy-done | bytes 552984
  1.5 0.0 copy-start.1
  1.5 5.6 %collective-permute-start.2 = (bf16[540,256]{1,0:T(8,128)(2,1)S(1)}, bf16[540,256]{1,0:T(8,128)(2,1)S(1)}, u32[]{:S(2)}, u32[]{:S(2)}) collective-permute-start(bf16[540,256]{1,0:T(8,128)(2,1)S(1)} %get-tuple-element.22.short_ref), channel_id=1, source_target_pairs={{0,30},{1,31},{2,16},{3,17},{4,18},{5,19},{6,20},{7,21},{8,22},{9,... | collective-permute-start | bytes 829448 | tf_op jit(solution)/shard_map/ppermute | solution.py:40
  7.2 0.0 collective-permute-start.1
  7.2 0.0 collective-permute-done.other_ref.state_ref
  7.2 0.0 copy-start.2
  7.2 0.8 %copy-done.2 = f32[45,256]{1,0:T(8,128)S(1)} copy-done((f32[45,256]{1,0:T(8,128)S(1)}, f32[45,256]{1,0:T(8,128)}, u32[]{:S(2)}) %copy-start.2) | copy-done | bytes 46104
  8.0 0.0 copy-start.3
  8.0 0.0 copy-start.4
  8.0 0.0 copy-start.5
  8.0 0.0 copy-start.6
  8.0 0.0 copy-start.7
  8.0 1.7 %collective-permute-start.5 = (bf16[5,45,256]{2,1,0:T(8,128)(2,1)S(1)}, bf16[5,45,256]{2,1,0:T(8,128)(2,1)S(1)}, u32[]{:S(2)}, u32[]{:S(2)}) collective-permute-start(bf16[5,45,256]{2,1,0:T(8,128)(2,1)S(1)} %shard_map.74), channel_id=1, source_target_pairs={{0,17},{1,16},{2,19},{3,18},{4,21},{5,20},{6,23},{7,22},{8,25},{9,... | collective-permute-start | bytes 345608 | tf_op jit(solution)/shard_map/ppermute | solution.py:40
  9.7 0.6 %collective-permute-start.4 = (bf16[90,256]{1,0:T(8,128)(2,1)S(1)}, bf16[90,256]{1,0:T(8,128)(2,1)S(1)}, u32[]{:S(2)}, u32[]{:S(2)}) collective-permute-start(bf16[90,256]{1,0:T(8,128)(2,1)S(1)} %get-tuple-element.23.head_ref), channel_id=1, source_target_pairs={{0,31},{1,30},{2,17},{3,16},{4,19},{5,18},{6,21},{7,20},{8,23},{9,... | collective-permute-start | bytes 138248 | tf_op jit(solution)/shard_map/ppermute | solution.py:40
  10.3 0.0 collective-permute-start.3
  10.3 0.0 copy-done.1
  10.3 0.0 copy-done.3
  10.3 0.0 copy-done.4
  10.3 0.0 copy-done.5
  10.3 0.0 copy-done.6
  10.3 0.0 copy-done.7
  10.3 1.2 %shard_map.75 = (bf16[768,512]{1,0:T(8,128)(2,1)S(1)}, bf16[540,256]{1,0:T(8,128)(2,1)S(1)}, f32[12,256]{1,0:T(8,128)S(1)}, f32[640,256]{1,0:T(8,128)S(1)}, f32[640,256]{1,0:T(8,128)S(1)}) custom-call(f32[1080,128]{1,0:T(8,128)S(1)} %bitcast.4, bf16[540,256]{1,0:T(8,128)(2,1)S(1)} %get-tuple-element.22.short_ref, s32[3,256]{1,0:T(4,128)S(1)} %copy-done.4, ...), custom_call_target="tpu_custom_call" | custom-call | bytes 30000 | tf_op jit(solution)/shard_map/pallas_call | solution.py:434
  11.5 2.1 %collective-permute-done.5.pack_ref = bf16[5,45,256]{2,1,0:T(8,128)(2,1)S(1)} collective-permute-done((bf16[5,45,256]{2,1,0:T(8,128)(2,1)S(1)}, bf16[5,45,256]{2,1,0:T(8,128)(2,1)S(1)}, u32[]{:S(2)}, u32[]{:S(2)}) %collective-permute-start.5) | collective-permute-done | bytes 115232 | tf_op jit(solution)/shard_map/ppermute | solution.py:40
  13.6 0.9 %shard_map.76 = (f32[12,8,256]{2,1,0:T(8,128)S(1)}, f32[12,8,256]{2,1,0:T(8,128)S(1)}, f32[12,8,256]{2,1,0:T(8,128)S(1)}, f32[12,8,256]{2,1,0:T(8,128)S(1)}, f32...) custom-call(f32[45,256]{1,0:T(8,128)S(1)} %copy-done.2, bf16[5,45,256]{2,1,0:T(8,128)(2,1)S(1)} %collective-permute-done.5.pack_ref), custom_call_target="tpu_custom_call" | custom-call | bytes 30000 | tf_op jit(solution)/shard_map/pallas_call | solution.py:451
  14.6 0.0 collective-permute-done.4.dright_ref
  14.6 0.0 collective-permute-done.3.dleft_ref
  14.6 0.0 collective-permute-done.2.right_ref
  14.6 0.0 collective-permute-done.1.left_ref
  14.7 1.3 %collective-permute-start.7 = (bf16[640,256]{1,0:T(8,128)(2,1)S(1)}, bf16[640,256]{1,0:T(8,128)(2,1)S(1)}, u32[]{:S(2)}, u32[]{:S(2)}) collective-permute-start(bf16[640,256]{1,0:T(8,128)(2,1)S(1)} %get-tuple-element.34.brief_ref), channel_id=1, source_target_pairs={{16,14},{17,15},{18,0},{19,1},{20,2},{21,3},{22,4},{23,5},{24,6},{... | collective-permute-start | bytes 983048 | tf_op jit(solution)/shard_map/ppermute | solution.py:40
  16.0 3.9 %collective-permute-start.6 = (bf16[640,256]{1,0:T(8,128)(2,1)S(1)}, bf16[640,256]{1,0:T(8,128)(2,1)S(1)}, u32[]{:S(2)}, u32[]{:S(2)}) collective-permute-start(bf16[640,256]{1,0:T(8,128)(2,1)S(1)} %get-tuple-element.34.brief_ref), channel_id=1, source_target_pairs={{16,2},{17,3},{18,4},{19,5},{20,6},{21,7},{22,8},{23,9},{24,10},{2... | collective-permute-start | bytes 983048 | tf_op jit(solution)/shard_map/ppermute | solution.py:40
  19.9 0.1 collective-permute-start.8
  20.0 0.4 %collective-permute-start.9 = (f32[224,256]{1,0:T(8,128)S(1)}, f32[224,256]{1,0:T(8,128)S(1)}, u32[]{:S(2)}, u32[]{:S(2)}) collective-permute-start(f32[224,256]{1,0:T(8,128)S(1)} %get-tuple-element.37), channel_id=1, source_target_pairs={{16,0},{17,1},{18,2},{19,3},{20,4},{21,5},{22,6},{23,7},{24,8},{25... | collective-permute-start | bytes 688136 | tf_op jit(solution)/shard_map/ppermute | solution.py:40
  20.4 0.1 collective-permute-start.10
  20.5 1.6 %collective-permute-done.10.rest_2_ = f32[192,256]{1,0:T(8,128)S(1)} collective-permute-done((f32[192,256]{1,0:T(8,128)S(1)}, f32[192,256]{1,0:T(8,128)S(1)}, u32[]{:S(2)}, u32[]{:S(2)}) %collective-permute-start.10) | collective-permute-done | bytes 196640 | tf_op jit(solution)/shard_map/ppermute | solution.py:40
  22.1 0.0 collective-permute-done.8.rest_0_
  22.1 0.0 collective-permute-done.9.rest_1_
  22.1 4.5 %collective-permute-done.7.right_ref = bf16[640,256]{1,0:T(8,128)(2,1)S(1)} collective-permute-done((bf16[640,256]{1,0:T(8,128)(2,1)S(1)}, bf16[640,256]{1,0:T(8,128)(2,1)S(1)}, u32[]{:S(2)}, u32[]{:S(2)}) %collective-permute-start.7) | collective-permute-done | bytes 327712 | tf_op jit(solution)/shard_map/ppermute | solution.py:40
  26.6 0.0 collective-permute-done.6.left_ref
  26.6 1.6 %shard_map.78 = f32[1080,128]{1,0:T(8,128)} custom-call(bf16[640,256]{1,0:T(8,128)(2,1)S(1)} %collective-permute-done.6.left_ref, bf16[640,256]{1,0:T(8,128)(2,1)S(1)} %collective-permute-done.7.right_ref, bf16[640,256]{1,0:T(8,128)(2,1)S(1)} %get-tuple-element.34.brief_ref, bf16[540,256]{1,0:T(8,128)(2,1)S(1)} %get-tuple-element.24.lagged_ref, ...), custom_call_target="tpu_custom_call" | custom-call | tf_op jit(solution)/shard_map/pallas_call | solution.py:478
  (3 shorter events, 0.1 us)
Async XLA Ops:
  0.0 7.2 %collective-permute-start = (f32[1080,128]{1,0:T(8,128)}, f32[1080,128]{1,0:T(8,128)S(1)}, u32[]{:S(2)}, u32[]{:S(2)}) collective-permute-start(f32[1080,128]{1,0:T(8,128)} %bitcast.2), channel_id=1, source_target_pairs={{0,16},{1,17},{2,18},{3,19},{4,20},{5,21},{6,22},{7,23},{8,24},{9,... | collective-permute-start | bytes 1658888 | tf_op jit(solution)/shard_map/ppermute | solution.py:40
  0.5 1.1 %copy-start = (f32[1,12,45,256]{3,0,2,1:T(1,128)S(1)}, f32[1,12,45,256]{3,0,2,1:T(1,128)}, u32[]{:S(2)}) copy-start(f32[1,12,45,256]{3,0,2,1:T(1,128)} %param.7) | copy-start | bytes 1658884
  1.5 8.8 %copy-start.1 = (f32[1,12,45,256]{3,0,2,1:T(1,128)S(1)}, f32[1,12,45,256]{3,0,2,1:T(1,128)}, u32[]{:S(2)}) copy-start(f32[1,12,45,256]{3,0,2,1:T(1,128)} %param.7) | copy-start | bytes 1658884
  1.5 13.1 %collective-permute-start.2 = (bf16[540,256]{1,0:T(8,128)(2,1)S(1)}, bf16[540,256]{1,0:T(8,128)(2,1)S(1)}, u32[]{:S(2)}, u32[]{:S(2)}) collective-permute-start(bf16[540,256]{1,0:T(8,128)(2,1)S(1)} %get-tuple-element.22.short_ref), channel_id=1, source_target_pairs={{0,30},{1,31},{2,16},{3,17},{4,18},{5,19},{6,20},{7,21},{8,22},{9,... | collective-permute-start | bytes 829448 | tf_op jit(solution)/shard_map/ppermute | solution.py:40
  7.2 7.4 %collective-permute-start.1 = (bf16[540,256]{1,0:T(8,128)(2,1)S(1)}, bf16[540,256]{1,0:T(8,128)(2,1)S(1)}, u32[]{:S(2)}, u32[]{:S(2)}) collective-permute-start(bf16[540,256]{1,0:T(8,128)(2,1)S(1)} %get-tuple-element.22.short_ref), channel_id=1, source_target_pairs={{0,18},{1,19},{2,20},{3,21},{4,22},{5,23},{6,24},{7,25},{8,26},{9,... | collective-permute-start | bytes 829448 | tf_op jit(solution)/shard_map/ppermute | solution.py:40
  7.2 0.8 %copy-start.2 = (f32[45,256]{1,0:T(8,128)S(1)}, f32[45,256]{1,0:T(8,128)}, u32[]{:S(2)}) copy-start(f32[45,256]{1,0:T(8,128)} %own_ref.1) | copy-start | bytes 138244
  8.0 2.3 %copy-start.3 = (s32[2,256]{1,0:T(2,128)S(1)}, s32[2,256]{1,0:T(2,128)}, u32[]{:S(2)}) copy-start(s32[2,256]{1,0:T(2,128)} %mask_ref.3) | copy-start | bytes 6148
  8.0 2.3 %copy-start.4 = (s32[3,256]{1,0:T(4,128)S(1)}, s32[3,256]{1,0:T(4,128)}, u32[]{:S(2)}) copy-start(s32[3,256]{1,0:T(4,128)} %nbr_ref.1) | copy-start | bytes 9220
  8.0 2.3 %copy-start.5 = (f32[3,256]{1,0:T(4,128)S(1)}, f32[3,256]{1,0:T(4,128)}, u32[]{:S(2)}) copy-start(f32[3,256]{1,0:T(4,128)} %weight_ref.1) | copy-start | bytes 9220
  8.0 2.3 %copy-start.6 = (f32[12]{0:T(128)S(1)}, f32[12]{0:T(128)}, u32[]{:S(2)}) copy-start(f32[12]{0:T(128)} %relax_ref.1) | copy-start | bytes 148
  8.0 2.3 %copy-start.7 = (f32[12]{0:T(128)S(1)}, f32[12]{0:T(128)}, u32[]{:S(2)}) copy-start(f32[12]{0:T(128)} %diff_ref.1) | copy-start | bytes 148
  8.0 5.6 %collective-permute-start.5 = (bf16[5,45,256]{2,1,0:T(8,128)(2,1)S(1)}, bf16[5,45,256]{2,1,0:T(8,128)(2,1)S(1)}, u32[]{:S(2)}, u32[]{:S(2)}) collective-permute-start(bf16[5,45,256]{2,1,0:T(8,128)(2,1)S(1)} %shard_map.74), channel_id=1, source_target_pairs={{0,17},{1,16},{2,19},{3,18},{4,21},{5,20},{6,23},{7,22},{8,25},{9,... | collective-permute-start | bytes 345608 | tf_op jit(solution)/shard_map/ppermute | solution.py:40
  9.7 4.9 %collective-permute-start.4 = (bf16[90,256]{1,0:T(8,128)(2,1)S(1)}, bf16[90,256]{1,0:T(8,128)(2,1)S(1)}, u32[]{:S(2)}, u32[]{:S(2)}) collective-permute-start(bf16[90,256]{1,0:T(8,128)(2,1)S(1)} %get-tuple-element.23.head_ref), channel_id=1, source_target_pairs={{0,31},{1,30},{2,17},{3,16},{4,19},{5,18},{6,21},{7,20},{8,23},{9,... | collective-permute-start | bytes 138248 | tf_op jit(solution)/shard_map/ppermute | solution.py:40
  10.3 4.3 %collective-permute-start.3 = (bf16[90,256]{1,0:T(8,128)(2,1)S(1)}, bf16[90,256]{1,0:T(8,128)(2,1)S(1)}, u32[]{:S(2)}, u32[]{:S(2)}) collective-permute-start(bf16[90,256]{1,0:T(8,128)(2,1)S(1)} %get-tuple-element.23.head_ref), channel_id=1, source_target_pairs={{0,19},{1,18},{2,21},{3,20},{4,23},{5,22},{6,25},{7,24},{8,27},{9,... | collective-permute-start | bytes 138248 | tf_op jit(solution)/shard_map/ppermute | solution.py:40
  14.7 11.9 %collective-permute-start.7 = (bf16[640,256]{1,0:T(8,128)(2,1)S(1)}, bf16[640,256]{1,0:T(8,128)(2,1)S(1)}, u32[]{:S(2)}, u32[]{:S(2)}) collective-permute-start(bf16[640,256]{1,0:T(8,128)(2,1)S(1)} %get-tuple-element.34.brief_ref), channel_id=1, source_target_pairs={{16,14},{17,15},{18,0},{19,1},{20,2},{21,3},{22,4},{23,5},{24,6},{... | collective-permute-start | bytes 983048 | tf_op jit(solution)/shard_map/ppermute | solution.py:40
  16.0 10.6 %collective-permute-start.6 = (bf16[640,256]{1,0:T(8,128)(2,1)S(1)}, bf16[640,256]{1,0:T(8,128)(2,1)S(1)}, u32[]{:S(2)}, u32[]{:S(2)}) collective-permute-start(bf16[640,256]{1,0:T(8,128)(2,1)S(1)} %get-tuple-element.34.brief_ref), channel_id=1, source_target_pairs={{16,2},{17,3},{18,4},{19,5},{20,6},{21,7},{22,8},{23,9},{24,10},{2... | collective-permute-start | bytes 983048 | tf_op jit(solution)/shard_map/ppermute | solution.py:40
  19.9 2.2 %collective-permute-start.8 = (f32[224,256]{1,0:T(8,128)S(1)}, f32[224,256]{1,0:T(8,128)S(1)}, u32[]{:S(2)}, u32[]{:S(2)}) collective-permute-start(f32[224,256]{1,0:T(8,128)S(1)} %get-tuple-element.36), channel_id=1, source_target_pairs={{16,0},{17,1},{18,2},{19,3},{20,4},{21,5},{22,6},{23,7},{24,8},{25... | collective-permute-start | bytes 688136 | tf_op jit(solution)/shard_map/ppermute | solution.py:40
  20.0 2.1 %collective-permute-start.9 = (f32[224,256]{1,0:T(8,128)S(1)}, f32[224,256]{1,0:T(8,128)S(1)}, u32[]{:S(2)}, u32[]{:S(2)}) collective-permute-start(f32[224,256]{1,0:T(8,128)S(1)} %get-tuple-element.37), channel_id=1, source_target_pairs={{16,0},{17,1},{18,2},{19,3},{20,4},{21,5},{22,6},{23,7},{24,8},{25... | collective-permute-start | bytes 688136 | tf_op jit(solution)/shard_map/ppermute | solution.py:40
  20.4 1.7 %collective-permute-start.10 = (f32[192,256]{1,0:T(8,128)S(1)}, f32[192,256]{1,0:T(8,128)S(1)}, u32[]{:S(2)}, u32[]{:S(2)}) collective-permute-start(f32[192,256]{1,0:T(8,128)S(1)} %get-tuple-element.38), channel_id=1, source_target_pairs={{16,0},{17,1},{18,2},{19,3},{20,4},{21,5},{22,6},{23,7},{24,8},{25... | collective-permute-start | bytes 589832 | tf_op jit(solution)/shard_map/ppermute | solution.py:40

commit v4 on v3

--- a/solution.py
+++ b/solution.py
@@ -1,3 +1,4 @@
+import functools
 import jax
 import jax.numpy as jnp
 from jax import lax
@@ -32,12 +33,24 @@
     doms, levs = lax.axis_size("dom"), lax.axis_size("lev")
     place = lambda s, d, v: (s * doms + d) * levs + v
     table = [
-        (place(a, d, v), place(b, (d + blocks) % doms, v ^ flip))
-        for a, b, blocks, flip in moves
+        (place(a, d, v), place(b, to_block(d) % doms, v ^ flip))
+        for a, b, to_block, flip in moves
         for d in range(doms)
         for v in range(levs)
     ]
     return lax.ppermute(array, AXES, table)
+
+
+def same(block):
+    return block
+
+
+def near(block):
+    return block ^ 1
+
+
+def far(block):
+    return block - 1 if block % 2 == 0 else block + 1
 
 
 def strips(array):
@@ -108,8 +121,10 @@
     reach, width = gather_ref.shape[0], nbr_ref.shape[1]
     half = lagged_ref.shape[0] // fields
     base = up(fields * half, TILE)
+    odd = lax.axis_index("dom") % 2
+    sides = (2 * width * (1 - odd), width, 2 * width * odd)
     for low, high in spans(0, reach, 64):
-        place = lax.broadcasted_iota(jnp.int32, (high - low, width), 0) + low
+        place = lax.broadcasted_iota(jnp.int32, (high - low, width), 0) + (low % width + sides[low // width])
         total = jnp.zeros((high - low, width), F32)
         for edge in range(EDGES):
             total = total + jnp.where(place == nbr_ref[edge : edge + 1, :], weight_ref[edge : edge + 1, :], 0.0)
@@ -169,12 +184,21 @@
         ref[h, pl.ds(start, SUB, stride=steps), :] = value[:, h * LANES : (h + 1) * LANES]
 
 
-def factor_kernel(own_ref, pack_ref, low_ref, fore_ref, inv_ref, high_ref, back_ref, scan_ref, kappa, ratio, inverse):
+def factor_kernel(
+    core, at, own_ref, other_ref, low_ref, fore_ref, inv_ref, high_ref, back_ref, scan_ref, kappa, ratio, inverse
+):
+    @pl.when(lax.axis_index("sec") == core)
+    def _():
+        factor(
+            own_ref, other_ref[at].astype(F32), low_ref, fore_ref, inv_ref, high_ref, back_ref, scan_ref, kappa, ratio, inverse
+        )
+
+
+def factor(own_ref, other, low_ref, fore_ref, inv_ref, high_ref, back_ref, scan_ref, kappa, ratio, inverse):
     half, width = own_ref.shape
     depth = 2 * half
     steps = low_ref.shape[0]
     level = lax.axis_index("lev")
-    other = pack_ref[2 * SOLVED].astype(F32)
     ratio[...] = jnp.zeros(ratio.shape, F32)
     inverse[...] = jnp.zeros(inverse.shape, F32)
 
@@ -247,14 +271,14 @@
         put_strided(right, t, steps, rows[t] + back_ref[t] * carry)
 
 
-def gathered(left, middle, right, gather_ref):
+def gathered(near_rows, middle, far_rows, gather_ref):
     width = gather_ref.shape[1] // 2
     high = middle.astype(BF16)
     low = (middle - high.astype(F32)).astype(BF16)
     mul = lambda rows, side, cols: jnp.dot(
         rows, gather_ref[side * width : (side + 1) * width, cols], preferred_element_type=F32
     )
-    both = mul(left, 0, slice(None)) + mul(high, 1, slice(None)) + mul(right, 2, slice(None))
+    both = mul(near_rows, 0, slice(None)) + mul(high, 1, slice(None)) + mul(far_rows, 2, slice(None))
     return both[:, :width] + both[:, width:] + mul(low, 1, slice(0, width))
 
 
@@ -282,7 +306,7 @@
 
 
 def first_kernel(
-    state_ref, left_ref, right_ref, dleft_ref, dright_ref, pack_ref, lagged_ref, keep_ref, take_ref, gather_ref, *rest
+    state_ref, far_ref, near_ref, dfar_ref, dnear_ref, pack_ref, lagged_ref, keep_ref, take_ref, gather_ref, *rest
 ):
     factors, (*full_refs, short_ref, smooth, columns) = rest[:6], rest[6:]
     _, half, width = pack_ref.shape
@@ -292,18 +316,24 @@
     parts = width // LANES
     piece = full_refs[0].shape[0]
 
+    def store(low, value):
+        for i, (start, stop) in enumerate(spans(0, piece * PIECES, piece)):
+            a, b = max(low, start), min(low + value.shape[0], stop)
+            if a < b:
+                full_refs[i][a - start : b - start, :] = value[a - low : b - low]
+
     @pl.when(lax.axis_index("sec") == 1)
     def _():
         middle = get_rows(state_ref, 0, own, parts)
         smooth[0:own, :] = middle * keep_ref[0:own, :] + take_ref[0:own, :] * gathered(
-            left_ref[...], middle, right_ref[...], gather_ref
+            near_ref[...], middle, far_ref[...], gather_ref
         )
         for f in range(SOLVED):
             smooth[base + f * half : base + (f + 1) * half, :] = pack_ref[f].astype(F32)
         rows = slice(base, base + SOLVED * half)
         middle = smooth[rows, :]
         smooth[rows, :] = middle * keep_ref[rows, :] + take_ref[rows, :] * gathered(
-            dleft_ref[...], middle, dright_ref[...], gather_ref
+            dnear_ref[...], middle, dfar_ref[...], gather_ref
         )
         solve_rows(smooth, columns, factors, half, base)
         for f in range(SOLVED):
@@ -327,16 +357,17 @@
                 smooth[low:stop, :] = value
                 value = smooth[low:high, :]
             short_ref[low:high, :] = value.astype(BF16)
-            full_refs[low // piece][low % piece : low % piece + high - low, :] = value
-
-
-def last_kernel(left_ref, right_ref, brief_ref, lagged_ref, mask_ref, rates_ref, keep_ref, take_ref, gather_ref, *rest):
+            store(low, value)
+        store(total, pack_ref[2 * SOLVED].astype(F32))
+
+
+def last_kernel(near_ref, far_ref, brief_ref, lagged_ref, mask_ref, rates_ref, keep_ref, take_ref, gather_ref, *rest):
     pieces, factors, (out_ref, smooth, columns, held, sems) = rest[:PIECES], rest[PIECES : PIECES + 6], rest[PIECES + 6 :]
     own, width = lagged_ref.shape
     fields = rates_ref.shape[0]
     half = own // fields
     base = up(own, TILE)
-    total = left_ref.shape[0]
+    total = near_ref.shape[0]
     parts = width // LANES
     first = up(SOLVED * half, CHUNK)
     piece = pieces[0].shape[0]
@@ -350,9 +381,9 @@
         for i in range(PIECES):
             low, high = i * piece, min((i + 1) * piece, total)
             rows = slice(low, high)
-            middle = pieces[i][...]
+            middle = pieces[i][0 : high - low, :]
             smooth[rows, :] = middle * keep_ref[rows, :] + take_ref[rows, :] * gathered(
-                left_ref[rows, :], middle, right_ref[rows, :], gather_ref
+                near_ref[rows, :], middle, far_ref[rows, :], gather_ref
             )
         for low, high in spans(first, own, CHUNK):
             put_rows(held, low, parts, smooth[low:high, :] + lagged_ref[low:high, :].astype(F32))
@@ -389,7 +420,7 @@
 
 
 def cost(us):
-    return pl.CostEstimate(flops=0, transcendentals=0, bytes_accessed=int(us * 3e6))
+    return pl.CostEstimate(flops=int(us * 1e9), transcendentals=0, bytes_accessed=0)
 
 
 def params(mib):
@@ -403,7 +434,7 @@
     depth = steps * SUB
     own = fields * half
     total = up(own, TILE) + up(SOLVED * half, TILE)
-    piece = up(-(-total // PIECES), CHUNK)
+    piece = up(-(-(total + half) // PIECES), SUB)
 
     mine = strips(sections)
     short, head = pl.pallas_call(
@@ -414,12 +445,12 @@
         compiler_params=params(4),
         cost_estimate=cost(0.01),
     )(mine)
-    back = (1, 0, 0, 0)
-    state = route(mine, (0, 1, 0, 0), (1, 0, 0, 0))
-    left = route(short, (0, 1, 1, 0), back)
-    right = route(short, (0, 1, -1, 0), back)
-    dleft = route(head, (0, 1, 1, 1), back)
-    dright = route(head, (0, 1, -1, 1), back)
+    back = (1, 0, same, 0)
+    state = route(mine, (0, 1, same, 0), back)
+    near_rows = route(short, (0, 1, near, 0), back)
+    far_rows = route(short, (0, 1, far, 0), back)
+    dnear = route(head, (0, 1, near, 1), back)
+    dfar = route(head, (0, 1, far, 1), back)
 
     pack = pl.pallas_call(
         pack_kernel,
@@ -429,7 +460,7 @@
         compiler_params=params(4),
         cost_estimate=cost(0.01),
     )(head, state, vert_coef)
-    pack = route(pack, (0, 1, 0, 1), (1, 0, 0, 1))
+    pack = route(pack, (0, 1, same, 1), back)
 
     gather, lagged, rates, keep, take = pl.pallas_call(
         prepare_kernel,
@@ -448,33 +479,38 @@
     )(mine, short, neighbours, edge_weight, precip_mask, relax_rate, field_diff)
 
     chunk = shape((steps, SUB, width), F32)
-    factors = pl.pallas_call(
-        factor_kernel,
-        out_shape=[chunk] * 5 + [shape((6, SUB, width), F32)],
-        in_specs=[VMEM] * 2,
-        out_specs=[VMEM] * 6,
-        scratch_shapes=[
-            pltpu.VMEM((2 * half, width), F32),
-            pltpu.VMEM((width // LANES, depth + 2 * SUB, LANES), F32),
-            pltpu.VMEM((width // LANES, depth, LANES), F32),
-        ],
-        compiler_params=params(8),
-        cost_estimate=cost(0.01),
-    )(vert_coef, pack)
+    def factors_of(core, at, other, us):
+        return pl.pallas_call(
+            functools.partial(factor_kernel, core, at),
+            out_shape=[chunk] * 5 + [shape((6, SUB, width), F32)],
+            in_specs=[VMEM] * 2,
+            out_specs=[VMEM] * 6,
+            scratch_shapes=[
+                pltpu.VMEM((2 * half, width), F32),
+                pltpu.VMEM((width // LANES, depth + 2 * SUB, LANES), F32),
+                pltpu.VMEM((width // LANES, depth, LANES), F32),
+            ],
+            compiler_params=params(8),
+            cost_estimate=cost(us),
+        )(vert_coef, other)
+
+    factors = factors_of(1, 2 * SOLVED, pack, 0.01)
 
     scratch = [pltpu.VMEM((total, width), F32), pltpu.VMEM((SOLVED, width // LANES, depth, LANES), F32)]
     *full, brief = pl.pallas_call(
         first_kernel,
-        out_shape=[shape((high - low, width), F32) for low, high in spans(0, total, piece)] + [shape((total, width), BF16)],
+        out_shape=[shape((piece, width), F32)] * PIECES + [shape((total, width), BF16)],
         in_specs=[VMEM] * 16,
         out_specs=[VMEM] * (PIECES + 1),
         scratch_shapes=scratch,
         compiler_params=params(24),
-    )(state, left, right, dleft, dright, pack, lagged, keep, take, gather, *factors)
-
-    left = route(brief, (1, 0, 1, 0), (0, 1, 0, 0))
-    right = route(brief, (1, 0, -1, 0))
-    pieces = [route(part, (1, 0, 0, 0), (0, 1, 0, 0)) for part in full]
+    )(state, far_rows, near_rows, dfar, dnear, pack, lagged, keep, take, gather, *factors)
+
+    near_rows = route(brief, (1, 0, near, 0), (0, 1, same, 0))
+    far_rows = route(brief, (1, 0, far, 0))
+    pieces = [route(part, back, (0, 1, same, 0)) for part in full]
+    last, low = divmod(total, piece)
+    factors = factors_of(0, slice(low, low + half), pieces[last], 0)
     out = pl.pallas_call(
         last_kernel,
         out_shape=shape(mine.shape, F32),
@@ -482,7 +518,7 @@
         out_specs=ANY,
         scratch_shapes=scratch + [pltpu.VMEM(mine.shape, F32), pltpu.SemaphoreType.DMA((2,))],
         compiler_params=params(24),
-    )(left, right, brief, lagged, precip_mask, rates, keep, take, gather, *pieces, *factors)
+    )(near_rows, far_rows, brief, lagged, precip_mask, rates, keep, take, gather, *pieces, *factors)
     return out.reshape(sections.shape)
 
 

time: 28.4 us -> 27.2 us (0.958)
  waiting for transfers between devices: 8.22 us -> 5.81 us
  starting transfers between devices: 14.1 us -> 15.2 us
    ppermute x11, waiting for transfers between devices: 8.22 us -> 5.81 us  [route(): return lax.ppermute(array, AXES, table)]
    ppermute x11, starting transfers between devices: 14.1 us -> 15.2 us  [route(): return lax.ppermute(array, AXES, table)]
    unnamed x16 -> x18, local copies, waits for them, and re-layouts: 1.87 us -> 1.88 us
    pallas_call x2 -> x3, Pallas kernels: 0.96 us -> 0.96 us  [the longest x2 0.96 us: factors_of(): pl.pallas_call(functools.partial(factor_kernel, core, at), out_shape=[chu...]
  transfers between devices with their start and end apart: 11 -> 11, of which waited for: 3 -> 4; matrix products, arithmetic and copies ran while one was open for 0% -> 0% of each run, Pallas kernels for 8% -> 8%
where the time goes in v4:
time: 27.2 us; the launch traced here: 27 us
  starting transfers between devices  15.2 us (56%)
  waiting for transfers between devices  5.81 us (21%)
  Pallas kernels  3.88 us (14%)
  local copies, waits for them, and re-layouts  1.88 us (7%)
    ppermute x11, starting transfers between devices, route(): return lax.ppermute(array, AXES, table)  15.2 us
    ppermute x11, waiting for transfers between devices, route(): return lax.ppermute(array, AXES, table)  5.81 us
    unnamed x18, local copies, waits for them, and re-layouts  1.88 us
    pallas_call x1, Pallas kernels, shards(): pl.pallas_call(last_kernel, out_shape=shape(mine.shape, F32), in_specs=[V...  1.65 us
    pallas_call x1, Pallas kernels, shards(): pl.pallas_call(prepare_kernel, out_shape=[shape((3 * width, 2 * width), B...  1.2 us
    pallas_call x2, Pallas kernels, factors_of(): pl.pallas_call(functools.partial(factor_kernel, core, at), out_shape=[chu...  0.96 us
  transfers between devices with their start and end apart: 11, of which 4 were waited for; matrix products, arithmetic and copies ran while one was open for 0% of the time, Pallas kernels for 8%

profile of v4, /device:TPU:0, one launch (start us, length us, event | category | flops | bytes accessed | tf_op | source)
XLA Modules:
  0.0 27.0 jit_solution(1409631565201017306)
XLA Ops:
  0.0 0.5 %collective-permute-start = (f32[1080,128]{1,0:T(8,128)}, f32[1080,128]{1,0:T(8,128)S(1)}, u32[]{:S(2)}, u32[]{:S(2)}) collective-permute-start(f32[1080,128]{1,0:T(8,128)} %bitcast.2), channel_id=1, source_target_pairs={{0,16},{1,17},{2,18},{3,19},{4,20},{5,21},{6,22},{7,23},{8,24},{9,... | collective-permute-start | bytes 1658888 | tf_op jit(solution)/shard_map/ppermute | solution.py:41
  0.5 0.0 copy-start
  0.5 1.0 %copy-done = f32[1,12,45,256]{3,0,2,1:T(1,128)S(1)} copy-done((f32[1,12,45,256]{3,0,2,1:T(1,128)S(1)}, f32[1,12,45,256]{3,0,2,1:T(1,128)}, u32[]{:S(2)}) %copy-start) | copy-done | bytes 552984
  1.5 0.0 copy-start.1
  1.5 2.6 %collective-permute-start.2 = (bf16[540,256]{1,0:T(8,128)(2,1)S(1)}, bf16[540,256]{1,0:T(8,128)(2,1)S(1)}, u32[]{:S(2)}, u32[]{:S(2)}) collective-permute-start(bf16[540,256]{1,0:T(8,128)(2,1)S(1)} %get-tuple-element.28.short_ref), channel_id=1, source_target_pairs={{0,18},{1,19},{2,16},{3,17},{4,22},{5,23},{6,20},{7,21},{8,26},{9,... | collective-permute-start | bytes 829448 | tf_op jit(solution)/shard_map/ppermute | solution.py:41
  4.1 3.1 %collective-permute-start.1 = (bf16[540,256]{1,0:T(8,128)(2,1)S(1)}, bf16[540,256]{1,0:T(8,128)(2,1)S(1)}, u32[]{:S(2)}, u32[]{:S(2)}) collective-permute-start(bf16[540,256]{1,0:T(8,128)(2,1)S(1)} %get-tuple-element.28.short_ref), channel_id=1, source_target_pairs={{0,30},{1,31},{2,20},{3,21},{4,18},{5,19},{6,24},{7,25},{8,22},{9,... | collective-permute-start | bytes 829448 | tf_op jit(solution)/shard_map/ppermute | solution.py:41
  7.3 0.0 collective-permute-done.other_ref.state_ref
  7.3 0.0 copy-start.2
  7.3 0.8 %copy-done.2 = f32[45,256]{1,0:T(8,128)S(1)} copy-done((f32[45,256]{1,0:T(8,128)S(1)}, f32[45,256]{1,0:T(8,128)}, u32[]{:S(2)}) %copy-start.2) | copy-done | bytes 46104
  8.1 0.0 copy-start.4
  8.1 0.0 copy-start.5
  8.1 0.0 copy-start.6
  8.1 0.0 copy-start.7
  8.1 0.0 copy-start.8
  8.1 0.0 copy-start.3
  8.2 0.1 collective-permute-start.5
  8.2 0.1 collective-permute-start.4
  8.3 2.1 %collective-permute-start.3 = (bf16[90,256]{1,0:T(8,128)(2,1)S(1)}, bf16[90,256]{1,0:T(8,128)(2,1)S(1)}, u32[]{:S(2)}, u32[]{:S(2)}) collective-permute-start(bf16[90,256]{1,0:T(8,128)(2,1)S(1)} %get-tuple-element.29.head_ref), channel_id=1, source_target_pairs={{0,31},{1,30},{2,21},{3,20},{4,19},{5,18},{6,25},{7,24},{8,23},{9,... | collective-permute-start | bytes 138248 | tf_op jit(solution)/shard_map/ppermute | solution.py:41
  10.4 0.0 copy-done.1
  10.4 0.0 copy-done.4
  10.4 0.0 copy-done.5
  10.4 0.0 copy-done.6
  10.4 0.0 copy-done.7
  10.4 0.0 copy-done.8
  10.4 1.2 %shard_map.75 = (bf16[768,512]{1,0:T(8,128)(2,1)S(1)}, bf16[540,256]{1,0:T(8,128)(2,1)S(1)}, f32[12,256]{1,0:T(8,128)S(1)}, f32[640,256]{1,0:T(8,128)S(1)}, f32[640,256]{1,0:T(8,128)S(1)}) custom-call(f32[1080,128]{1,0:T(8,128)S(1)} %bitcast.4, bf16[540,256]{1,0:T(8,128)(2,1)S(1)} %get-tuple-element.28.short_ref, s32[3,256]{1,0:T(4,128)S(1)} %copy-done.5, ...), custom_call_target="tpu_custom_call" | custom-call | flops 10000000 | tf_op jit(solution)/shard_map/pallas_call | solution.py:465
  11.6 0.0 collective-permute-done.5.other_ref.pack_ref
  11.7 0.0 copy-done.3
  11.7 0.0 collective-permute-done.4.dnear_ref
  11.7 0.5 %collective-permute-done.3.dfar_ref = bf16[90,256]{1,0:T(8,128)(2,1)S(1)} collective-permute-done((bf16[90,256]{1,0:T(8,128)(2,1)S(1)}, bf16[90,256]{1,0:T(8,128)(2,1)S(1)}, u32[]{:S(2)}, u32[]{:S(2)}) %collective-permute-start.3) | collective-permute-done | bytes 46112 | tf_op jit(solution)/shard_map/ppermute | solution.py:41
  12.2 0.0 collective-permute-done.2.near_ref
  12.2 0.0 collective-permute-done.1.far_ref
  12.2 1.3 %collective-permute-start.7 = (bf16[640,256]{1,0:T(8,128)(2,1)S(1)}, bf16[640,256]{1,0:T(8,128)(2,1)S(1)}, u32[]{:S(2)}, u32[]{:S(2)}) collective-permute-start(bf16[640,256]{1,0:T(8,128)(2,1)S(1)} %get-tuple-element.40.brief_ref), channel_id=1, source_target_pairs={{16,14},{17,15},{18,4},{19,5},{20,2},{21,3},{22,8},{23,9},{24,6},{... | collective-permute-start | bytes 983048 | tf_op jit(solution)/shard_map/ppermute | solution.py:41
  13.5 5.0 %collective-permute-start.6 = (bf16[640,256]{1,0:T(8,128)(2,1)S(1)}, bf16[640,256]{1,0:T(8,128)(2,1)S(1)}, u32[]{:S(2)}, u32[]{:S(2)}) collective-permute-start(bf16[640,256]{1,0:T(8,128)(2,1)S(1)} %get-tuple-element.40.brief_ref), channel_id=1, source_target_pairs={{16,2},{17,3},{18,0},{19,1},{20,6},{21,7},{22,4},{23,5},{24,10},{2... | collective-permute-start | bytes 983048 | tf_op jit(solution)/shard_map/ppermute | solution.py:41
  18.4 0.1 collective-permute-start.10
  18.5 0.4 %collective-permute-start.8 = (f32[232,256]{1,0:T(8,128)S(1)}, f32[232,256]{1,0:T(8,128)S(1)}, u32[]{:S(2)}, u32[]{:S(2)}) collective-permute-start(f32[232,256]{1,0:T(8,128)S(1)} %get-tuple-element.42), channel_id=1, source_target_pairs={{16,0},{17,1},{18,2},{19,3},{20,4},{21,5},{22,6},{23,7},{24,8},{25... | collective-permute-start | bytes 712712 | tf_op jit(solution)/shard_map/ppermute | solution.py:41
  18.9 0.1 collective-permute-start.9
  19.0 1.0 %collective-permute-done.10.other_ref.rest_2_ = f32[232,256]{1,0:T(8,128)S(1)} collective-permute-done((f32[232,256]{1,0:T(8,128)S(1)}, f32[232,256]{1,0:T(8,128)S(1)}, u32[]{:S(2)}, u32[]{:S(2)}) %collective-permute-start.10) | collective-permute-done | bytes 237600 | tf_op jit(solution)/shard_map/ppermute | solution.py:41
  20.0 0.9 %shard_map.78 = (f32[12,8,256]{2,1,0:T(8,128)S(1)}, f32[12,8,256]{2,1,0:T(8,128)S(1)}, f32[12,8,256]{2,1,0:T(8,128)S(1)}, f32[12,8,256]{2,1,0:T(8,128)S(1)}, f32...) custom-call(f32[45,256]{1,0:T(8,128)S(1)} %copy-done.3, f32[232,256]{1,0:T(8,128)S(1)} %collective-permute-done.10.other_ref.rest_2_), custom_call_target="tpu_custom_call" | custom-call | tf_op jit(solution)/shard_map/pallas_call | solution.py:483
  21.0 0.0 collective-permute-done.8.rest_0_
  21.0 0.0 collective-permute-done.9.rest_1_
  21.0 4.3 %collective-permute-done.7.far_ref = bf16[640,256]{1,0:T(8,128)(2,1)S(1)} collective-permute-done((bf16[640,256]{1,0:T(8,128)(2,1)S(1)}, bf16[640,256]{1,0:T(8,128)(2,1)S(1)}, u32[]{:S(2)}, u32[]{:S(2)}) %collective-permute-start.7) | collective-permute-done | bytes 327712 | tf_op jit(solution)/shard_map/ppermute | solution.py:41
  25.3 0.1 collective-permute-done.6.near_ref
  25.3 1.7 %shard_map.79 = f32[1080,128]{1,0:T(8,128)} custom-call(bf16[640,256]{1,0:T(8,128)(2,1)S(1)} %collective-permute-done.6.near_ref, bf16[640,256]{1,0:T(8,128)(2,1)S(1)} %collective-permute-done.7.far_ref, bf16[640,256]{1,0:T(8,128)(2,1)S(1)} %get-tuple-element.40.brief_ref, bf16[540,256]{1,0:T(8,128)(2,1)S(1)} %get-tuple-element.30.lagged_ref, ...), custom_call_target="tpu_custom_call" | custom-call | tf_op jit(solution)/shard_map/pallas_call | solution.py:514
  (4 shorter events, 0.1 us)
Async XLA Ops:
  0.0 7.3 %collective-permute-start = (f32[1080,128]{1,0:T(8,128)}, f32[1080,128]{1,0:T(8,128)S(1)}, u32[]{:S(2)}, u32[]{:S(2)}) collective-permute-start(f32[1080,128]{1,0:T(8,128)} %bitcast.2), channel_id=1, source_target_pairs={{0,16},{1,17},{2,18},{3,19},{4,20},{5,21},{6,22},{7,23},{8,24},{9,... | collective-permute-start | bytes 1658888 | tf_op jit(solution)/shard_map/ppermute | solution.py:41
  0.5 1.1 %copy-start = (f32[1,12,45,256]{3,0,2,1:T(1,128)S(1)}, f32[1,12,45,256]{3,0,2,1:T(1,128)}, u32[]{:S(2)}) copy-start(f32[1,12,45,256]{3,0,2,1:T(1,128)} %param.7) | copy-start | bytes 1658884
  1.5 8.9 %copy-start.1 = (f32[1,12,45,256]{3,0,2,1:T(1,128)S(1)}, f32[1,12,45,256]{3,0,2,1:T(1,128)}, u32[]{:S(2)}) copy-start(f32[1,12,45,256]{3,0,2,1:T(1,128)} %param.7) | copy-start | bytes 1658884
  1.5 10.6 %collective-permute-start.2 = (bf16[540,256]{1,0:T(8,128)(2,1)S(1)}, bf16[540,256]{1,0:T(8,128)(2,1)S(1)}, u32[]{:S(2)}, u32[]{:S(2)}) collective-permute-start(bf16[540,256]{1,0:T(8,128)(2,1)S(1)} %get-tuple-element.28.short_ref), channel_id=1, source_target_pairs={{0,18},{1,19},{2,16},{3,17},{4,22},{5,23},{6,20},{7,21},{8,26},{9,... | collective-permute-start | bytes 829448 | tf_op jit(solution)/shard_map/ppermute | solution.py:41
  4.1 8.0 %collective-permute-start.1 = (bf16[540,256]{1,0:T(8,128)(2,1)S(1)}, bf16[540,256]{1,0:T(8,128)(2,1)S(1)}, u32[]{:S(2)}, u32[]{:S(2)}) collective-permute-start(bf16[540,256]{1,0:T(8,128)(2,1)S(1)} %get-tuple-element.28.short_ref), channel_id=1, source_target_pairs={{0,30},{1,31},{2,20},{3,21},{4,18},{5,19},{6,24},{7,25},{8,22},{9,... | collective-permute-start | bytes 829448 | tf_op jit(solution)/shard_map/ppermute | solution.py:41
  7.3 0.8 %copy-start.2 = (f32[45,256]{1,0:T(8,128)S(1)}, f32[45,256]{1,0:T(8,128)}, u32[]{:S(2)}) copy-start(f32[45,256]{1,0:T(8,128)} %own_ref.3) | copy-start | bytes 138244
  8.1 2.3 %copy-start.4 = (s32[2,256]{1,0:T(2,128)S(1)}, s32[2,256]{1,0:T(2,128)}, u32[]{:S(2)}) copy-start(s32[2,256]{1,0:T(2,128)} %mask_ref.3) | copy-start | bytes 6148
  8.1 2.3 %copy-start.5 = (s32[3,256]{1,0:T(4,128)S(1)}, s32[3,256]{1,0:T(4,128)}, u32[]{:S(2)}) copy-start(s32[3,256]{1,0:T(4,128)} %nbr_ref.1) | copy-start | bytes 9220
  8.1 2.3 %copy-start.6 = (f32[3,256]{1,0:T(4,128)S(1)}, f32[3,256]{1,0:T(4,128)}, u32[]{:S(2)}) copy-start(f32[3,256]{1,0:T(4,128)} %weight_ref.1) | copy-start | bytes 9220
  8.1 2.3 %copy-start.7 = (f32[12]{0:T(128)S(1)}, f32[12]{0:T(128)}, u32[]{:S(2)}) copy-start(f32[12]{0:T(128)} %relax_ref.1) | copy-start | bytes 148
  8.1 2.3 %copy-start.8 = (f32[12]{0:T(128)S(1)}, f32[12]{0:T(128)}, u32[]{:S(2)}) copy-start(f32[12]{0:T(128)} %diff_ref.1) | copy-start | bytes 148
  8.1 3.5 %copy-start.3 = (f32[45,256]{1,0:T(8,128)S(1)}, f32[45,256]{1,0:T(8,128)}, u32[]{:S(2)}) copy-start(f32[45,256]{1,0:T(8,128)} %own_ref.3) | copy-start | bytes 138244
  8.2 3.5 %collective-permute-start.5 = (bf16[5,45,256]{2,1,0:T(8,128)(2,1)S(1)}, bf16[5,45,256]{2,1,0:T(8,128)(2,1)S(1)}, u32[]{:S(2)}, u32[]{:S(2)}) collective-permute-start(bf16[5,45,256]{2,1,0:T(8,128)(2,1)S(1)} %shard_map.74), channel_id=1, source_target_pairs={{0,17},{1,16},{2,19},{3,18},{4,21},{5,20},{6,23},{7,22},{8,25},{9,... | collective-permute-start | bytes 345608 | tf_op jit(solution)/shard_map/ppermute | solution.py:41
  8.2 3.5 %collective-permute-start.4 = (bf16[90,256]{1,0:T(8,128)(2,1)S(1)}, bf16[90,256]{1,0:T(8,128)(2,1)S(1)}, u32[]{:S(2)}, u32[]{:S(2)}) collective-permute-start(bf16[90,256]{1,0:T(8,128)(2,1)S(1)} %get-tuple-element.29.head_ref), channel_id=1, source_target_pairs={{0,19},{1,18},{2,17},{3,16},{4,23},{5,22},{6,21},{7,20},{8,27},{9,... | collective-permute-start | bytes 138248 | tf_op jit(solution)/shard_map/ppermute | solution.py:41
  8.3 3.9 %collective-permute-start.3 = (bf16[90,256]{1,0:T(8,128)(2,1)S(1)}, bf16[90,256]{1,0:T(8,128)(2,1)S(1)}, u32[]{:S(2)}, u32[]{:S(2)}) collective-permute-start(bf16[90,256]{1,0:T(8,128)(2,1)S(1)} %get-tuple-element.29.head_ref), channel_id=1, source_target_pairs={{0,31},{1,30},{2,21},{3,20},{4,19},{5,18},{6,25},{7,24},{8,23},{9,... | collective-permute-start | bytes 138248 | tf_op jit(solution)/shard_map/ppermute | solution.py:41
  12.2 13.1 %collective-permute-start.7 = (bf16[640,256]{1,0:T(8,128)(2,1)S(1)}, bf16[640,256]{1,0:T(8,128)(2,1)S(1)}, u32[]{:S(2)}, u32[]{:S(2)}) collective-permute-start(bf16[640,256]{1,0:T(8,128)(2,1)S(1)} %get-tuple-element.40.brief_ref), channel_id=1, source_target_pairs={{16,14},{17,15},{18,4},{19,5},{20,2},{21,3},{22,8},{23,9},{24,6},{... | collective-permute-start | bytes 983048 | tf_op jit(solution)/shard_map/ppermute | solution.py:41
  13.5 11.9 %collective-permute-start.6 = (bf16[640,256]{1,0:T(8,128)(2,1)S(1)}, bf16[640,256]{1,0:T(8,128)(2,1)S(1)}, u32[]{:S(2)}, u32[]{:S(2)}) collective-permute-start(bf16[640,256]{1,0:T(8,128)(2,1)S(1)} %get-tuple-element.40.brief_ref), channel_id=1, source_target_pairs={{16,2},{17,3},{18,0},{19,1},{20,6},{21,7},{22,4},{23,5},{24,10},{2... | collective-permute-start | bytes 983048 | tf_op jit(solution)/shard_map/ppermute | solution.py:41
  18.4 1.6 %collective-permute-start.10 = (f32[232,256]{1,0:T(8,128)S(1)}, f32[232,256]{1,0:T(8,128)S(1)}, u32[]{:S(2)}, u32[]{:S(2)}) collective-permute-start(f32[232,256]{1,0:T(8,128)S(1)} %get-tuple-element.44), channel_id=1, source_target_pairs={{16,0},{17,1},{18,2},{19,3},{20,4},{21,5},{22,6},{23,7},{24,8},{25... | collective-permute-start | bytes 712712 | tf_op jit(solution)/shard_map/ppermute | solution.py:41
  18.5 2.5 %collective-permute-start.8 = (f32[232,256]{1,0:T(8,128)S(1)}, f32[232,256]{1,0:T(8,128)S(1)}, u32[]{:S(2)}, u32[]{:S(2)}) collective-permute-start(f32[232,256]{1,0:T(8,128)S(1)} %get-tuple-element.42), channel_id=1, source_target_pairs={{16,0},{17,1},{18,2},{19,3},{20,4},{21,5},{22,6},{23,7},{24,8},{25... | collective-permute-start | bytes 712712 | tf_op jit(solution)/shard_map/ppermute | solution.py:41
  18.9 2.0 %collective-permute-start.9 = (f32[232,256]{1,0:T(8,128)S(1)}, f32[232,256]{1,0:T(8,128)S(1)}, u32[]{:S(2)}, u32[]{:S(2)}) collective-permute-start(f32[232,256]{1,0:T(8,128)S(1)} %get-tuple-element.43), channel_id=1, source_target_pairs={{16,0},{17,1},{18,2},{19,3},{20,4},{21,5},{22,6},{23,7},{24,8},{25... | collective-permute-start | bytes 712712 | tf_op jit(solution)/shard_map/ppermute | solution.py:41

commit v5 on v4

--- a/solution.py
+++ b/solution.py
@@ -86,18 +86,27 @@
         emit(f, clear)
 
 
-def shorten_kernel(mine_ref, short_ref, head_ref):
+def shorten_kernel(mine_ref, short_ref, head_ref, wide, sems):
     own, width = short_ref.shape
     parts = width // LANES
-
-    @pl.when(lax.axis_index("sec") == 0)
-    def _():
-        for low, high in spans(0, own, CHUNK):
-            value = get_rows(mine_ref, low, high, parts).astype(BF16)
+    pieces = spans(0, own, up(-(-own // 4), TILE))
+    copies = []
+    for i, (low, high) in enumerate(pieces):
+        rows = pl.ds(low * parts, (high - low) * parts)
+        copies.append(pltpu.make_async_copy(mine_ref.at[rows], wide.at[rows], sems.at[i]))
+        copies[-1].start()
+    for copy, (start, stop) in zip(copies, pieces):
+        copy.wait()
+        for low, high in spans(start, stop, CHUNK):
+            value = get_rows(wide, low, high, parts).astype(BF16)
             short_ref[low:high, :] = value
             end = min(high, head_ref.shape[0])
             if low < end:
                 head_ref[low:end, :] = value[: end - low]
+
+
+def nothing_kernel(short_ref, head_ref):
+    head_ref[...] = jnp.zeros(head_ref.shape, BF16)
 
 
 def pack_kernel(head_ref, other_ref, kappa_ref, pack_ref):
@@ -118,19 +127,23 @@
     lagged,
 ):
     fields = rates_ref.shape[0]
-    reach, width = gather_ref.shape[0], nbr_ref.shape[1]
+    width = nbr_ref.shape[1]
     half = lagged_ref.shape[0] // fields
     base = up(fields * half, TILE)
     odd = lax.axis_index("dom") % 2
-    sides = (2 * width * (1 - odd), width, 2 * width * odd)
-    for low, high in spans(0, reach, 64):
-        place = lax.broadcasted_iota(jnp.int32, (high - low, width), 0) + (low % width + sides[low // width])
-        total = jnp.zeros((high - low, width), F32)
-        for edge in range(EDGES):
-            total = total + jnp.where(place == nbr_ref[edge : edge + 1, :], weight_ref[edge : edge + 1, :], 0.0)
-        first = total.astype(BF16)
-        gather_ref[low:high, 0:width] = first
-        gather_ref[low:high, width : 2 * width] = (total - first.astype(F32)).astype(BF16)
+    sides = (2 * width * (1 - odd), 2 * width * odd, width)
+    for side, start in enumerate(sides):
+        for low, high in spans(0, width, 64):
+            place = lax.broadcasted_iota(jnp.int32, (high - low, width), 0) + (low + start)
+            total = jnp.zeros((high - low, width), F32)
+            for edge in range(EDGES):
+                total = total + jnp.where(place == nbr_ref[edge : edge + 1, :], weight_ref[edge : edge + 1, :], 0.0)
+            first = total.astype(BF16)
+            at = 2 * side * width + low
+            gather_ref[at : at + high - low, :] = first
+            gather_ref[at + width : at + width + high - low, :] = (total - first.astype(F32)).astype(BF16)
+            if side == 2:
+                gather_ref[at + 2 * width : at + 2 * width + high - low, :] = first
     total = weight_ref[0:1, :] + weight_ref[1:2, :] + weight_ref[2:3, :]
     keep_ref[...] = jnp.zeros(keep_ref.shape, F32)
     take_ref[...] = jnp.zeros(take_ref.shape, F32)
@@ -184,14 +197,56 @@
         ref[h, pl.ds(start, SUB, stride=steps), :] = value[:, h * LANES : (h + 1) * LANES]
 
 
-def factor_kernel(
-    core, at, own_ref, other_ref, low_ref, fore_ref, inv_ref, high_ref, back_ref, scan_ref, kappa, ratio, inverse
-):
-    @pl.when(lax.axis_index("sec") == core)
-    def _():
-        factor(
-            own_ref, other_ref[at].astype(F32), low_ref, fore_ref, inv_ref, high_ref, back_ref, scan_ref, kappa, ratio, inverse
-        )
+def ready_first_kernel(kappa_ref, pack_ref, state_ref, lagged_ref, keep_ref, take_ref, gather_ref, *rest):
+    factors, (start_ref, middle, *work) = rest[:6], rest[6:]
+    _, half, width = pack_ref.shape
+    own = lagged_ref.shape[0]
+    base = up(own, TILE)
+
+    @pl.when(lax.axis_index("sec") == 1)
+    def _():
+        factor(kappa_ref, pack_ref[2 * SOLVED].astype(F32), *factors, *work)
+        middle[0:own, :] = get_rows(state_ref, 0, own, width // LANES)
+        for f in range(SOLVED):
+            middle[base + f * half : base + (f + 1) * half, :] = pack_ref[f].astype(F32)
+        own_share(start_ref, middle, lagged_ref, keep_ref, take_ref, gather_ref, half)
+
+
+def ready_last_kernel(at, kappa_ref, lagged_ref, keep_ref, take_ref, gather_ref, *rest):
+    pieces, factors, (start_ref, middle, *work) = rest[:PIECES], rest[PIECES : PIECES + 6], rest[PIECES + 6 :]
+    half = kappa_ref.shape[0]
+    piece = pieces[0].shape[0]
+
+    @pl.when(lax.axis_index("sec") == 0)
+    def _():
+        factor(kappa_ref, pieces[at // piece][at % piece : at % piece + half, :], *factors, *work)
+        for i in range(PIECES):
+            low, high = i * piece, min((i + 1) * piece, middle.shape[0])
+            middle[low:high, :] = pieces[i][0 : high - low, :]
+        own_share(start_ref, middle, lagged_ref, keep_ref, take_ref, gather_ref, half)
+
+
+def own_share(start_ref, middle, lagged_ref, keep_ref, take_ref, gather_ref, half):
+    width = middle.shape[1]
+    solved, own = SOLVED * half, lagged_ref.shape[0]
+    values = middle[...]
+    high = values.astype(BF16)
+    low = (values - high.astype(F32)).astype(BF16)
+    share = jnp.dot(
+        jnp.concatenate([high, high, low], axis=1), gather_ref[4 * width : 7 * width, :], preferred_element_type=F32
+    )
+    start_ref[...] = values * keep_ref[...] + take_ref[...] * share
+    for low, high in spans(solved // CHUNK * CHUNK, own, CHUNK):
+        lag = lagged_ref[low:high, :].astype(F32)
+        if low < solved:
+            lag = jnp.where(lax.broadcasted_iota(jnp.int32, lag.shape, 0) >= solved - low, lag, 0.0)
+        start_ref[low:high, :] += lag
+
+
+def sides_share(near_rows, far_rows, gather_ref):
+    width = near_rows.shape[1]
+    rows = jnp.concatenate([near_rows, near_rows, far_rows, far_rows], axis=1)
+    return jnp.dot(rows, gather_ref[0 : 4 * width, :], preferred_element_type=F32)
 
 
 def factor(own_ref, other, low_ref, fore_ref, inv_ref, high_ref, back_ref, scan_ref, kappa, ratio, inverse):
@@ -271,49 +326,29 @@
         put_strided(right, t, steps, rows[t] + back_ref[t] * carry)
 
 
-def gathered(near_rows, middle, far_rows, gather_ref):
-    width = gather_ref.shape[1] // 2
-    high = middle.astype(BF16)
-    low = (middle - high.astype(F32)).astype(BF16)
-    mul = lambda rows, side, cols: jnp.dot(
-        rows, gather_ref[side * width : (side + 1) * width, cols], preferred_element_type=F32
-    )
-    both = mul(near_rows, 0, slice(None)) + mul(high, 1, slice(None)) + mul(far_rows, 2, slice(None))
-    return both[:, :width] + both[:, width:] + mul(low, 1, slice(0, width))
-
-
-def solve_rows(smooth, columns, factors, half, base):
-    level = lax.axis_index("lev")
+def solve_rows(own, other, columns, factors):
+    upper = lax.axis_index("lev") == 0
+    half, width = own[0].shape
     depth = 2 * half
-    width = smooth.shape[1]
     for f in range(SOLVED):
         put(columns.at[f], depth, jnp.zeros((columns.shape[2] - depth, width), F32))
-        mine = smooth[f * half : (f + 1) * half, :]
-        theirs = smooth[base + f * half : base + (f + 1) * half, :]
-
-        @pl.when(level == 0)
-        def _():
-            put(columns.at[f], 0, mine)
-            put(columns.at[f], half, theirs)
-
-        @pl.when(level == 1)
-        def _():
-            put(columns.at[f], 0, theirs)
-            put(columns.at[f], half, mine)
-
+        put(columns.at[f], 0, jnp.where(upper, own[f], other[f]))
+        put(columns.at[f], half, jnp.where(upper, other[f], own[f]))
     for f in range(SOLVED):
         solve(columns.at[f], factors)
+    halves = [(get(columns.at[f], 0, half), get(columns.at[f], half, half)) for f in range(SOLVED)]
+    return [jnp.where(upper, a, b) for a, b in halves], [jnp.where(upper, b, a) for a, b in halves]
 
 
 def first_kernel(
-    state_ref, far_ref, near_ref, dfar_ref, dnear_ref, pack_ref, lagged_ref, keep_ref, take_ref, gather_ref, *rest
+    far_ref, near_ref, dfar_ref, dnear_ref, pack_ref, start_ref, lagged_ref, take_ref, gather_ref, *rest
 ):
     factors, (*full_refs, short_ref, smooth, columns) = rest[:6], rest[6:]
     _, half, width = pack_ref.shape
     own = lagged_ref.shape[0]
     total = short_ref.shape[0]
     base = up(own, TILE)
-    parts = width // LANES
+    first = up(SOLVED * half, CHUNK)
     piece = full_refs[0].shape[0]
 
     def store(low, value):
@@ -322,47 +357,41 @@
             if a < b:
                 full_refs[i][a - start : b - start, :] = value[a - low : b - low]
 
+    def emit(low, value):
+        short_ref[low : low + value.shape[0], :] = value.astype(BF16)
+        store(low, value)
+
     @pl.when(lax.axis_index("sec") == 1)
     def _():
-        middle = get_rows(state_ref, 0, own, parts)
-        smooth[0:own, :] = middle * keep_ref[0:own, :] + take_ref[0:own, :] * gathered(
-            near_ref[...], middle, far_ref[...], gather_ref
+        others = slice(base, base + SOLVED * half)
+        smooth[others, :] = start_ref[others, :] + take_ref[others, :] * sides_share(
+            dnear_ref[...], dfar_ref[...], gather_ref
         )
+        rows = slice(0, first)
+        smooth[rows, :] = start_ref[rows, :] + take_ref[rows, :] * sides_share(
+            near_ref[rows, :], far_ref[rows, :], gather_ref
+        )
+        part = lambda low: [smooth[low + f * half : low + (f + 1) * half, :] for f in range(SOLVED)]
+        mine, theirs = solve_rows(part(0), part(base), columns, factors)
+        rows = slice(first, own)
+        value = start_ref[rows, :] + take_ref[rows, :] * sides_share(near_ref[rows, :], far_ref[rows, :], gather_ref)
+        for low, high in spans(first, own, CHUNK):
+            emit(low, value[low - first : high - first])
         for f in range(SOLVED):
-            smooth[base + f * half : base + (f + 1) * half, :] = pack_ref[f].astype(F32)
-        rows = slice(base, base + SOLVED * half)
-        middle = smooth[rows, :]
-        smooth[rows, :] = middle * keep_ref[rows, :] + take_ref[rows, :] * gathered(
-            dnear_ref[...], middle, dfar_ref[...], gather_ref
-        )
-        solve_rows(smooth, columns, factors, half, base)
-        for f in range(SOLVED):
-            lag = pack_ref[SOLVED + f].astype(F32)
-
-            @pl.when(lax.axis_index("lev") == 0)
-            def _():
-                smooth[f * half : (f + 1) * half, :] = get(columns.at[f], 0, half)
-                smooth[base + f * half : base + (f + 1) * half, :] = get(columns.at[f], half, half) + lag
-
-            @pl.when(lax.axis_index("lev") == 1)
-            def _():
-                smooth[f * half : (f + 1) * half, :] = get(columns.at[f], half, half)
-                smooth[base + f * half : base + (f + 1) * half, :] = get(columns.at[f], 0, half) + lag
-
-        for low, high in spans(0, total, CHUNK):
-            value = smooth[low:high, :]
-            if low < own:
-                stop = min(high, own)
-                value = smooth[low:stop, :] + lagged_ref[low:stop, :].astype(F32)
-                smooth[low:stop, :] = value
-                value = smooth[low:high, :]
-            short_ref[low:high, :] = value.astype(BF16)
-            store(low, value)
+            smooth[f * half : (f + 1) * half, :] = mine[f]
+            smooth[base + f * half : base + (f + 1) * half, :] = theirs[f] + pack_ref[SOLVED + f].astype(F32)
+        for low, high in spans(0, first, CHUNK):
+            lag = lagged_ref[low:high, :].astype(F32)
+            if high > SOLVED * half:
+                lag = jnp.where(lax.broadcasted_iota(jnp.int32, lag.shape, 0) < SOLVED * half - low, lag, 0.0)
+            emit(low, smooth[low:high, :] + lag)
+        for low, high in spans(base, total, CHUNK):
+            emit(low, smooth[low:high, :])
         store(total, pack_ref[2 * SOLVED].astype(F32))
 
 
-def last_kernel(near_ref, far_ref, brief_ref, lagged_ref, mask_ref, rates_ref, keep_ref, take_ref, gather_ref, *rest):
-    pieces, factors, (out_ref, smooth, columns, held, sems) = rest[:PIECES], rest[PIECES : PIECES + 6], rest[PIECES + 6 :]
+def last_kernel(near_ref, far_ref, brief_ref, start_ref, lagged_ref, mask_ref, rates_ref, take_ref, gather_ref, *rest):
+    factors, (out_ref, smooth, columns, held, sems) = rest[:6], rest[6:]
     own, width = lagged_ref.shape
     fields = rates_ref.shape[0]
     half = own // fields
@@ -370,7 +399,6 @@
     total = near_ref.shape[0]
     parts = width // LANES
     first = up(SOLVED * half, CHUNK)
-    piece = pieces[0].shape[0]
 
     def send(low, high, sem):
         rows = pl.ds(low * parts, (high - low) * parts)
@@ -378,29 +406,24 @@
 
     @pl.when(lax.axis_index("sec") == 0)
     def _():
-        for i in range(PIECES):
-            low, high = i * piece, min((i + 1) * piece, total)
+        def smoothed(low, high):
             rows = slice(low, high)
-            middle = pieces[i][0 : high - low, :]
-            smooth[rows, :] = middle * keep_ref[rows, :] + take_ref[rows, :] * gathered(
-                near_ref[rows, :], middle, far_ref[rows, :], gather_ref
-            )
-        for low, high in spans(first, own, CHUNK):
-            put_rows(held, low, parts, smooth[low:high, :] + lagged_ref[low:high, :].astype(F32))
+            share = sides_share(near_ref[rows, :], far_ref[rows, :], gather_ref)
+            return start_ref[rows, :] + take_ref[rows, :] * share
+
+        smooth[0:first, :] = smoothed(0, first)
+        smooth[base:total, :] = smoothed(base, total)
+        part = lambda low: [smooth[low + f * half : low + (f + 1) * half, :] for f in range(SOLVED)]
+        mine, _ = solve_rows(part(0), part(base), columns, factors)
+        put_rows(held, first, parts, smoothed(first, own))
         send(first, own, 0).start()
-        solve_rows(smooth, columns, factors, half, base)
         for f in range(SOLVED):
-
-            @pl.when(lax.axis_index("lev") == 0)
-            def _():
-                smooth[f * half : (f + 1) * half, :] = get(columns.at[f], 0, half)
-
-            @pl.when(lax.axis_index("lev") == 1)
-            def _():
-                smooth[f * half : (f + 1) * half, :] = get(columns.at[f], half, half)
-
+            smooth[f * half : (f + 1) * half, :] = mine[f]
         for low, high in spans(0, first, CHUNK):
-            put_rows(held, low, parts, smooth[low:high, :] + lagged_ref[low:high, :].astype(F32))
+            lag = lagged_ref[low:high, :].astype(F32)
+            if high > SOLVED * half:
+                lag = jnp.where(lax.broadcasted_iota(jnp.int32, lag.shape, 0) < SOLVED * half - low, lag, 0.0)
+            put_rows(held, low, parts, smooth[low:high, :] + lag)
 
     @pl.when(lax.axis_index("sec") == 1)
     def _():
@@ -437,14 +460,23 @@
     piece = up(-(-(total + half) // PIECES), SUB)
 
     mine = strips(sections)
-    short, head = pl.pallas_call(
-        shorten_kernel,
-        out_shape=[shape((own, width), BF16), shape((SOLVED * half, width), BF16)],
-        in_specs=[VMEM],
-        out_specs=[VMEM] * 2,
-        compiler_params=params(4),
-        cost_estimate=cost(0.01),
-    )(mine)
+    shorts = [shape((own, width), BF16), shape((SOLVED * half, width), BF16)]
+    short, head = lax.cond(
+        lax.axis_index("sec") == 0,
+        pl.pallas_call(
+            shorten_kernel,
+            out_shape=shorts,
+            in_specs=[ANY],
+            out_specs=[VMEM] * 2,
+            scratch_shapes=[pltpu.VMEM(mine.shape, F32), pltpu.SemaphoreType.DMA((4,))],
+            compiler_params=params(4),
+            cost_estimate=cost(3),
+        ),
+        lambda _: pl.pallas_call(
+            nothing_kernel, out_shape=shorts, out_specs=[VMEM] * 2, compiler_params=params(4), cost_estimate=cost(3)
+        )(),
+        mine,
+    )
     back = (1, 0, same, 0)
     state = route(mine, (0, 1, same, 0), back)
     near_rows = route(short, (0, 1, near, 0), back)
@@ -465,7 +497,7 @@
     gather, lagged, rates, keep, take = pl.pallas_call(
         prepare_kernel,
         out_shape=[
-            shape((3 * width, 2 * width), BF16),
+            shape((7 * width, width), BF16),
             shape((own, width), BF16),
             shape((fields, width), F32),
             shape((total, width), F32),
@@ -479,46 +511,50 @@
     )(mine, short, neighbours, edge_weight, precip_mask, relax_rate, field_diff)
 
     chunk = shape((steps, SUB, width), F32)
-    def factors_of(core, at, other, us):
-        return pl.pallas_call(
-            functools.partial(factor_kernel, core, at),
-            out_shape=[chunk] * 5 + [shape((6, SUB, width), F32)],
-            in_specs=[VMEM] * 2,
-            out_specs=[VMEM] * 6,
+
+    def ready(kernel, *operands):
+        start, *factors = pl.pallas_call(
+            kernel,
+            out_shape=[chunk] * 5 + [shape((6, SUB, width), F32), shape((total, width), F32)],
+            in_specs=[VMEM] * len(operands),
+            out_specs=[VMEM] * 7,
             scratch_shapes=[
+                pltpu.VMEM((total, width), F32),
                 pltpu.VMEM((2 * half, width), F32),
                 pltpu.VMEM((width // LANES, depth + 2 * SUB, LANES), F32),
                 pltpu.VMEM((width // LANES, depth, LANES), F32),
             ],
-            compiler_params=params(8),
-            cost_estimate=cost(us),
-        )(vert_coef, other)
-
-    factors = factors_of(1, 2 * SOLVED, pack, 0.01)
+            compiler_params=params(16),
+            cost_estimate=cost(0),
+        )(*operands)[::-1]
+        return start, factors[::-1]
+
+    start, factors = ready(ready_first_kernel, vert_coef, pack, state, lagged, keep, take, gather)
 
     scratch = [pltpu.VMEM((total, width), F32), pltpu.VMEM((SOLVED, width // LANES, depth, LANES), F32)]
     *full, brief = pl.pallas_call(
         first_kernel,
         out_shape=[shape((piece, width), F32)] * PIECES + [shape((total, width), BF16)],
-        in_specs=[VMEM] * 16,
+        in_specs=[VMEM] * 15,
         out_specs=[VMEM] * (PIECES + 1),
         scratch_shapes=scratch,
         compiler_params=params(24),
-    )(state, far_rows, near_rows, dfar, dnear, pack, lagged, keep, take, gather, *factors)
+    )(far_rows, near_rows, dfar, dnear, pack, start, lagged, take, gather, *factors)
 
     near_rows = route(brief, (1, 0, near, 0), (0, 1, same, 0))
     far_rows = route(brief, (1, 0, far, 0))
     pieces = [route(part, back, (0, 1, same, 0)) for part in full]
-    last, low = divmod(total, piece)
-    factors = factors_of(0, slice(low, low + half), pieces[last], 0)
+    start, factors = ready(
+        functools.partial(ready_last_kernel, total), vert_coef, lagged, keep, take, gather, *pieces
+    )
     out = pl.pallas_call(
         last_kernel,
         out_shape=shape(mine.shape, F32),
-        in_specs=[VMEM] * (15 + PIECES),
+        in_specs=[VMEM] * 15,
         out_specs=ANY,
         scratch_shapes=scratch + [pltpu.VMEM(mine.shape, F32), pltpu.SemaphoreType.DMA((2,))],
         compiler_params=params(24),
-    )(near_rows, far_rows, brief, lagged, precip_mask, rates, keep, take, gather, *pieces, *factors)
+    )(near_rows, far_rows, brief, start, lagged, precip_mask, rates, take, gather, *factors)
     return out.reshape(sections.shape)
 
 

time: 27.2 us -> 25.8 us (0.949)
  local copies, waits for them, and re-layouts: 1.88 us -> 0.04 us
  Pallas kernels: 3.88 us -> 4.89 us
  starting transfers between devices: 15.2 us -> 14.4 us
  waiting for transfers between devices: 5.81 us -> 6.17 us
    unnamed x18 -> x14, local copies, waits for them, and re-layouts: 1.88 us -> 0.04 us
    pallas_call x4, Pallas kernels: 2.19 us -> 3.44 us  [the longest x1 1.2 us: shards(): pl.pallas_call(prepare_kernel, out_shape=[shape((7 * width, width), BF16)...]
    ppermute x11, starting transfers between devices: 15.2 us -> 14.4 us  [route(): return lax.ppermute(array, AXES, table)]
    ppermute x11, waiting for transfers between devices: 5.81 us -> 6.17 us  [route(): return lax.ppermute(array, AXES, table)]
  transfers between devices with their start and end apart: 11 -> 11, of which waited for: 4 -> 6; matrix products, arithmetic and copies ran while one was open for 0% -> 0% of each run, Pallas kernels for 8% -> 14%
where the time goes in v5:
time: 25.8 us; the launch traced here: 25.6 us
  starting transfers between devices  14.4 us (56%)
  waiting for transfers between devices  6.17 us (24%)
  Pallas kernels  4.89 us (19%)
    ppermute x11, starting transfers between devices, route(): return lax.ppermute(array, AXES, table)  14.4 us
    ppermute x11, waiting for transfers between devices, route(): return lax.ppermute(array, AXES, table)  6.17 us
    pallas_call x1, Pallas kernels, shards(): pl.pallas_call(last_kernel, out_shape=shape(mine.shape, F32), in_specs=[V...  1.42 us
    pallas_call x1, Pallas kernels, shards(): pl.pallas_call(prepare_kernel, out_shape=[shape((7 * width, width), BF16)...  1.2 us
    pallas_call x1, Pallas kernels, shards(): lax.cond(lax.axis_index('sec') == 0, pl.pallas_call(shorten_kernel, out_s...  1.16 us
    pallas_call x2, Pallas kernels, ready(): pl.pallas_call(kernel, out_shape=[chunk] * 5 + [shape((6, SUB, width), F3...  1.08 us
  transfers between devices with their start and end apart: 11, of which 6 were waited for; matrix products, arithmetic and copies ran while one was open for 0% of the time, Pallas kernels for 14%

profile of v5, /device:TPU:0, one launch (start us, length us, event | category | flops | bytes accessed | tf_op | source)
XLA Modules:
  0.0 25.6 jit_solution(149964998560298198)
XLA Ops:
  0.0 0.5 %collective-permute-start.4 = (f32[1080,128]{1,0:T(8,128)}, f32[1080,128]{1,0:T(8,128)S(1)}, u32[]{:S(2)}, u32[]{:S(2)}) collective-permute-start(f32[1080,128]{1,0:T(8,128)} %bitcast.2), channel_id=1, source_target_pairs={{0,16},{1,17},{2,18},{3,19},{4,20},{5,21},{6,22},{7,23},{8,24},{9,... | collective-permute-start | bytes 1658888 | tf_op jit(solution)/shard_map/ppermute | solution.py:41
  0.5 0.0 copy-start
  0.5 1.2 %conditional.1 = ((bf16[540,256]{1,0:T(8,128)(2,1)S(1)}, bf16[90,256]{1,0:T(8,128)(2,1)S(1)})) conditional(s32[]{:T(128)} %convert_element_type.3, () %tuple.11, f32[1080,128]{1,0:T(8,128)} %bitcast.3), branch_computations={%region_0.0_spmd, %region_1.0_spmd} | conditional | flops 3000000000 | bytes 8 | solution.py:464
  0.5 1.2 %branch_1_fun.1 = (bf16[540,256]{1,0:T(8,128)(2,1)S(1)}, bf16[90,256]{1,0:T(8,128)(2,1)S(1)}) custom-call(f32[1080,128]{1,0:T(8,128)} %mine_ref), custom_call_target="tpu_custom_call" | custom-call | flops 3000000000 | tf_op jit(solution)/shard_map/cond/branch_1_fun/pallas_call | solution.py:464
  1.6 0.0 copy-start.6
  1.6 1.5 %collective-permute-start.1 = (bf16[540,256]{1,0:T(8,128)(2,1)S(1)}, bf16[540,256]{1,0:T(8,128)(2,1)S(1)}, u32[]{:S(2)}, u32[]{:S(2)}) collective-permute-start(bf16[540,256]{1,0:T(8,128)(2,1)S(1)} %get-tuple-element.31.short_ref), channel_id=1, source_target_pairs={{0,18},{1,19},{2,16},{3,17},{4,22},{5,23},{6,20},{7,21},{8,26},{9,... | collective-permute-start | bytes 829448 | tf_op jit(solution)/shard_map/ppermute | solution.py:41
  3.2 4.2 %collective-permute-start = (bf16[540,256]{1,0:T(8,128)(2,1)S(1)}, bf16[540,256]{1,0:T(8,128)(2,1)S(1)}, u32[]{:S(2)}, u32[]{:S(2)}) collective-permute-start(bf16[540,256]{1,0:T(8,128)(2,1)S(1)} %get-tuple-element.31.short_ref), channel_id=1, source_target_pairs={{0,30},{1,31},{2,20},{3,21},{4,18},{5,19},{6,24},{7,25},{8,22},{9,... | collective-permute-start | bytes 829448 | tf_op jit(solution)/shard_map/ppermute | solution.py:41
  7.4 0.0 collective-permute-done.4.other_ref.state_ref
  7.4 0.0 copy-done
  7.4 0.0 copy-start.1
  7.4 0.0 copy-start.2
  7.4 0.0 copy-start.3
  7.4 0.0 copy-start.4
  7.4 0.0 copy-start.5
  7.5 0.1 collective-permute-start.5
  7.5 0.1 collective-permute-start.3
  7.6 2.0 %collective-permute-start.2 = (bf16[90,256]{1,0:T(8,128)(2,1)S(1)}, bf16[90,256]{1,0:T(8,128)(2,1)S(1)}, u32[]{:S(2)}, u32[]{:S(2)}) collective-permute-start(bf16[90,256]{1,0:T(8,128)(2,1)S(1)} %get-tuple-element.32.head_ref), channel_id=1, source_target_pairs={{0,31},{1,30},{2,21},{3,20},{4,19},{5,18},{6,25},{7,24},{8,23},{9,... | collective-permute-start | bytes 138248 | tf_op jit(solution)/shard_map/ppermute | solution.py:41
  9.6 0.0 copy-done.6
  9.6 0.0 copy-done.1
  9.6 0.0 copy-done.2
  9.6 0.0 copy-done.3
  9.6 0.0 copy-done.4
  9.6 0.0 copy-done.5
  9.6 1.2 %shard_map.74 = (bf16[1792,256]{1,0:T(8,128)(2,1)S(1)}, bf16[540,256]{1,0:T(8,128)(2,1)S(1)}, f32[12,256]{1,0:T(8,128)S(1)}, f32[640,256]{1,0:T(8,128)S(1)}, f32[640,256]{1,0:T(8,128)S(1)}) custom-call(f32[1080,128]{1,0:T(8,128)S(1)} %bitcast.4, bf16[540,256]{1,0:T(8,128)(2,1)S(1)} %get-tuple-element.31.short_ref, s32[3,256]{1,0:T(4,128)S(1)} %copy-done.2, ...), custom_call_target="tpu_custom_call" | custom-call | flops 10000000 | tf_op jit(solution)/shard_map/pallas_call | solution.py:497
  10.8 0.0 collective-permute-done.5.pack_ref
  10.9 0.1 collective-permute-done.3.dnear_ref
  11.0 1.0 %collective-permute-done.2.dfar_ref = bf16[90,256]{1,0:T(8,128)(2,1)S(1)} collective-permute-done((bf16[90,256]{1,0:T(8,128)(2,1)S(1)}, bf16[90,256]{1,0:T(8,128)(2,1)S(1)}, u32[]{:S(2)}, u32[]{:S(2)}) %collective-permute-start.2) | collective-permute-done | bytes 46112 | tf_op jit(solution)/shard_map/ppermute | solution.py:41
  12.0 0.0 collective-permute-done.1.near_ref
  12.0 0.0 collective-permute-done.far_ref
  12.0 1.3 %collective-permute-start.7 = (bf16[640,256]{1,0:T(8,128)(2,1)S(1)}, bf16[640,256]{1,0:T(8,128)(2,1)S(1)}, u32[]{:S(2)}, u32[]{:S(2)}) collective-permute-start(bf16[640,256]{1,0:T(8,128)(2,1)S(1)} %get-tuple-element.44.brief_ref), channel_id=1, source_target_pairs={{16,14},{17,15},{18,4},{19,5},{20,2},{21,3},{22,8},{23,9},{24,6},{... | collective-permute-start | bytes 983048 | tf_op jit(solution)/shard_map/ppermute | solution.py:41
  13.3 4.2 %collective-permute-start.6 = (bf16[640,256]{1,0:T(8,128)(2,1)S(1)}, bf16[640,256]{1,0:T(8,128)(2,1)S(1)}, u32[]{:S(2)}, u32[]{:S(2)}) collective-permute-start(bf16[640,256]{1,0:T(8,128)(2,1)S(1)} %get-tuple-element.44.brief_ref), channel_id=1, source_target_pairs={{16,2},{17,3},{18,0},{19,1},{20,6},{21,7},{22,4},{23,5},{24,10},{2... | collective-permute-start | bytes 983048 | tf_op jit(solution)/shard_map/ppermute | solution.py:41
  17.5 0.1 collective-permute-start.8
  17.5 0.4 %collective-permute-start.9 = (f32[232,256]{1,0:T(8,128)S(1)}, f32[232,256]{1,0:T(8,128)S(1)}, u32[]{:S(2)}, u32[]{:S(2)}) collective-permute-start(f32[232,256]{1,0:T(8,128)S(1)} %get-tuple-element.46), channel_id=1, source_target_pairs={{16,0},{17,1},{18,2},{19,3},{20,4},{21,5},{22,6},{23,7},{24,8},{25... | collective-permute-start | bytes 712712 | tf_op jit(solution)/shard_map/ppermute | solution.py:41
  18.0 0.1 collective-permute-start.10
  18.1 1.0 %collective-permute-done.8.rest_0_ = f32[232,256]{1,0:T(8,128)S(1)} collective-permute-done((f32[232,256]{1,0:T(8,128)S(1)}, f32[232,256]{1,0:T(8,128)S(1)}, u32[]{:S(2)}, u32[]{:S(2)}) %collective-permute-start.8) | collective-permute-done | bytes 237600 | tf_op jit(solution)/shard_map/ppermute | solution.py:41
  19.1 0.3 %collective-permute-done.9.rest_1_ = f32[232,256]{1,0:T(8,128)S(1)} collective-permute-done((f32[232,256]{1,0:T(8,128)S(1)}, f32[232,256]{1,0:T(8,128)S(1)}, u32[]{:S(2)}, u32[]{:S(2)}) %collective-permute-start.9) | collective-permute-done | bytes 237600 | tf_op jit(solution)/shard_map/ppermute | solution.py:41
  19.4 0.3 %collective-permute-done.10.rest_2_ = f32[232,256]{1,0:T(8,128)S(1)} collective-permute-done((f32[232,256]{1,0:T(8,128)S(1)}, f32[232,256]{1,0:T(8,128)S(1)}, u32[]{:S(2)}, u32[]{:S(2)}) %collective-permute-start.10) | collective-permute-done | bytes 237600 | tf_op jit(solution)/shard_map/ppermute | solution.py:41
  19.7 1.1 %shard_map.77 = (f32[12,8,256]{2,1,0:T(8,128)S(1)}, f32[12,8,256]{2,1,0:T(8,128)S(1)}, f32[12,8,256]{2,1,0:T(8,128)S(1)}, f32[12,8,256]{2,1,0:T(8,128)S(1)}, f32...) custom-call(f32[45,256]{1,0:T(8,128)S(1)} %copy-done, ...), custom_call_target="tpu_custom_call" | custom-call | tf_op jit(solution)/shard_map/pallas_call | solution.py:516
  20.8 3.4 %collective-permute-done.7.far_ref = bf16[640,256]{1,0:T(8,128)(2,1)S(1)} collective-permute-done((bf16[640,256]{1,0:T(8,128)(2,1)S(1)}, bf16[640,256]{1,0:T(8,128)(2,1)S(1)}, u32[]{:S(2)}, u32[]{:S(2)}) %collective-permute-start.7) | collective-permute-done | bytes 327712 | tf_op jit(solution)/shard_map/ppermute | solution.py:41
  24.2 0.0 collective-permute-done.6.near_ref
  24.2 1.4 %shard_map.78 = f32[1080,128]{1,0:T(8,128)} custom-call(bf16[640,256]{1,0:T(8,128)(2,1)S(1)} %collective-permute-done.6.near_ref, bf16[640,256]{1,0:T(8,128)(2,1)S(1)} %collective-permute-done.7.far_ref, bf16[640,256]{1,0:T(8,128)(2,1)S(1)} %get-tuple-element.44.brief_ref, f32[640,256]{1,0:T(8,128)S(1)} %get-tuple-element.48.start_ref, ...), custom_call_target="tpu_custom_call" | custom-call | tf_op jit(solution)/shard_map/pallas_call | solution.py:550
  (3 shorter events, 0.1 us)
Async XLA Ops:
  0.0 7.4 %collective-permute-start.4 = (f32[1080,128]{1,0:T(8,128)}, f32[1080,128]{1,0:T(8,128)S(1)}, u32[]{:S(2)}, u32[]{:S(2)}) collective-permute-start(f32[1080,128]{1,0:T(8,128)} %bitcast.2), channel_id=1, source_target_pairs={{0,16},{1,17},{2,18},{3,19},{4,20},{5,21},{6,22},{7,23},{8,24},{9,... | collective-permute-start | bytes 1658888 | tf_op jit(solution)/shard_map/ppermute | solution.py:41
  0.5 6.9 %copy-start = (f32[45,256]{1,0:T(8,128)S(1)}, f32[45,256]{1,0:T(8,128)}, u32[]{:S(2)}) copy-start(f32[45,256]{1,0:T(8,128)} %kappa_ref.5) | copy-start | bytes 138244
  1.6 8.0 %copy-start.6 = (f32[1,12,45,256]{3,0,2,1:T(1,128)S(1)}, f32[1,12,45,256]{3,0,2,1:T(1,128)}, u32[]{:S(2)}) copy-start(f32[1,12,45,256]{3,0,2,1:T(1,128)} %param.9) | copy-start | bytes 1658884
  1.6 10.3 %collective-permute-start.1 = (bf16[540,256]{1,0:T(8,128)(2,1)S(1)}, bf16[540,256]{1,0:T(8,128)(2,1)S(1)}, u32[]{:S(2)}, u32[]{:S(2)}) collective-permute-start(bf16[540,256]{1,0:T(8,128)(2,1)S(1)} %get-tuple-element.31.short_ref), channel_id=1, source_target_pairs={{0,18},{1,19},{2,16},{3,17},{4,22},{5,23},{6,20},{7,21},{8,26},{9,... | collective-permute-start | bytes 829448 | tf_op jit(solution)/shard_map/ppermute | solution.py:41
  3.2 8.8 %collective-permute-start = (bf16[540,256]{1,0:T(8,128)(2,1)S(1)}, bf16[540,256]{1,0:T(8,128)(2,1)S(1)}, u32[]{:S(2)}, u32[]{:S(2)}) collective-permute-start(bf16[540,256]{1,0:T(8,128)(2,1)S(1)} %get-tuple-element.31.short_ref), channel_id=1, source_target_pairs={{0,30},{1,31},{2,20},{3,21},{4,18},{5,19},{6,24},{7,25},{8,22},{9,... | collective-permute-start | bytes 829448 | tf_op jit(solution)/shard_map/ppermute | solution.py:41
  7.4 2.2 %copy-start.1 = (s32[2,256]{1,0:T(2,128)S(1)}, s32[2,256]{1,0:T(2,128)}, u32[]{:S(2)}) copy-start(s32[2,256]{1,0:T(2,128)} %mask_ref.3) | copy-start | bytes 6148
  7.4 2.2 %copy-start.2 = (s32[3,256]{1,0:T(4,128)S(1)}, s32[3,256]{1,0:T(4,128)}, u32[]{:S(2)}) copy-start(s32[3,256]{1,0:T(4,128)} %nbr_ref.1) | copy-start | bytes 9220
  7.4 2.2 %copy-start.3 = (f32[3,256]{1,0:T(4,128)S(1)}, f32[3,256]{1,0:T(4,128)}, u32[]{:S(2)}) copy-start(f32[3,256]{1,0:T(4,128)} %weight_ref.1) | copy-start | bytes 9220
  7.4 2.2 %copy-start.4 = (f32[12]{0:T(128)S(1)}, f32[12]{0:T(128)}, u32[]{:S(2)}) copy-start(f32[12]{0:T(128)} %relax_ref.1) | copy-start | bytes 148
  7.4 2.2 %copy-start.5 = (f32[12]{0:T(128)S(1)}, f32[12]{0:T(128)}, u32[]{:S(2)}) copy-start(f32[12]{0:T(128)} %diff_ref.1) | copy-start | bytes 148
  7.5 3.4 %collective-permute-start.5 = (bf16[5,45,256]{2,1,0:T(8,128)(2,1)S(1)}, bf16[5,45,256]{2,1,0:T(8,128)(2,1)S(1)}, u32[]{:S(2)}, u32[]{:S(2)}) collective-permute-start(bf16[5,45,256]{2,1,0:T(8,128)(2,1)S(1)} %shard_map.73), channel_id=1, source_target_pairs={{0,17},{1,16},{2,19},{3,18},{4,21},{5,20},{6,23},{7,22},{8,25},{9,... | collective-permute-start | bytes 345608 | tf_op jit(solution)/shard_map/ppermute | solution.py:41
  7.5 3.4 %collective-permute-start.3 = (bf16[90,256]{1,0:T(8,128)(2,1)S(1)}, bf16[90,256]{1,0:T(8,128)(2,1)S(1)}, u32[]{:S(2)}, u32[]{:S(2)}) collective-permute-start(bf16[90,256]{1,0:T(8,128)(2,1)S(1)} %get-tuple-element.32.head_ref), channel_id=1, source_target_pairs={{0,19},{1,18},{2,17},{3,16},{4,23},{5,22},{6,21},{7,20},{8,27},{9,... | collective-permute-start | bytes 138248 | tf_op jit(solution)/shard_map/ppermute | solution.py:41
  7.6 4.4 %collective-permute-start.2 = (bf16[90,256]{1,0:T(8,128)(2,1)S(1)}, bf16[90,256]{1,0:T(8,128)(2,1)S(1)}, u32[]{:S(2)}, u32[]{:S(2)}) collective-permute-start(bf16[90,256]{1,0:T(8,128)(2,1)S(1)} %get-tuple-element.32.head_ref), channel_id=1, source_target_pairs={{0,31},{1,30},{2,21},{3,20},{4,19},{5,18},{6,25},{7,24},{8,23},{9,... | collective-permute-start | bytes 138248 | tf_op jit(solution)/shard_map/ppermute | solution.py:41
  12.0 12.2 %collective-permute-start.7 = (bf16[640,256]{1,0:T(8,128)(2,1)S(1)}, bf16[640,256]{1,0:T(8,128)(2,1)S(1)}, u32[]{:S(2)}, u32[]{:S(2)}) collective-permute-start(bf16[640,256]{1,0:T(8,128)(2,1)S(1)} %get-tuple-element.44.brief_ref), channel_id=1, source_target_pairs={{16,14},{17,15},{18,4},{19,5},{20,2},{21,3},{22,8},{23,9},{24,6},{... | collective-permute-start | bytes 983048 | tf_op jit(solution)/shard_map/ppermute | solution.py:41
  13.3 10.9 %collective-permute-start.6 = (bf16[640,256]{1,0:T(8,128)(2,1)S(1)}, bf16[640,256]{1,0:T(8,128)(2,1)S(1)}, u32[]{:S(2)}, u32[]{:S(2)}) collective-permute-start(bf16[640,256]{1,0:T(8,128)(2,1)S(1)} %get-tuple-element.44.brief_ref), channel_id=1, source_target_pairs={{16,2},{17,3},{18,0},{19,1},{20,6},{21,7},{22,4},{23,5},{24,10},{2... | collective-permute-start | bytes 983048 | tf_op jit(solution)/shard_map/ppermute | solution.py:41
  17.5 1.6 %collective-permute-start.8 = (f32[232,256]{1,0:T(8,128)S(1)}, f32[232,256]{1,0:T(8,128)S(1)}, u32[]{:S(2)}, u32[]{:S(2)}) collective-permute-start(f32[232,256]{1,0:T(8,128)S(1)} %get-tuple-element.45), channel_id=1, source_target_pairs={{16,0},{17,1},{18,2},{19,3},{20,4},{21,5},{22,6},{23,7},{24,8},{25... | collective-permute-start | bytes 712712 | tf_op jit(solution)/shard_map/ppermute | solution.py:41
  17.5 1.9 %collective-permute-start.9 = (f32[232,256]{1,0:T(8,128)S(1)}, f32[232,256]{1,0:T(8,128)S(1)}, u32[]{:S(2)}, u32[]{:S(2)}) collective-permute-start(f32[232,256]{1,0:T(8,128)S(1)} %get-tuple-element.46), channel_id=1, source_target_pairs={{16,0},{17,1},{18,2},{19,3},{20,4},{21,5},{22,6},{23,7},{24,8},{25... | collective-permute-start | bytes 712712 | tf_op jit(solution)/shard_map/ppermute | solution.py:41
  18.0 1.8 %collective-permute-start.10 = (f32[232,256]{1,0:T(8,128)S(1)}, f32[232,256]{1,0:T(8,128)S(1)}, u32[]{:S(2)}, u32[]{:S(2)}) collective-permute-start(f32[232,256]{1,0:T(8,128)S(1)} %get-tuple-element.47), channel_id=1, source_target_pairs={{16,0},{17,1},{18,2},{19,3},{20,4},{21,5},{22,6},{23,7},{24,8},{25... | collective-permute-start | bytes 712712 | tf_op jit(solution)/shard_map/ppermute | solution.py:41

commit v6 on v5

--- a/solution.py
+++ b/solution.py
@@ -89,7 +89,7 @@
 def shorten_kernel(mine_ref, short_ref, head_ref, wide, sems):
     own, width = short_ref.shape
     parts = width // LANES
-    pieces = spans(0, own, up(-(-own // 4), TILE))
+    pieces = spans(0, own, up(-(-own // 2), TILE))
     copies = []
     for i, (low, high) in enumerate(pieces):
         rows = pl.ds(low * parts, (high - low) * parts)
@@ -243,6 +243,15 @@
         start_ref[low:high, :] += lag
 
 
+def side_share(rows, gather_ref, side):
+    width = rows.shape[1]
+    return jnp.dot(
+        jnp.concatenate([rows, rows], axis=1),
+        gather_ref[2 * side * width : 2 * (side + 1) * width, :],
+        preferred_element_type=F32,
+    )
+
+
 def sides_share(near_rows, far_rows, gather_ref):
     width = near_rows.shape[1]
     rows = jnp.concatenate([near_rows, near_rows, far_rows, far_rows], axis=1)
@@ -340,8 +349,19 @@
     return [jnp.where(upper, a, b) for a, b in halves], [jnp.where(upper, b, a) for a, b in halves]
 
 
+def near_kernel(core, near_ref, start_ref, take_ref, gather_ref, out_ref):
+    rows = slice(0, near_ref.shape[0])
+
+    @pl.when(lax.axis_index("sec") == core)
+    def _():
+        out_ref[rows, :] = start_ref[rows, :] + take_ref[rows, :] * side_share(near_ref[...], gather_ref, 0)
+        if near_ref.shape[0] < out_ref.shape[0]:
+            rest = slice(up(near_ref.shape[0], TILE), out_ref.shape[0])
+            out_ref[rest, :] = start_ref[rest, :]
+
+
 def first_kernel(
-    far_ref, near_ref, dfar_ref, dnear_ref, pack_ref, start_ref, lagged_ref, take_ref, gather_ref, *rest
+    dfar_ref, dnear_ref, far_ref, pack_ref, start_ref, lagged_ref, take_ref, gather_ref, *rest
 ):
     factors, (*full_refs, short_ref, smooth, columns) = rest[:6], rest[6:]
     _, half, width = pack_ref.shape
@@ -368,13 +388,11 @@
             dnear_ref[...], dfar_ref[...], gather_ref
         )
         rows = slice(0, first)
-        smooth[rows, :] = start_ref[rows, :] + take_ref[rows, :] * sides_share(
-            near_ref[rows, :], far_ref[rows, :], gather_ref
-        )
+        smooth[rows, :] = start_ref[rows, :] + take_ref[rows, :] * side_share(far_ref[rows, :], gather_ref, 1)
         part = lambda low: [smooth[low + f * half : low + (f + 1) * half, :] for f in range(SOLVED)]
         mine, theirs = solve_rows(part(0), part(base), columns, factors)
         rows = slice(first, own)
-        value = start_ref[rows, :] + take_ref[rows, :] * sides_share(near_ref[rows, :], far_ref[rows, :], gather_ref)
+        value = start_ref[rows, :] + take_ref[rows, :] * side_share(far_ref[rows, :], gather_ref, 1)
         for low, high in spans(first, own, CHUNK):
             emit(low, value[low - first : high - first])
         for f in range(SOLVED):
@@ -390,13 +408,13 @@
         store(total, pack_ref[2 * SOLVED].astype(F32))
 
 
-def last_kernel(near_ref, far_ref, brief_ref, start_ref, lagged_ref, mask_ref, rates_ref, take_ref, gather_ref, *rest):
+def last_kernel(far_ref, brief_ref, start_ref, lagged_ref, mask_ref, rates_ref, take_ref, gather_ref, *rest):
     factors, (out_ref, smooth, columns, held, sems) = rest[:6], rest[6:]
     own, width = lagged_ref.shape
     fields = rates_ref.shape[0]
     half = own // fields
     base = up(own, TILE)
-    total = near_ref.shape[0]
+    total = far_ref.shape[0]
     parts = width // LANES
     first = up(SOLVED * half, CHUNK)
 
@@ -408,8 +426,7 @@
     def _():
         def smoothed(low, high):
             rows = slice(low, high)
-            share = sides_share(near_ref[rows, :], far_ref[rows, :], gather_ref)
-            return start_ref[rows, :] + take_ref[rows, :] * share
+            return start_ref[rows, :] + take_ref[rows, :] * side_share(far_ref[rows, :], gather_ref, 1)
 
         smooth[0:first, :] = smoothed(0, first)
         smooth[base:total, :] = smoothed(base, total)
@@ -468,7 +485,7 @@
             out_shape=shorts,
             in_specs=[ANY],
             out_specs=[VMEM] * 2,
-            scratch_shapes=[pltpu.VMEM(mine.shape, F32), pltpu.SemaphoreType.DMA((4,))],
+            scratch_shapes=[pltpu.VMEM(mine.shape, F32), pltpu.SemaphoreType.DMA((2,))],
             compiler_params=params(4),
             cost_estimate=cost(3),
         ),
@@ -529,32 +546,45 @@
         )(*operands)[::-1]
         return start, factors[::-1]
 
+    def with_near(core, rows, start):
+        return pl.pallas_call(
+            functools.partial(near_kernel, core),
+            out_shape=shape((total, width), F32),
+            in_specs=[VMEM] * 4,
+            out_specs=VMEM,
+            compiler_params=params(8),
+            cost_estimate=cost(0),
+        )(rows, start, take, gather)
+
     start, factors = ready(ready_first_kernel, vert_coef, pack, state, lagged, keep, take, gather)
+
+    start = with_near(1, near_rows, start)
 
     scratch = [pltpu.VMEM((total, width), F32), pltpu.VMEM((SOLVED, width // LANES, depth, LANES), F32)]
     *full, brief = pl.pallas_call(
         first_kernel,
         out_shape=[shape((piece, width), F32)] * PIECES + [shape((total, width), BF16)],
-        in_specs=[VMEM] * 15,
+        in_specs=[VMEM] * 14,
         out_specs=[VMEM] * (PIECES + 1),
         scratch_shapes=scratch,
         compiler_params=params(24),
-    )(far_rows, near_rows, dfar, dnear, pack, start, lagged, take, gather, *factors)
-
-    near_rows = route(brief, (1, 0, near, 0), (0, 1, same, 0))
-    far_rows = route(brief, (1, 0, far, 0))
+    )(dfar, dnear, far_rows, pack, start, lagged, take, gather, *factors)
+
+    near_rows = route(brief, (1, 0, near, 0))
+    far_rows = route(brief, (1, 0, far, 0), (0, 1, same, 0))
     pieces = [route(part, back, (0, 1, same, 0)) for part in full]
     start, factors = ready(
         functools.partial(ready_last_kernel, total), vert_coef, lagged, keep, take, gather, *pieces
     )
+    start = with_near(0, near_rows, start)
     out = pl.pallas_call(
         last_kernel,
         out_shape=shape(mine.shape, F32),
-        in_specs=[VMEM] * 15,
+        in_specs=[VMEM] * 14,
         out_specs=ANY,
         scratch_shapes=scratch + [pltpu.VMEM(mine.shape, F32), pltpu.SemaphoreType.DMA((2,))],
         compiler_params=params(24),
-    )(near_rows, far_rows, brief, start, lagged, precip_mask, rates, take, gather, *factors)
+    )(far_rows, brief, start, lagged, precip_mask, rates, take, gather, *factors)
     return out.reshape(sections.shape)
 
 

time: 25.8 us -> 25.5 us (0.988)
    pallas_call x0 -> x2, Pallas kernels: none -> 0.37 us  [with_near(): pl.pallas_call(functools.partial(near_kernel, core), out_shape=shape((tot...]
  transfers between devices with their start and end apart: 11 -> 11, of which waited for: 6 -> 5; matrix products, arithmetic and copies ran while one was open for 0% -> 0% of each run, Pallas kernels for 14% -> 15%
where the time goes in v6:
time: 25.5 us; the launch traced here: 25.4 us
  starting transfers between devices  14.2 us (56%)
  waiting for transfers between devices  6 us (24%)
  Pallas kernels  4.99 us (20%)
    ppermute x11, starting transfers between devices, route(): return lax.ppermute(array, AXES, table)  14.2 us
    ppermute x11, waiting for transfers between devices, route(): return lax.ppermute(array, AXES, table)  6 us
    pallas_call x1, Pallas kernels, shards(): pl.pallas_call(last_kernel, out_shape=shape(mine.shape, F32), in_specs=[V...  1.23 us
    pallas_call x1, Pallas kernels, shards(): pl.pallas_call(prepare_kernel, out_shape=[shape((7 * width, width), BF16)...  1.2 us
    pallas_call x1, Pallas kernels, shards(): lax.cond(lax.axis_index('sec') == 0, pl.pallas_call(shorten_kernel, out_s...  1.08 us
    pallas_call x2, Pallas kernels, ready(): pl.pallas_call(kernel, out_shape=[chunk] * 5 + [shape((6, SUB, width), F3...  1.08 us
  transfers between devices with their start and end apart: 11, of which 5 were waited for; matrix products, arithmetic and copies ran while one was open for 0% of the time, Pallas kernels for 15%

profile of v6, /device:TPU:0, one launch (start us, length us, event | category | flops | bytes accessed | tf_op | source)
XLA Modules:
  0.0 25.4 jit_solution(7691203488012306509)
XLA Ops:
  0.0 0.5 %collective-permute-start.3 = (f32[1080,128]{1,0:T(8,128)}, f32[1080,128]{1,0:T(8,128)S(1)}, u32[]{:S(2)}, u32[]{:S(2)}) collective-permute-start(f32[1080,128]{1,0:T(8,128)} %bitcast.2), channel_id=1, source_target_pairs={{0,16},{1,17},{2,18},{3,19},{4,20},{5,21},{6,22},{7,23},{8,24},{9,... | collective-permute-start | bytes 1658888 | tf_op jit(solution)/shard_map/ppermute | solution.py:41
  0.5 0.0 copy-start
  0.5 1.1 %conditional.1 = ((bf16[540,256]{1,0:T(8,128)(2,1)S(1)}, bf16[90,256]{1,0:T(8,128)(2,1)S(1)})) conditional(s32[]{:T(128)} %convert_element_type.3, () %tuple.11, f32[1080,128]{1,0:T(8,128)} %bitcast.3), branch_computations={%region_0.0_spmd, %region_1.0_spmd} | conditional | flops 3000000000 | bytes 8 | solution.py:481
  0.5 1.1 %branch_1_fun.1 = (bf16[540,256]{1,0:T(8,128)(2,1)S(1)}, bf16[90,256]{1,0:T(8,128)(2,1)S(1)}) custom-call(f32[1080,128]{1,0:T(8,128)} %mine_ref), custom_call_target="tpu_custom_call" | custom-call | flops 3000000000 | tf_op jit(solution)/shard_map/cond/branch_1_fun/pallas_call | solution.py:481
  1.5 0.0 copy-start.6
  1.6 1.6 %collective-permute-start.5 = (bf16[540,256]{1,0:T(8,128)(2,1)S(1)}, bf16[540,256]{1,0:T(8,128)(2,1)S(1)}, u32[]{:S(2)}, u32[]{:S(2)}) collective-permute-start(bf16[540,256]{1,0:T(8,128)(2,1)S(1)} %get-tuple-element.32.short_ref), channel_id=1, source_target_pairs={{0,18},{1,19},{2,16},{3,17},{4,22},{5,23},{6,20},{7,21},{8,26},{9,... | collective-permute-start | bytes 829448 | tf_op jit(solution)/shard_map/ppermute | solution.py:41
  3.2 4.1 %collective-permute-start.2 = (bf16[540,256]{1,0:T(8,128)(2,1)S(1)}, bf16[540,256]{1,0:T(8,128)(2,1)S(1)}, u32[]{:S(2)}, u32[]{:S(2)}) collective-permute-start(bf16[540,256]{1,0:T(8,128)(2,1)S(1)} %get-tuple-element.32.short_ref), channel_id=1, source_target_pairs={{0,30},{1,31},{2,20},{3,21},{4,18},{5,19},{6,24},{7,25},{8,22},{9,... | collective-permute-start | bytes 829448 | tf_op jit(solution)/shard_map/ppermute | solution.py:41
  7.3 0.0 collective-permute-done.3.other_ref.state_ref
  7.3 0.0 copy-done
  7.3 0.0 copy-start.1
  7.3 0.0 copy-start.2
  7.3 0.0 copy-start.3
  7.3 0.0 copy-start.4
  7.3 0.0 copy-start.5
  7.4 0.1 collective-permute-start.4
  7.5 0.1 collective-permute-start.1
  7.5 2.1 %collective-permute-start = (bf16[90,256]{1,0:T(8,128)(2,1)S(1)}, bf16[90,256]{1,0:T(8,128)(2,1)S(1)}, u32[]{:S(2)}, u32[]{:S(2)}) collective-permute-start(bf16[90,256]{1,0:T(8,128)(2,1)S(1)} %get-tuple-element.31.head_ref), channel_id=1, source_target_pairs={{0,31},{1,30},{2,21},{3,20},{4,19},{5,18},{6,25},{7,24},{8,23},{9,... | collective-permute-start | bytes 138248 | tf_op jit(solution)/shard_map/ppermute | solution.py:41
  9.6 0.0 copy-done.6
  9.6 0.0 copy-done.1
  9.6 0.0 copy-done.2
  9.6 0.0 copy-done.3
  9.6 0.0 copy-done.4
  9.6 0.0 copy-done.5
  9.6 1.2 %shard_map.74 = (bf16[1792,256]{1,0:T(8,128)(2,1)S(1)}, bf16[540,256]{1,0:T(8,128)(2,1)S(1)}, f32[12,256]{1,0:T(8,128)S(1)}, f32[640,256]{1,0:T(8,128)S(1)}, f32[640,256]{1,0:T(8,128)S(1)}) custom-call(f32[1080,128]{1,0:T(8,128)S(1)} %bitcast.4, bf16[540,256]{1,0:T(8,128)(2,1)S(1)} %get-tuple-element.32.short_ref, s32[3,256]{1,0:T(4,128)S(1)} %copy-done.2, ...), custom_call_target="tpu_custom_call" | custom-call | flops 10000000 | tf_op jit(solution)/shard_map/pallas_call | solution.py:514
  10.8 0.0 collective-permute-done.4.pack_ref
  10.9 0.0 collective-permute-done.5.near_ref
  10.9 0.0 collective-permute-done.1.dnear_ref
  10.9 1.0 %collective-permute-done.dfar_ref = bf16[90,256]{1,0:T(8,128)(2,1)S(1)} collective-permute-done((bf16[90,256]{1,0:T(8,128)(2,1)S(1)}, bf16[90,256]{1,0:T(8,128)(2,1)S(1)}, u32[]{:S(2)}, u32[]{:S(2)}) %collective-permute-start) | collective-permute-done | bytes 46112 | tf_op jit(solution)/shard_map/ppermute | solution.py:41
  11.9 0.0 collective-permute-done.2.far_ref
  11.9 1.3 %collective-permute-start.7 = (bf16[640,256]{1,0:T(8,128)(2,1)S(1)}, bf16[640,256]{1,0:T(8,128)(2,1)S(1)}, u32[]{:S(2)}, u32[]{:S(2)}) collective-permute-start(bf16[640,256]{1,0:T(8,128)(2,1)S(1)} %get-tuple-element.44.brief_ref), channel_id=1, source_target_pairs={{16,2},{17,3},{18,0},{19,1},{20,6},{21,7},{22,4},{23,5},{24,10},{2... | collective-permute-start | bytes 983048 | tf_op jit(solution)/shard_map/ppermute | solution.py:41
  13.2 3.9 %collective-permute-start.6 = (bf16[640,256]{1,0:T(8,128)(2,1)S(1)}, bf16[640,256]{1,0:T(8,128)(2,1)S(1)}, u32[]{:S(2)}, u32[]{:S(2)}) collective-permute-start(bf16[640,256]{1,0:T(8,128)(2,1)S(1)} %get-tuple-element.44.brief_ref), channel_id=1, source_target_pairs={{16,14},{17,15},{18,4},{19,5},{20,2},{21,3},{22,8},{23,9},{24,6},{... | collective-permute-start | bytes 983048 | tf_op jit(solution)/shard_map/ppermute | solution.py:41
  17.1 0.1 collective-permute-start.8
  17.2 0.4 %collective-permute-start.9 = (f32[232,256]{1,0:T(8,128)S(1)}, f32[232,256]{1,0:T(8,128)S(1)}, u32[]{:S(2)}, u32[]{:S(2)}) collective-permute-start(f32[232,256]{1,0:T(8,128)S(1)} %get-tuple-element.46), channel_id=1, source_target_pairs={{16,0},{17,1},{18,2},{19,3},{20,4},{21,5},{22,6},{23,7},{24,8},{25... | collective-permute-start | bytes 712712 | tf_op jit(solution)/shard_map/ppermute | solution.py:41
  17.6 0.1 collective-permute-start.10
  17.7 1.0 %collective-permute-done.8.rest_0_ = f32[232,256]{1,0:T(8,128)S(1)} collective-permute-done((f32[232,256]{1,0:T(8,128)S(1)}, f32[232,256]{1,0:T(8,128)S(1)}, u32[]{:S(2)}, u32[]{:S(2)}) %collective-permute-start.8) | collective-permute-done | bytes 237600 | tf_op jit(solution)/shard_map/ppermute | solution.py:41
  18.7 0.3 %collective-permute-done.9.rest_1_ = f32[232,256]{1,0:T(8,128)S(1)} collective-permute-done((f32[232,256]{1,0:T(8,128)S(1)}, f32[232,256]{1,0:T(8,128)S(1)}, u32[]{:S(2)}, u32[]{:S(2)}) %collective-permute-start.9) | collective-permute-done | bytes 237600 | tf_op jit(solution)/shard_map/ppermute | solution.py:41
  19.0 0.3 %collective-permute-done.10.rest_2_ = f32[232,256]{1,0:T(8,128)S(1)} collective-permute-done((f32[232,256]{1,0:T(8,128)S(1)}, f32[232,256]{1,0:T(8,128)S(1)}, u32[]{:S(2)}, u32[]{:S(2)}) %collective-permute-start.10) | collective-permute-done | bytes 237600 | tf_op jit(solution)/shard_map/ppermute | solution.py:41
  19.3 1.1 %shard_map.78 = (f32[12,8,256]{2,1,0:T(8,128)S(1)}, f32[12,8,256]{2,1,0:T(8,128)S(1)}, f32[12,8,256]{2,1,0:T(8,128)S(1)}, f32[12,8,256]{2,1,0:T(8,128)S(1)}, f32...) custom-call(f32[45,256]{1,0:T(8,128)S(1)} %copy-done, ...), custom_call_target="tpu_custom_call" | custom-call | tf_op jit(solution)/shard_map/pallas_call | solution.py:533
  20.4 0.0 collective-permute-done.7.near_ref
  20.4 0.4 %shard_map.79.start_ref = f32[640,256]{1,0:T(8,128)S(1)} custom-call(bf16[640,256]{1,0:T(8,128)(2,1)S(1)} %collective-permute-done.7.near_ref, f32[640,256]{1,0:T(8,128)S(1)} %get-tuple-element.48.start_ref, f32[640,256]{1,0:T(8,128)S(1)} %get-tuple-element.35.take_ref, bf16[1792,256]{1,0:T(8,128)(2,1)S(1)} %get-tuple-element.36.gather_ref), custom_call_target="tpu_custom_call" | custom-call | tf_op jit(solution)/shard_map/pallas_call | solution.py:550
  20.8 3.3 %collective-permute-done.6.far_ref = bf16[640,256]{1,0:T(8,128)(2,1)S(1)} collective-permute-done((bf16[640,256]{1,0:T(8,128)(2,1)S(1)}, bf16[640,256]{1,0:T(8,128)(2,1)S(1)}, u32[]{:S(2)}, u32[]{:S(2)}) %collective-permute-start.6) | collective-permute-done | bytes 327712 | tf_op jit(solution)/shard_map/ppermute | solution.py:41
  24.1 1.2 %shard_map.80 = f32[1080,128]{1,0:T(8,128)} custom-call(bf16[640,256]{1,0:T(8,128)(2,1)S(1)} %collective-permute-done.6.far_ref, bf16[640,256]{1,0:T(8,128)(2,1)S(1)} %get-tuple-element.44.brief_ref, f32[640,256]{1,0:T(8,128)S(1)} %shard_map.79.start_ref, bf16[540,256]{1,0:T(8,128)(2,1)S(1)} %get-tuple-element.33.lagged_ref, s32[2,256]{1,0:T(2,128)S(1)} %copy-done.1, ...), custom_call_target="tpu_custom_call" | custom-call | tf_op jit(solution)/shard_map/pallas_call | solution.py:580
  (4 shorter events, 0.1 us)
Async XLA Ops:
  0.0 7.3 %collective-permute-start.3 = (f32[1080,128]{1,0:T(8,128)}, f32[1080,128]{1,0:T(8,128)S(1)}, u32[]{:S(2)}, u32[]{:S(2)}) collective-permute-start(f32[1080,128]{1,0:T(8,128)} %bitcast.2), channel_id=1, source_target_pairs={{0,16},{1,17},{2,18},{3,19},{4,20},{5,21},{6,22},{7,23},{8,24},{9,... | collective-permute-start | bytes 1658888 | tf_op jit(solution)/shard_map/ppermute | solution.py:41
  0.5 6.8 %copy-start = (f32[45,256]{1,0:T(8,128)S(1)}, f32[45,256]{1,0:T(8,128)}, u32[]{:S(2)}) copy-start(f32[45,256]{1,0:T(8,128)} %kappa_ref.5) | copy-start | bytes 138244
  1.5 8.1 %copy-start.6 = (f32[1,12,45,256]{3,0,2,1:T(1,128)S(1)}, f32[1,12,45,256]{3,0,2,1:T(1,128)}, u32[]{:S(2)}) copy-start(f32[1,12,45,256]{3,0,2,1:T(1,128)} %param.9) | copy-start | bytes 1658884
  1.6 9.3 %collective-permute-start.5 = (bf16[540,256]{1,0:T(8,128)(2,1)S(1)}, bf16[540,256]{1,0:T(8,128)(2,1)S(1)}, u32[]{:S(2)}, u32[]{:S(2)}) collective-permute-start(bf16[540,256]{1,0:T(8,128)(2,1)S(1)} %get-tuple-element.32.short_ref), channel_id=1, source_target_pairs={{0,18},{1,19},{2,16},{3,17},{4,22},{5,23},{6,20},{7,21},{8,26},{9,... | collective-permute-start | bytes 829448 | tf_op jit(solution)/shard_map/ppermute | solution.py:41
  3.2 8.7 %collective-permute-start.2 = (bf16[540,256]{1,0:T(8,128)(2,1)S(1)}, bf16[540,256]{1,0:T(8,128)(2,1)S(1)}, u32[]{:S(2)}, u32[]{:S(2)}) collective-permute-start(bf16[540,256]{1,0:T(8,128)(2,1)S(1)} %get-tuple-element.32.short_ref), channel_id=1, source_target_pairs={{0,30},{1,31},{2,20},{3,21},{4,18},{5,19},{6,24},{7,25},{8,22},{9,... | collective-permute-start | bytes 829448 | tf_op jit(solution)/shard_map/ppermute | solution.py:41
  7.3 2.3 %copy-start.1 = (s32[2,256]{1,0:T(2,128)S(1)}, s32[2,256]{1,0:T(2,128)}, u32[]{:S(2)}) copy-start(s32[2,256]{1,0:T(2,128)} %mask_ref.3) | copy-start | bytes 6148
  7.3 2.3 %copy-start.2 = (s32[3,256]{1,0:T(4,128)S(1)}, s32[3,256]{1,0:T(4,128)}, u32[]{:S(2)}) copy-start(s32[3,256]{1,0:T(4,128)} %nbr_ref.1) | copy-start | bytes 9220
  7.3 2.3 %copy-start.3 = (f32[3,256]{1,0:T(4,128)S(1)}, f32[3,256]{1,0:T(4,128)}, u32[]{:S(2)}) copy-start(f32[3,256]{1,0:T(4,128)} %weight_ref.1) | copy-start | bytes 9220
  7.3 2.3 %copy-start.4 = (f32[12]{0:T(128)S(1)}, f32[12]{0:T(128)}, u32[]{:S(2)}) copy-start(f32[12]{0:T(128)} %relax_ref.1) | copy-start | bytes 148
  7.3 2.3 %copy-start.5 = (f32[12]{0:T(128)S(1)}, f32[12]{0:T(128)}, u32[]{:S(2)}) copy-start(f32[12]{0:T(128)} %diff_ref.1) | copy-start | bytes 148
  7.4 3.5 %collective-permute-start.4 = (bf16[5,45,256]{2,1,0:T(8,128)(2,1)S(1)}, bf16[5,45,256]{2,1,0:T(8,128)(2,1)S(1)}, u32[]{:S(2)}, u32[]{:S(2)}) collective-permute-start(bf16[5,45,256]{2,1,0:T(8,128)(2,1)S(1)} %shard_map.73), channel_id=1, source_target_pairs={{0,17},{1,16},{2,19},{3,18},{4,21},{5,20},{6,23},{7,22},{8,25},{9,... | collective-permute-start | bytes 345608 | tf_op jit(solution)/shard_map/ppermute | solution.py:41
  7.5 3.5 %collective-permute-start.1 = (bf16[90,256]{1,0:T(8,128)(2,1)S(1)}, bf16[90,256]{1,0:T(8,128)(2,1)S(1)}, u32[]{:S(2)}, u32[]{:S(2)}) collective-permute-start(bf16[90,256]{1,0:T(8,128)(2,1)S(1)} %get-tuple-element.31.head_ref), channel_id=1, source_target_pairs={{0,19},{1,18},{2,17},{3,16},{4,23},{5,22},{6,21},{7,20},{8,27},{9,... | collective-permute-start | bytes 138248 | tf_op jit(solution)/shard_map/ppermute | solution.py:41
  7.5 4.4 %collective-permute-start = (bf16[90,256]{1,0:T(8,128)(2,1)S(1)}, bf16[90,256]{1,0:T(8,128)(2,1)S(1)}, u32[]{:S(2)}, u32[]{:S(2)}) collective-permute-start(bf16[90,256]{1,0:T(8,128)(2,1)S(1)} %get-tuple-element.31.head_ref), channel_id=1, source_target_pairs={{0,31},{1,30},{2,21},{3,20},{4,19},{5,18},{6,25},{7,24},{8,23},{9,... | collective-permute-start | bytes 138248 | tf_op jit(solution)/shard_map/ppermute | solution.py:41
  11.9 8.5 %collective-permute-start.7 = (bf16[640,256]{1,0:T(8,128)(2,1)S(1)}, bf16[640,256]{1,0:T(8,128)(2,1)S(1)}, u32[]{:S(2)}, u32[]{:S(2)}) collective-permute-start(bf16[640,256]{1,0:T(8,128)(2,1)S(1)} %get-tuple-element.44.brief_ref), channel_id=1, source_target_pairs={{16,2},{17,3},{18,0},{19,1},{20,6},{21,7},{22,4},{23,5},{24,10},{2... | collective-permute-start | bytes 983048 | tf_op jit(solution)/shard_map/ppermute | solution.py:41
  13.2 10.9 %collective-permute-start.6 = (bf16[640,256]{1,0:T(8,128)(2,1)S(1)}, bf16[640,256]{1,0:T(8,128)(2,1)S(1)}, u32[]{:S(2)}, u32[]{:S(2)}) collective-permute-start(bf16[640,256]{1,0:T(8,128)(2,1)S(1)} %get-tuple-element.44.brief_ref), channel_id=1, source_target_pairs={{16,14},{17,15},{18,4},{19,5},{20,2},{21,3},{22,8},{23,9},{24,6},{... | collective-permute-start | bytes 983048 | tf_op jit(solution)/shard_map/ppermute | solution.py:41
  17.1 1.6 %collective-permute-start.8 = (f32[232,256]{1,0:T(8,128)S(1)}, f32[232,256]{1,0:T(8,128)S(1)}, u32[]{:S(2)}, u32[]{:S(2)}) collective-permute-start(f32[232,256]{1,0:T(8,128)S(1)} %get-tuple-element.45), channel_id=1, source_target_pairs={{16,0},{17,1},{18,2},{19,3},{20,4},{21,5},{22,6},{23,7},{24,8},{25... | collective-permute-start | bytes 712712 | tf_op jit(solution)/shard_map/ppermute | solution.py:41
  17.2 1.9 %collective-permute-start.9 = (f32[232,256]{1,0:T(8,128)S(1)}, f32[232,256]{1,0:T(8,128)S(1)}, u32[]{:S(2)}, u32[]{:S(2)}) collective-permute-start(f32[232,256]{1,0:T(8,128)S(1)} %get-tuple-element.46), channel_id=1, source_target_pairs={{16,0},{17,1},{18,2},{19,3},{20,4},{21,5},{22,6},{23,7},{24,8},{25... | collective-permute-start | bytes 712712 | tf_op jit(solution)/shard_map/ppermute | solution.py:41
  17.6 1.8 %collective-permute-start.10 = (f32[232,256]{1,0:T(8,128)S(1)}, f32[232,256]{1,0:T(8,128)S(1)}, u32[]{:S(2)}, u32[]{:S(2)}) collective-permute-start(f32[232,256]{1,0:T(8,128)S(1)} %get-tuple-element.47), channel_id=1, source_target_pairs={{16,0},{17,1},{18,2},{19,3},{20,4},{21,5},{22,6},{23,7},{24,8},{25... | collective-permute-start | bytes 712712 | tf_op jit(solution)/shard_map/ppermute | solution.py:41

commit v7 on v6

--- a/solution.py
+++ b/solution.py
@@ -115,8 +115,9 @@
 
     @pl.when(lax.axis_index("sec") == 0)
     def _():
+        head = head_ref[...].astype(F32)
         for f in range(SOLVED):
-            pack_ref[f] = head_ref[f * half : (f + 1) * half, :]
+            pack_ref[f] = head[f * half : (f + 1) * half].astype(BF16)
             pack_ref[SOLVED + f] = get_rows(other_ref, f * half, (f + 1) * half, parts).astype(BF16)
 
     pack_ref[2 * SOLVED] = kappa_ref[...].astype(BF16)

time: 25.5 us -> 25.5 us (level)
  no operation moved by 1% of the time
where the time goes in v7:
time: 25.5 us; the launch traced here: 25.4 us
  starting transfers between devices  14.2 us (56%)
  waiting for transfers between devices  6 us (24%)
  Pallas kernels  4.98 us (20%)
    ppermute x11, starting transfers between devices, route(): return lax.ppermute(array, AXES, table)  14.2 us
    ppermute x11, waiting for transfers between devices, route(): return lax.ppermute(array, AXES, table)  6 us
    pallas_call x1, Pallas kernels, shards(): pl.pallas_call(last_kernel, out_shape=shape(mine.shape, F32), in_specs=[V...  1.23 us
    pallas_call x1, Pallas kernels, shards(): pl.pallas_call(prepare_kernel, out_shape=[shape((7 * width, width), BF16)...  1.2 us
    pallas_call x1, Pallas kernels, shards(): lax.cond(lax.axis_index('sec') == 0, pl.pallas_call(shorten_kernel, out_s...  1.08 us
    pallas_call x2, Pallas kernels, ready(): pl.pallas_call(kernel, out_shape=[chunk] * 5 + [shape((6, SUB, width), F3...  1.07 us
  transfers between devices with their start and end apart: 11, of which 5 were waited for; matrix products, arithmetic and copies ran while one was open for 0% of the time, Pallas kernels for 15%

profile of v7, /device:TPU:0, one launch (start us, length us, event | category | flops | bytes accessed | tf_op | source)
XLA Modules:
  0.0 25.4 jit_solution(16355827309468257342)
XLA Ops:
  0.0 0.5 %collective-permute-start.3 = (f32[1080,128]{1,0:T(8,128)}, f32[1080,128]{1,0:T(8,128)S(1)}, u32[]{:S(2)}, u32[]{:S(2)}) collective-permute-start(f32[1080,128]{1,0:T(8,128)} %bitcast.2), channel_id=1, source_target_pairs={{0,16},{1,17},{2,18},{3,19},{4,20},{5,21},{6,22},{7,23},{8,24},{9,... | collective-permute-start | bytes 1658888 | tf_op jit(solution)/shard_map/ppermute | solution.py:41
  0.5 0.0 copy-start
  0.5 1.1 %conditional.1 = ((bf16[540,256]{1,0:T(8,128)(2,1)S(1)}, bf16[90,256]{1,0:T(8,128)(2,1)S(1)})) conditional(s32[]{:T(128)} %convert_element_type.3, () %tuple.11, f32[1080,128]{1,0:T(8,128)} %bitcast.3), branch_computations={%region_0.0_spmd, %region_1.0_spmd} | conditional | flops 3000000000 | bytes 8 | solution.py:482
  0.5 1.1 %branch_1_fun.1 = (bf16[540,256]{1,0:T(8,128)(2,1)S(1)}, bf16[90,256]{1,0:T(8,128)(2,1)S(1)}) custom-call(f32[1080,128]{1,0:T(8,128)} %mine_ref), custom_call_target="tpu_custom_call" | custom-call | flops 3000000000 | tf_op jit(solution)/shard_map/cond/branch_1_fun/pallas_call | solution.py:482
  1.5 0.0 copy-start.6
  1.6 1.6 %collective-permute-start.5 = (bf16[540,256]{1,0:T(8,128)(2,1)S(1)}, bf16[540,256]{1,0:T(8,128)(2,1)S(1)}, u32[]{:S(2)}, u32[]{:S(2)}) collective-permute-start(bf16[540,256]{1,0:T(8,128)(2,1)S(1)} %get-tuple-element.32.short_ref), channel_id=1, source_target_pairs={{0,18},{1,19},{2,16},{3,17},{4,22},{5,23},{6,20},{7,21},{8,26},{9,... | collective-permute-start | bytes 829448 | tf_op jit(solution)/shard_map/ppermute | solution.py:41
  3.2 4.1 %collective-permute-start.2 = (bf16[540,256]{1,0:T(8,128)(2,1)S(1)}, bf16[540,256]{1,0:T(8,128)(2,1)S(1)}, u32[]{:S(2)}, u32[]{:S(2)}) collective-permute-start(bf16[540,256]{1,0:T(8,128)(2,1)S(1)} %get-tuple-element.32.short_ref), channel_id=1, source_target_pairs={{0,30},{1,31},{2,20},{3,21},{4,18},{5,19},{6,24},{7,25},{8,22},{9,... | collective-permute-start | bytes 829448 | tf_op jit(solution)/shard_map/ppermute | solution.py:41
  7.3 0.0 collective-permute-done.3.other_ref.state_ref
  7.3 0.0 copy-done
  7.3 0.0 copy-start.1
  7.3 0.0 copy-start.2
  7.3 0.0 copy-start.3
  7.3 0.0 copy-start.4
  7.3 0.0 copy-start.5
  7.4 0.1 collective-permute-start.4
  7.4 0.1 collective-permute-start.1
  7.5 2.1 %collective-permute-start = (bf16[90,256]{1,0:T(8,128)(2,1)S(1)}, bf16[90,256]{1,0:T(8,128)(2,1)S(1)}, u32[]{:S(2)}, u32[]{:S(2)}) collective-permute-start(bf16[90,256]{1,0:T(8,128)(2,1)S(1)} %get-tuple-element.31.head_ref), channel_id=1, source_target_pairs={{0,31},{1,30},{2,21},{3,20},{4,19},{5,18},{6,25},{7,24},{8,23},{9,... | collective-permute-start | bytes 138248 | tf_op jit(solution)/shard_map/ppermute | solution.py:41
  9.6 0.0 copy-done.6
  9.6 0.0 copy-done.1
  9.6 0.0 copy-done.2
  9.6 0.0 copy-done.3
  9.6 0.0 copy-done.4
  9.6 0.0 copy-done.5
  9.6 1.2 %shard_map.74 = (bf16[1792,256]{1,0:T(8,128)(2,1)S(1)}, bf16[540,256]{1,0:T(8,128)(2,1)S(1)}, f32[12,256]{1,0:T(8,128)S(1)}, f32[640,256]{1,0:T(8,128)S(1)}, f32[640,256]{1,0:T(8,128)S(1)}) custom-call(f32[1080,128]{1,0:T(8,128)S(1)} %bitcast.4, bf16[540,256]{1,0:T(8,128)(2,1)S(1)} %get-tuple-element.32.short_ref, s32[3,256]{1,0:T(4,128)S(1)} %copy-done.2, ...), custom_call_target="tpu_custom_call" | custom-call | flops 10000000 | tf_op jit(solution)/shard_map/pallas_call | solution.py:515
  10.8 0.0 collective-permute-done.4.pack_ref
  10.9 0.0 collective-permute-done.5.near_ref
  10.9 0.0 collective-permute-done.1.dnear_ref
  10.9 1.0 %collective-permute-done.dfar_ref = bf16[90,256]{1,0:T(8,128)(2,1)S(1)} collective-permute-done((bf16[90,256]{1,0:T(8,128)(2,1)S(1)}, bf16[90,256]{1,0:T(8,128)(2,1)S(1)}, u32[]{:S(2)}, u32[]{:S(2)}) %collective-permute-start) | collective-permute-done | bytes 46112 | tf_op jit(solution)/shard_map/ppermute | solution.py:41
  11.9 0.0 collective-permute-done.2.far_ref
  11.9 1.3 %collective-permute-start.7 = (bf16[640,256]{1,0:T(8,128)(2,1)S(1)}, bf16[640,256]{1,0:T(8,128)(2,1)S(1)}, u32[]{:S(2)}, u32[]{:S(2)}) collective-permute-start(bf16[640,256]{1,0:T(8,128)(2,1)S(1)} %get-tuple-element.44.brief_ref), channel_id=1, source_target_pairs={{16,2},{17,3},{18,0},{19,1},{20,6},{21,7},{22,4},{23,5},{24,10},{2... | collective-permute-start | bytes 983048 | tf_op jit(solution)/shard_map/ppermute | solution.py:41
  13.2 3.9 %collective-permute-start.6 = (bf16[640,256]{1,0:T(8,128)(2,1)S(1)}, bf16[640,256]{1,0:T(8,128)(2,1)S(1)}, u32[]{:S(2)}, u32[]{:S(2)}) collective-permute-start(bf16[640,256]{1,0:T(8,128)(2,1)S(1)} %get-tuple-element.44.brief_ref), channel_id=1, source_target_pairs={{16,14},{17,15},{18,4},{19,5},{20,2},{21,3},{22,8},{23,9},{24,6},{... | collective-permute-start | bytes 983048 | tf_op jit(solution)/shard_map/ppermute | solution.py:41
  17.1 0.1 collective-permute-start.8
  17.2 0.4 %collective-permute-start.9 = (f32[232,256]{1,0:T(8,128)S(1)}, f32[232,256]{1,0:T(8,128)S(1)}, u32[]{:S(2)}, u32[]{:S(2)}) collective-permute-start(f32[232,256]{1,0:T(8,128)S(1)} %get-tuple-element.46), channel_id=1, source_target_pairs={{16,0},{17,1},{18,2},{19,3},{20,4},{21,5},{22,6},{23,7},{24,8},{25... | collective-permute-start | bytes 712712 | tf_op jit(solution)/shard_map/ppermute | solution.py:41
  17.6 0.1 collective-permute-start.10
  17.7 1.0 %collective-permute-done.8.rest_0_ = f32[232,256]{1,0:T(8,128)S(1)} collective-permute-done((f32[232,256]{1,0:T(8,128)S(1)}, f32[232,256]{1,0:T(8,128)S(1)}, u32[]{:S(2)}, u32[]{:S(2)}) %collective-permute-start.8) | collective-permute-done | bytes 237600 | tf_op jit(solution)/shard_map/ppermute | solution.py:41
  18.7 0.3 %collective-permute-done.9.rest_1_ = f32[232,256]{1,0:T(8,128)S(1)} collective-permute-done((f32[232,256]{1,0:T(8,128)S(1)}, f32[232,256]{1,0:T(8,128)S(1)}, u32[]{:S(2)}, u32[]{:S(2)}) %collective-permute-start.9) | collective-permute-done | bytes 237600 | tf_op jit(solution)/shard_map/ppermute | solution.py:41
  19.0 0.3 %collective-permute-done.10.rest_2_ = f32[232,256]{1,0:T(8,128)S(1)} collective-permute-done((f32[232,256]{1,0:T(8,128)S(1)}, f32[232,256]{1,0:T(8,128)S(1)}, u32[]{:S(2)}, u32[]{:S(2)}) %collective-permute-start.10) | collective-permute-done | bytes 237600 | tf_op jit(solution)/shard_map/ppermute | solution.py:41
  19.3 1.1 %shard_map.78 = (f32[12,8,256]{2,1,0:T(8,128)S(1)}, f32[12,8,256]{2,1,0:T(8,128)S(1)}, f32[12,8,256]{2,1,0:T(8,128)S(1)}, f32[12,8,256]{2,1,0:T(8,128)S(1)}, f32...) custom-call(f32[45,256]{1,0:T(8,128)S(1)} %copy-done, ...), custom_call_target="tpu_custom_call" | custom-call | tf_op jit(solution)/shard_map/pallas_call | solution.py:534
  20.4 0.0 collective-permute-done.7.near_ref
  20.4 0.4 %shard_map.79.start_ref = f32[640,256]{1,0:T(8,128)S(1)} custom-call(bf16[640,256]{1,0:T(8,128)(2,1)S(1)} %collective-permute-done.7.near_ref, f32[640,256]{1,0:T(8,128)S(1)} %get-tuple-element.48.start_ref, f32[640,256]{1,0:T(8,128)S(1)} %get-tuple-element.35.take_ref, bf16[1792,256]{1,0:T(8,128)(2,1)S(1)} %get-tuple-element.36.gather_ref), custom_call_target="tpu_custom_call" | custom-call | tf_op jit(solution)/shard_map/pallas_call | solution.py:551
  20.8 3.3 %collective-permute-done.6.far_ref = bf16[640,256]{1,0:T(8,128)(2,1)S(1)} collective-permute-done((bf16[640,256]{1,0:T(8,128)(2,1)S(1)}, bf16[640,256]{1,0:T(8,128)(2,1)S(1)}, u32[]{:S(2)}, u32[]{:S(2)}) %collective-permute-start.6) | collective-permute-done | bytes 327712 | tf_op jit(solution)/shard_map/ppermute | solution.py:41
  24.1 1.2 %shard_map.80 = f32[1080,128]{1,0:T(8,128)} custom-call(bf16[640,256]{1,0:T(8,128)(2,1)S(1)} %collective-permute-done.6.far_ref, bf16[640,256]{1,0:T(8,128)(2,1)S(1)} %get-tuple-element.44.brief_ref, f32[640,256]{1,0:T(8,128)S(1)} %shard_map.79.start_ref, bf16[540,256]{1,0:T(8,128)(2,1)S(1)} %get-tuple-element.33.lagged_ref, s32[2,256]{1,0:T(2,128)S(1)} %copy-done.1, ...), custom_call_target="tpu_custom_call" | custom-call | tf_op jit(solution)/shard_map/pallas_call | solution.py:581
  (4 shorter events, 0.1 us)
Async XLA Ops:
  0.0 7.3 %collective-permute-start.3 = (f32[1080,128]{1,0:T(8,128)}, f32[1080,128]{1,0:T(8,128)S(1)}, u32[]{:S(2)}, u32[]{:S(2)}) collective-permute-start(f32[1080,128]{1,0:T(8,128)} %bitcast.2), channel_id=1, source_target_pairs={{0,16},{1,17},{2,18},{3,19},{4,20},{5,21},{6,22},{7,23},{8,24},{9,... | collective-permute-start | bytes 1658888 | tf_op jit(solution)/shard_map/ppermute | solution.py:41
  0.5 6.8 %copy-start = (f32[45,256]{1,0:T(8,128)S(1)}, f32[45,256]{1,0:T(8,128)}, u32[]{:S(2)}) copy-start(f32[45,256]{1,0:T(8,128)} %kappa_ref.5) | copy-start | bytes 138244
  1.5 8.1 %copy-start.6 = (f32[1,12,45,256]{3,0,2,1:T(1,128)S(1)}, f32[1,12,45,256]{3,0,2,1:T(1,128)}, u32[]{:S(2)}) copy-start(f32[1,12,45,256]{3,0,2,1:T(1,128)} %param.9) | copy-start | bytes 1658884
  1.6 9.3 %collective-permute-start.5 = (bf16[540,256]{1,0:T(8,128)(2,1)S(1)}, bf16[540,256]{1,0:T(8,128)(2,1)S(1)}, u32[]{:S(2)}, u32[]{:S(2)}) collective-permute-start(bf16[540,256]{1,0:T(8,128)(2,1)S(1)} %get-tuple-element.32.short_ref), channel_id=1, source_target_pairs={{0,18},{1,19},{2,16},{3,17},{4,22},{5,23},{6,20},{7,21},{8,26},{9,... | collective-permute-start | bytes 829448 | tf_op jit(solution)/shard_map/ppermute | solution.py:41
  3.2 8.7 %collective-permute-start.2 = (bf16[540,256]{1,0:T(8,128)(2,1)S(1)}, bf16[540,256]{1,0:T(8,128)(2,1)S(1)}, u32[]{:S(2)}, u32[]{:S(2)}) collective-permute-start(bf16[540,256]{1,0:T(8,128)(2,1)S(1)} %get-tuple-element.32.short_ref), channel_id=1, source_target_pairs={{0,30},{1,31},{2,20},{3,21},{4,18},{5,19},{6,24},{7,25},{8,22},{9,... | collective-permute-start | bytes 829448 | tf_op jit(solution)/shard_map/ppermute | solution.py:41
  7.3 2.3 %copy-start.1 = (s32[2,256]{1,0:T(2,128)S(1)}, s32[2,256]{1,0:T(2,128)}, u32[]{:S(2)}) copy-start(s32[2,256]{1,0:T(2,128)} %mask_ref.3) | copy-start | bytes 6148
  7.3 2.3 %copy-start.2 = (s32[3,256]{1,0:T(4,128)S(1)}, s32[3,256]{1,0:T(4,128)}, u32[]{:S(2)}) copy-start(s32[3,256]{1,0:T(4,128)} %nbr_ref.1) | copy-start | bytes 9220
  7.3 2.3 %copy-start.3 = (f32[3,256]{1,0:T(4,128)S(1)}, f32[3,256]{1,0:T(4,128)}, u32[]{:S(2)}) copy-start(f32[3,256]{1,0:T(4,128)} %weight_ref.1) | copy-start | bytes 9220
  7.3 2.3 %copy-start.4 = (f32[12]{0:T(128)S(1)}, f32[12]{0:T(128)}, u32[]{:S(2)}) copy-start(f32[12]{0:T(128)} %relax_ref.1) | copy-start | bytes 148
  7.3 2.3 %copy-start.5 = (f32[12]{0:T(128)S(1)}, f32[12]{0:T(128)}, u32[]{:S(2)}) copy-start(f32[12]{0:T(128)} %diff_ref.1) | copy-start | bytes 148
  7.4 3.5 %collective-permute-start.4 = (bf16[5,45,256]{2,1,0:T(8,128)(2,1)S(1)}, bf16[5,45,256]{2,1,0:T(8,128)(2,1)S(1)}, u32[]{:S(2)}, u32[]{:S(2)}) collective-permute-start(bf16[5,45,256]{2,1,0:T(8,128)(2,1)S(1)} %shard_map.73), channel_id=1, source_target_pairs={{0,17},{1,16},{2,19},{3,18},{4,21},{5,20},{6,23},{7,22},{8,25},{9,... | collective-permute-start | bytes 345608 | tf_op jit(solution)/shard_map/ppermute | solution.py:41
  7.4 3.5 %collective-permute-start.1 = (bf16[90,256]{1,0:T(8,128)(2,1)S(1)}, bf16[90,256]{1,0:T(8,128)(2,1)S(1)}, u32[]{:S(2)}, u32[]{:S(2)}) collective-permute-start(bf16[90,256]{1,0:T(8,128)(2,1)S(1)} %get-tuple-element.31.head_ref), channel_id=1, source_target_pairs={{0,19},{1,18},{2,17},{3,16},{4,23},{5,22},{6,21},{7,20},{8,27},{9,... | collective-permute-start | bytes 138248 | tf_op jit(solution)/shard_map/ppermute | solution.py:41
  7.5 4.4 %collective-permute-start = (bf16[90,256]{1,0:T(8,128)(2,1)S(1)}, bf16[90,256]{1,0:T(8,128)(2,1)S(1)}, u32[]{:S(2)}, u32[]{:S(2)}) collective-permute-start(bf16[90,256]{1,0:T(8,128)(2,1)S(1)} %get-tuple-element.31.head_ref), channel_id=1, source_target_pairs={{0,31},{1,30},{2,21},{3,20},{4,19},{5,18},{6,25},{7,24},{8,23},{9,... | collective-permute-start | bytes 138248 | tf_op jit(solution)/shard_map/ppermute | solution.py:41
  11.9 8.5 %collective-permute-start.7 = (bf16[640,256]{1,0:T(8,128)(2,1)S(1)}, bf16[640,256]{1,0:T(8,128)(2,1)S(1)}, u32[]{:S(2)}, u32[]{:S(2)}) collective-permute-start(bf16[640,256]{1,0:T(8,128)(2,1)S(1)} %get-tuple-element.44.brief_ref), channel_id=1, source_target_pairs={{16,2},{17,3},{18,0},{19,1},{20,6},{21,7},{22,4},{23,5},{24,10},{2... | collective-permute-start | bytes 983048 | tf_op jit(solution)/shard_map/ppermute | solution.py:41
  13.2 10.9 %collective-permute-start.6 = (bf16[640,256]{1,0:T(8,128)(2,1)S(1)}, bf16[640,256]{1,0:T(8,128)(2,1)S(1)}, u32[]{:S(2)}, u32[]{:S(2)}) collective-permute-start(bf16[640,256]{1,0:T(8,128)(2,1)S(1)} %get-tuple-element.44.brief_ref), channel_id=1, source_target_pairs={{16,14},{17,15},{18,4},{19,5},{20,2},{21,3},{22,8},{23,9},{24,6},{... | collective-permute-start | bytes 983048 | tf_op jit(solution)/shard_map/ppermute | solution.py:41
  17.1 1.6 %collective-permute-start.8 = (f32[232,256]{1,0:T(8,128)S(1)}, f32[232,256]{1,0:T(8,128)S(1)}, u32[]{:S(2)}, u32[]{:S(2)}) collective-permute-start(f32[232,256]{1,0:T(8,128)S(1)} %get-tuple-element.45), channel_id=1, source_target_pairs={{16,0},{17,1},{18,2},{19,3},{20,4},{21,5},{22,6},{23,7},{24,8},{25... | collective-permute-start | bytes 712712 | tf_op jit(solution)/shard_map/ppermute | solution.py:41
  17.2 1.9 %collective-permute-start.9 = (f32[232,256]{1,0:T(8,128)S(1)}, f32[232,256]{1,0:T(8,128)S(1)}, u32[]{:S(2)}, u32[]{:S(2)}) collective-permute-start(f32[232,256]{1,0:T(8,128)S(1)} %get-tuple-element.46), channel_id=1, source_target_pairs={{16,0},{17,1},{18,2},{19,3},{20,4},{21,5},{22,6},{23,7},{24,8},{25... | collective-permute-start | bytes 712712 | tf_op jit(solution)/shard_map/ppermute | solution.py:41
  17.6 1.8 %collective-permute-start.10 = (f32[232,256]{1,0:T(8,128)S(1)}, f32[232,256]{1,0:T(8,128)S(1)}, u32[]{:S(2)}, u32[]{:S(2)}) collective-permute-start(f32[232,256]{1,0:T(8,128)S(1)} %get-tuple-element.47), channel_id=1, source_target_pairs={{16,0},{17,1},{18,2},{19,3},{20,4},{21,5},{22,6},{23,7},{24,8},{25... | collective-permute-start | bytes 712712 | tf_op jit(solution)/shard_map/ppermute | solution.py:41

commit v8 on v7

--- a/solution.py
+++ b/solution.py
@@ -361,8 +361,17 @@
             out_ref[rest, :] = start_ref[rest, :]
 
 
+def early_kernel(far_ref, start_ref, take_ref, gather_ref, value_ref):
+    own = far_ref.shape[0]
+    rows = slice(own - value_ref.shape[0], own)
+
+    @pl.when(lax.axis_index("sec") == 1)
+    def _():
+        value_ref[...] = start_ref[rows, :] + take_ref[rows, :] * side_share(far_ref[rows, :], gather_ref, 1)
+
+
 def first_kernel(
-    dfar_ref, dnear_ref, far_ref, pack_ref, start_ref, lagged_ref, take_ref, gather_ref, *rest
+    dfar_ref, dnear_ref, far_ref, early_ref, pack_ref, start_ref, lagged_ref, take_ref, gather_ref, *rest
 ):
     factors, (*full_refs, short_ref, smooth, columns) = rest[:6], rest[6:]
     _, half, width = pack_ref.shape
@@ -392,10 +401,8 @@
         smooth[rows, :] = start_ref[rows, :] + take_ref[rows, :] * side_share(far_ref[rows, :], gather_ref, 1)
         part = lambda low: [smooth[low + f * half : low + (f + 1) * half, :] for f in range(SOLVED)]
         mine, theirs = solve_rows(part(0), part(base), columns, factors)
-        rows = slice(first, own)
-        value = start_ref[rows, :] + take_ref[rows, :] * side_share(far_ref[rows, :], gather_ref, 1)
         for low, high in spans(first, own, CHUNK):
-            emit(low, value[low - first : high - first])
+            emit(low, early_ref[low - first : high - first, :])
         for f in range(SOLVED):
             smooth[f * half : (f + 1) * half, :] = mine[f]
             smooth[base + f * half : base + (f + 1) * half, :] = theirs[f] + pack_ref[SOLVED + f].astype(F32)
@@ -562,14 +569,23 @@
     start = with_near(1, near_rows, start)
 
     scratch = [pltpu.VMEM((total, width), F32), pltpu.VMEM((SOLVED, width // LANES, depth, LANES), F32)]
+    first = up(SOLVED * half, CHUNK)
+    early = pl.pallas_call(
+        early_kernel,
+        out_shape=shape((own - first, width), F32),
+        in_specs=[VMEM] * 4,
+        out_specs=VMEM,
+        compiler_params=params(8),
+        cost_estimate=cost(0),
+    )(far_rows, start, take, gather)
     *full, brief = pl.pallas_call(
         first_kernel,
         out_shape=[shape((piece, width), F32)] * PIECES + [shape((total, width), BF16)],
-        in_specs=[VMEM] * 14,
+        in_specs=[VMEM] * 15,
         out_specs=[VMEM] * (PIECES + 1),
         scratch_shapes=scratch,
         compiler_params=params(24),
-    )(dfar, dnear, far_rows, pack, start, lagged, take, gather, *factors)
+    )(dfar, dnear, far_rows, early, pack, start, lagged, take, gather, *factors)
 
     near_rows = route(brief, (1, 0, near, 0))
     far_rows = route(brief, (1, 0, far, 0), (0, 1, same, 0))

time: 25.5 us -> 25.4 us (level)
  transfers between devices with their start and end apart: 11 -> 11, of which waited for: 5 -> 6; matrix products, arithmetic and copies ran while one was open for 0% -> 0% of each run, Pallas kernels for 15% -> 15%
where the time goes in v8:
time: 25.4 us; the launch traced here: 25.3 us
  starting transfers between devices  14.1 us (56%)
  waiting for transfers between devices  6 us (24%)
  Pallas kernels  4.99 us (20%)
    ppermute x11, starting transfers between devices, route(): return lax.ppermute(array, AXES, table)  14.1 us
    ppermute x11, waiting for transfers between devices, route(): return lax.ppermute(array, AXES, table)  6 us
    pallas_call x1, Pallas kernels, shards(): pl.pallas_call(last_kernel, out_shape=shape(mine.shape, F32), in_specs=[V...  1.23 us
    pallas_call x1, Pallas kernels, shards(): pl.pallas_call(prepare_kernel, out_shape=[shape((7 * width, width), BF16)...  1.2 us
    pallas_call x1, Pallas kernels, shards(): lax.cond(lax.axis_index('sec') == 0, pl.pallas_call(shorten_kernel, out_s...  1.08 us
    pallas_call x2, Pallas kernels, ready(): pl.pallas_call(kernel, out_shape=[chunk] * 5 + [shape((6, SUB, width), F3...  1.08 us
  transfers between devices with their start and end apart: 11, of which 6 were waited for; matrix products, arithmetic and copies ran while one was open for 0% of the time, Pallas kernels for 15%

profile of v8, /device:TPU:0, one launch (start us, length us, event | category | flops | bytes accessed | tf_op | source)
XLA Modules:
  0.0 25.3 jit_solution(10609176294935204123)
XLA Ops:
  0.0 0.5 %collective-permute-start.4 = (f32[1080,128]{1,0:T(8,128)}, f32[1080,128]{1,0:T(8,128)S(1)}, u32[]{:S(2)}, u32[]{:S(2)}) collective-permute-start(f32[1080,128]{1,0:T(8,128)} %bitcast.2), channel_id=1, source_target_pairs={{0,16},{1,17},{2,18},{3,19},{4,20},{5,21},{6,22},{7,23},{8,24},{9,... | collective-permute-start | bytes 1658888 | tf_op jit(solution)/shard_map/ppermute | solution.py:41
  0.5 0.0 copy-start
  0.5 1.1 %conditional.1 = ((bf16[540,256]{1,0:T(8,128)(2,1)S(1)}, bf16[90,256]{1,0:T(8,128)(2,1)S(1)})) conditional(s32[]{:T(128)} %convert_element_type.3, () %tuple.11, f32[1080,128]{1,0:T(8,128)} %bitcast.3), branch_computations={%region_0.0_spmd, %region_1.0_spmd} | conditional | flops 3000000000 | bytes 8 | solution.py:489
  0.5 1.1 %branch_1_fun.1 = (bf16[540,256]{1,0:T(8,128)(2,1)S(1)}, bf16[90,256]{1,0:T(8,128)(2,1)S(1)}) custom-call(f32[1080,128]{1,0:T(8,128)} %mine_ref), custom_call_target="tpu_custom_call" | custom-call | flops 3000000000 | tf_op jit(solution)/shard_map/cond/branch_1_fun/pallas_call | solution.py:489
  1.5 0.0 copy-start.6
  1.6 1.6 %collective-permute-start.3 = (bf16[540,256]{1,0:T(8,128)(2,1)S(1)}, bf16[540,256]{1,0:T(8,128)(2,1)S(1)}, u32[]{:S(2)}, u32[]{:S(2)}) collective-permute-start(bf16[540,256]{1,0:T(8,128)(2,1)S(1)} %get-tuple-element.32.short_ref), channel_id=1, source_target_pairs={{0,18},{1,19},{2,16},{3,17},{4,22},{5,23},{6,20},{7,21},{8,26},{9,... | collective-permute-start | bytes 829448 | tf_op jit(solution)/shard_map/ppermute | solution.py:41
  3.2 4.1 %collective-permute-start.2 = (bf16[540,256]{1,0:T(8,128)(2,1)S(1)}, bf16[540,256]{1,0:T(8,128)(2,1)S(1)}, u32[]{:S(2)}, u32[]{:S(2)}) collective-permute-start(bf16[540,256]{1,0:T(8,128)(2,1)S(1)} %get-tuple-element.32.short_ref), channel_id=1, source_target_pairs={{0,30},{1,31},{2,20},{3,21},{4,18},{5,19},{6,24},{7,25},{8,22},{9,... | collective-permute-start | bytes 829448 | tf_op jit(solution)/shard_map/ppermute | solution.py:41
  7.3 0.0 collective-permute-done.4.other_ref.state_ref
  7.3 0.0 copy-done
  7.3 0.0 copy-start.1
  7.3 0.0 copy-start.2
  7.3 0.0 copy-start.3
  7.3 0.0 copy-start.4
  7.3 0.0 copy-start.5
  7.4 0.1 collective-permute-start.5
  7.4 0.1 collective-permute-start.1
  7.5 2.1 %collective-permute-start = (bf16[90,256]{1,0:T(8,128)(2,1)S(1)}, bf16[90,256]{1,0:T(8,128)(2,1)S(1)}, u32[]{:S(2)}, u32[]{:S(2)}) collective-permute-start(bf16[90,256]{1,0:T(8,128)(2,1)S(1)} %get-tuple-element.31.head_ref), channel_id=1, source_target_pairs={{0,31},{1,30},{2,21},{3,20},{4,19},{5,18},{6,25},{7,24},{8,23},{9,... | collective-permute-start | bytes 138248 | tf_op jit(solution)/shard_map/ppermute | solution.py:41
  9.6 0.0 copy-done.6
  9.6 0.0 copy-done.1
  9.6 0.0 copy-done.2
  9.6 0.0 copy-done.3
  9.6 0.0 copy-done.4
  9.6 0.0 copy-done.5
  9.6 1.2 %shard_map.74 = (bf16[1792,256]{1,0:T(8,128)(2,1)S(1)}, bf16[540,256]{1,0:T(8,128)(2,1)S(1)}, f32[12,256]{1,0:T(8,128)S(1)}, f32[640,256]{1,0:T(8,128)S(1)}, f32[640,256]{1,0:T(8,128)S(1)}) custom-call(f32[1080,128]{1,0:T(8,128)S(1)} %bitcast.4, bf16[540,256]{1,0:T(8,128)(2,1)S(1)} %get-tuple-element.32.short_ref, s32[3,256]{1,0:T(4,128)S(1)} %copy-done.2, ...), custom_call_target="tpu_custom_call" | custom-call | flops 10000000 | tf_op jit(solution)/shard_map/pallas_call | solution.py:522
  10.8 0.0 collective-permute-done.5.pack_ref
  10.9 0.0 collective-permute-done.3.near_ref
  10.9 0.4 %collective-permute-done.2.far_ref = bf16[540,256]{1,0:T(8,128)(2,1)S(1)} collective-permute-done((bf16[540,256]{1,0:T(8,128)(2,1)S(1)}, bf16[540,256]{1,0:T(8,128)(2,1)S(1)}, u32[]{:S(2)}, u32[]{:S(2)}) %collective-permute-start.2) | collective-permute-done | bytes 276512 | tf_op jit(solution)/shard_map/ppermute | solution.py:41
  11.4 0.0 collective-permute-done.1.dnear_ref
  11.4 0.5 %collective-permute-done.dfar_ref = bf16[90,256]{1,0:T(8,128)(2,1)S(1)} collective-permute-done((bf16[90,256]{1,0:T(8,128)(2,1)S(1)}, bf16[90,256]{1,0:T(8,128)(2,1)S(1)}, u32[]{:S(2)}, u32[]{:S(2)}) %collective-permute-start) | collective-permute-done | bytes 46112 | tf_op jit(solution)/shard_map/ppermute | solution.py:41
  11.9 1.3 %collective-permute-start.7 = (bf16[640,256]{1,0:T(8,128)(2,1)S(1)}, bf16[640,256]{1,0:T(8,128)(2,1)S(1)}, u32[]{:S(2)}, u32[]{:S(2)}) collective-permute-start(bf16[640,256]{1,0:T(8,128)(2,1)S(1)} %get-tuple-element.44.brief_ref), channel_id=1, source_target_pairs={{16,2},{17,3},{18,0},{19,1},{20,6},{21,7},{22,4},{23,5},{24,10},{2... | collective-permute-start | bytes 983048 | tf_op jit(solution)/shard_map/ppermute | solution.py:41
  13.2 3.8 %collective-permute-start.6 = (bf16[640,256]{1,0:T(8,128)(2,1)S(1)}, bf16[640,256]{1,0:T(8,128)(2,1)S(1)}, u32[]{:S(2)}, u32[]{:S(2)}) collective-permute-start(bf16[640,256]{1,0:T(8,128)(2,1)S(1)} %get-tuple-element.44.brief_ref), channel_id=1, source_target_pairs={{16,14},{17,15},{18,4},{19,5},{20,2},{21,3},{22,8},{23,9},{24,6},{... | collective-permute-start | bytes 983048 | tf_op jit(solution)/shard_map/ppermute | solution.py:41
  17.0 0.1 collective-permute-start.8
  17.1 0.4 %collective-permute-start.9 = (f32[232,256]{1,0:T(8,128)S(1)}, f32[232,256]{1,0:T(8,128)S(1)}, u32[]{:S(2)}, u32[]{:S(2)}) collective-permute-start(f32[232,256]{1,0:T(8,128)S(1)} %get-tuple-element.46), channel_id=1, source_target_pairs={{16,0},{17,1},{18,2},{19,3},{20,4},{21,5},{22,6},{23,7},{24,8},{25... | collective-permute-start | bytes 712712 | tf_op jit(solution)/shard_map/ppermute | solution.py:41
  17.5 0.1 collective-permute-start.10
  17.6 1.0 %collective-permute-done.8.rest_0_ = f32[232,256]{1,0:T(8,128)S(1)} collective-permute-done((f32[232,256]{1,0:T(8,128)S(1)}, f32[232,256]{1,0:T(8,128)S(1)}, u32[]{:S(2)}, u32[]{:S(2)}) %collective-permute-start.8) | collective-permute-done | bytes 237600 | tf_op jit(solution)/shard_map/ppermute | solution.py:41
  18.6 0.3 %collective-permute-done.9.rest_1_ = f32[232,256]{1,0:T(8,128)S(1)} collective-permute-done((f32[232,256]{1,0:T(8,128)S(1)}, f32[232,256]{1,0:T(8,128)S(1)}, u32[]{:S(2)}, u32[]{:S(2)}) %collective-permute-start.9) | collective-permute-done | bytes 237600 | tf_op jit(solution)/shard_map/ppermute | solution.py:41
  18.9 0.3 %collective-permute-done.10.rest_2_ = f32[232,256]{1,0:T(8,128)S(1)} collective-permute-done((f32[232,256]{1,0:T(8,128)S(1)}, f32[232,256]{1,0:T(8,128)S(1)}, u32[]{:S(2)}, u32[]{:S(2)}) %collective-permute-start.10) | collective-permute-done | bytes 237600 | tf_op jit(solution)/shard_map/ppermute | solution.py:41
  19.3 1.1 %shard_map.79 = (f32[12,8,256]{2,1,0:T(8,128)S(1)}, f32[12,8,256]{2,1,0:T(8,128)S(1)}, f32[12,8,256]{2,1,0:T(8,128)S(1)}, f32[12,8,256]{2,1,0:T(8,128)S(1)}, f32...) custom-call(f32[45,256]{1,0:T(8,128)S(1)} %copy-done, ...), custom_call_target="tpu_custom_call" | custom-call | tf_op jit(solution)/shard_map/pallas_call | solution.py:541
  20.3 0.0 collective-permute-done.7.near_ref
  20.3 0.4 %shard_map.80.start_ref = f32[640,256]{1,0:T(8,128)S(1)} custom-call(bf16[640,256]{1,0:T(8,128)(2,1)S(1)} %collective-permute-done.7.near_ref, f32[640,256]{1,0:T(8,128)S(1)} %get-tuple-element.48.start_ref, f32[640,256]{1,0:T(8,128)S(1)} %get-tuple-element.35.take_ref, bf16[1792,256]{1,0:T(8,128)(2,1)S(1)} %get-tuple-element.36.gather_ref), custom_call_target="tpu_custom_call" | custom-call | tf_op jit(solution)/shard_map/pallas_call | solution.py:558
  20.7 3.3 %collective-permute-done.6.far_ref = bf16[640,256]{1,0:T(8,128)(2,1)S(1)} collective-permute-done((bf16[640,256]{1,0:T(8,128)(2,1)S(1)}, bf16[640,256]{1,0:T(8,128)(2,1)S(1)}, u32[]{:S(2)}, u32[]{:S(2)}) %collective-permute-start.6) | collective-permute-done | bytes 327712 | tf_op jit(solution)/shard_map/ppermute | solution.py:41
  24.0 1.2 %shard_map.81 = f32[1080,128]{1,0:T(8,128)} custom-call(bf16[640,256]{1,0:T(8,128)(2,1)S(1)} %collective-permute-done.6.far_ref, bf16[640,256]{1,0:T(8,128)(2,1)S(1)} %get-tuple-element.44.brief_ref, f32[640,256]{1,0:T(8,128)S(1)} %shard_map.80.start_ref, bf16[540,256]{1,0:T(8,128)(2,1)S(1)} %get-tuple-element.33.lagged_ref, s32[2,256]{1,0:T(2,128)S(1)} %copy-done.1, ...), custom_call_target="tpu_custom_call" | custom-call | tf_op jit(solution)/shard_map/pallas_call | solution.py:597
  (5 shorter events, 0.1 us)
Async XLA Ops:
  0.0 7.3 %collective-permute-start.4 = (f32[1080,128]{1,0:T(8,128)}, f32[1080,128]{1,0:T(8,128)S(1)}, u32[]{:S(2)}, u32[]{:S(2)}) collective-permute-start(f32[1080,128]{1,0:T(8,128)} %bitcast.2), channel_id=1, source_target_pairs={{0,16},{1,17},{2,18},{3,19},{4,20},{5,21},{6,22},{7,23},{8,24},{9,... | collective-permute-start | bytes 1658888 | tf_op jit(solution)/shard_map/ppermute | solution.py:41
  0.5 6.8 %copy-start = (f32[45,256]{1,0:T(8,128)S(1)}, f32[45,256]{1,0:T(8,128)}, u32[]{:S(2)}) copy-start(f32[45,256]{1,0:T(8,128)} %kappa_ref.5) | copy-start | bytes 138244
  1.5 8.1 %copy-start.6 = (f32[1,12,45,256]{3,0,2,1:T(1,128)S(1)}, f32[1,12,45,256]{3,0,2,1:T(1,128)}, u32[]{:S(2)}) copy-start(f32[1,12,45,256]{3,0,2,1:T(1,128)} %param.9) | copy-start | bytes 1658884
  1.6 9.3 %collective-permute-start.3 = (bf16[540,256]{1,0:T(8,128)(2,1)S(1)}, bf16[540,256]{1,0:T(8,128)(2,1)S(1)}, u32[]{:S(2)}, u32[]{:S(2)}) collective-permute-start(bf16[540,256]{1,0:T(8,128)(2,1)S(1)} %get-tuple-element.32.short_ref), channel_id=1, source_target_pairs={{0,18},{1,19},{2,16},{3,17},{4,22},{5,23},{6,20},{7,21},{8,26},{9,... | collective-permute-start | bytes 829448 | tf_op jit(solution)/shard_map/ppermute | solution.py:41
  3.2 8.2 %collective-permute-start.2 = (bf16[540,256]{1,0:T(8,128)(2,1)S(1)}, bf16[540,256]{1,0:T(8,128)(2,1)S(1)}, u32[]{:S(2)}, u32[]{:S(2)}) collective-permute-start(bf16[540,256]{1,0:T(8,128)(2,1)S(1)} %get-tuple-element.32.short_ref), channel_id=1, source_target_pairs={{0,30},{1,31},{2,20},{3,21},{4,18},{5,19},{6,24},{7,25},{8,22},{9,... | collective-permute-start | bytes 829448 | tf_op jit(solution)/shard_map/ppermute | solution.py:41
  7.3 2.3 %copy-start.1 = (s32[2,256]{1,0:T(2,128)S(1)}, s32[2,256]{1,0:T(2,128)}, u32[]{:S(2)}) copy-start(s32[2,256]{1,0:T(2,128)} %mask_ref.3) | copy-start | bytes 6148
  7.3 2.3 %copy-start.2 = (s32[3,256]{1,0:T(4,128)S(1)}, s32[3,256]{1,0:T(4,128)}, u32[]{:S(2)}) copy-start(s32[3,256]{1,0:T(4,128)} %nbr_ref.1) | copy-start | bytes 9220
  7.3 2.3 %copy-start.3 = (f32[3,256]{1,0:T(4,128)S(1)}, f32[3,256]{1,0:T(4,128)}, u32[]{:S(2)}) copy-start(f32[3,256]{1,0:T(4,128)} %weight_ref.1) | copy-start | bytes 9220
  7.3 2.3 %copy-start.4 = (f32[12]{0:T(128)S(1)}, f32[12]{0:T(128)}, u32[]{:S(2)}) copy-start(f32[12]{0:T(128)} %relax_ref.1) | copy-start | bytes 148
  7.3 2.3 %copy-start.5 = (f32[12]{0:T(128)S(1)}, f32[12]{0:T(128)}, u32[]{:S(2)}) copy-start(f32[12]{0:T(128)} %diff_ref.1) | copy-start | bytes 148
  7.4 3.5 %collective-permute-start.5 = (bf16[5,45,256]{2,1,0:T(8,128)(2,1)S(1)}, bf16[5,45,256]{2,1,0:T(8,128)(2,1)S(1)}, u32[]{:S(2)}, u32[]{:S(2)}) collective-permute-start(bf16[5,45,256]{2,1,0:T(8,128)(2,1)S(1)} %shard_map.73), channel_id=1, source_target_pairs={{0,17},{1,16},{2,19},{3,18},{4,21},{5,20},{6,23},{7,22},{8,25},{9,... | collective-permute-start | bytes 345608 | tf_op jit(solution)/shard_map/ppermute | solution.py:41
  7.4 3.9 %collective-permute-start.1 = (bf16[90,256]{1,0:T(8,128)(2,1)S(1)}, bf16[90,256]{1,0:T(8,128)(2,1)S(1)}, u32[]{:S(2)}, u32[]{:S(2)}) collective-permute-start(bf16[90,256]{1,0:T(8,128)(2,1)S(1)} %get-tuple-element.31.head_ref), channel_id=1, source_target_pairs={{0,19},{1,18},{2,17},{3,16},{4,23},{5,22},{6,21},{7,20},{8,27},{9,... | collective-permute-start | bytes 138248 | tf_op jit(solution)/shard_map/ppermute | solution.py:41
  7.5 4.4 %collective-permute-start = (bf16[90,256]{1,0:T(8,128)(2,1)S(1)}, bf16[90,256]{1,0:T(8,128)(2,1)S(1)}, u32[]{:S(2)}, u32[]{:S(2)}) collective-permute-start(bf16[90,256]{1,0:T(8,128)(2,1)S(1)} %get-tuple-element.31.head_ref), channel_id=1, source_target_pairs={{0,31},{1,30},{2,21},{3,20},{4,19},{5,18},{6,25},{7,24},{8,23},{9,... | collective-permute-start | bytes 138248 | tf_op jit(solution)/shard_map/ppermute | solution.py:41
  11.9 8.4 %collective-permute-start.7 = (bf16[640,256]{1,0:T(8,128)(2,1)S(1)}, bf16[640,256]{1,0:T(8,128)(2,1)S(1)}, u32[]{:S(2)}, u32[]{:S(2)}) collective-permute-start(bf16[640,256]{1,0:T(8,128)(2,1)S(1)} %get-tuple-element.44.brief_ref), channel_id=1, source_target_pairs={{16,2},{17,3},{18,0},{19,1},{20,6},{21,7},{22,4},{23,5},{24,10},{2... | collective-permute-start | bytes 983048 | tf_op jit(solution)/shard_map/ppermute | solution.py:41
  13.2 10.9 %collective-permute-start.6 = (bf16[640,256]{1,0:T(8,128)(2,1)S(1)}, bf16[640,256]{1,0:T(8,128)(2,1)S(1)}, u32[]{:S(2)}, u32[]{:S(2)}) collective-permute-start(bf16[640,256]{1,0:T(8,128)(2,1)S(1)} %get-tuple-element.44.brief_ref), channel_id=1, source_target_pairs={{16,14},{17,15},{18,4},{19,5},{20,2},{21,3},{22,8},{23,9},{24,6},{... | collective-permute-start | bytes 983048 | tf_op jit(solution)/shard_map/ppermute | solution.py:41
  17.0 1.6 %collective-permute-start.8 = (f32[232,256]{1,0:T(8,128)S(1)}, f32[232,256]{1,0:T(8,128)S(1)}, u32[]{:S(2)}, u32[]{:S(2)}) collective-permute-start(f32[232,256]{1,0:T(8,128)S(1)} %get-tuple-element.45), channel_id=1, source_target_pairs={{16,0},{17,1},{18,2},{19,3},{20,4},{21,5},{22,6},{23,7},{24,8},{25... | collective-permute-start | bytes 712712 | tf_op jit(solution)/shard_map/ppermute | solution.py:41
  17.1 1.9 %collective-permute-start.9 = (f32[232,256]{1,0:T(8,128)S(1)}, f32[232,256]{1,0:T(8,128)S(1)}, u32[]{:S(2)}, u32[]{:S(2)}) collective-permute-start(f32[232,256]{1,0:T(8,128)S(1)} %get-tuple-element.46), channel_id=1, source_target_pairs={{16,0},{17,1},{18,2},{19,3},{20,4},{21,5},{22,6},{23,7},{24,8},{25... | collective-permute-start | bytes 712712 | tf_op jit(solution)/shard_map/ppermute | solution.py:41
  17.5 1.8 %collective-permute-start.10 = (f32[232,256]{1,0:T(8,128)S(1)}, f32[232,256]{1,0:T(8,128)S(1)}, u32[]{:S(2)}, u32[]{:S(2)}) collective-permute-start(f32[232,256]{1,0:T(8,128)S(1)} %get-tuple-element.47), channel_id=1, source_target_pairs={{16,0},{17,1},{18,2},{19,3},{20,4},{21,5},{22,6},{23,7},{24,8},{25... | collective-permute-start | bytes 712712 | tf_op jit(solution)/shard_map/ppermute | solution.py:41

commit v9 on v8

--- a/solution.py
+++ b/solution.py
@@ -362,16 +362,15 @@
 
 
 def early_kernel(far_ref, start_ref, take_ref, gather_ref, value_ref):
-    own = far_ref.shape[0]
-    rows = slice(own - value_ref.shape[0], own)
+    rows = slice(0, far_ref.shape[0])
 
     @pl.when(lax.axis_index("sec") == 1)
     def _():
-        value_ref[...] = start_ref[rows, :] + take_ref[rows, :] * side_share(far_ref[rows, :], gather_ref, 1)
+        value_ref[...] = start_ref[rows, :] + take_ref[rows, :] * side_share(far_ref[...], gather_ref, 1)
 
 
 def first_kernel(
-    dfar_ref, dnear_ref, far_ref, early_ref, pack_ref, start_ref, lagged_ref, take_ref, gather_ref, *rest
+    dfar_ref, dnear_ref, early_ref, pack_ref, start_ref, lagged_ref, take_ref, gather_ref, *rest
 ):
     factors, (*full_refs, short_ref, smooth, columns) = rest[:6], rest[6:]
     _, half, width = pack_ref.shape
@@ -397,12 +396,11 @@
         smooth[others, :] = start_ref[others, :] + take_ref[others, :] * sides_share(
             dnear_ref[...], dfar_ref[...], gather_ref
         )
-        rows = slice(0, first)
-        smooth[rows, :] = start_ref[rows, :] + take_ref[rows, :] * side_share(far_ref[rows, :], gather_ref, 1)
+        smooth[0:first, :] = early_ref[0:first, :]
         part = lambda low: [smooth[low + f * half : low + (f + 1) * half, :] for f in range(SOLVED)]
         mine, theirs = solve_rows(part(0), part(base), columns, factors)
         for low, high in spans(first, own, CHUNK):
-            emit(low, early_ref[low - first : high - first, :])
+            emit(low, early_ref[low:high, :])
         for f in range(SOLVED):
             smooth[f * half : (f + 1) * half, :] = mine[f]
             smooth[base + f * half : base + (f + 1) * half, :] = theirs[f] + pack_ref[SOLVED + f].astype(F32)
@@ -569,10 +567,9 @@
     start = with_near(1, near_rows, start)
 
     scratch = [pltpu.VMEM((total, width), F32), pltpu.VMEM((SOLVED, width // LANES, depth, LANES), F32)]
-    first = up(SOLVED * half, CHUNK)
     early = pl.pallas_call(
         early_kernel,
-        out_shape=shape((own - first, width), F32),
+        out_shape=shape((own, width), F32),
         in_specs=[VMEM] * 4,
         out_specs=VMEM,
         compiler_params=params(8),
@@ -581,11 +578,11 @@
     *full, brief = pl.pallas_call(
         first_kernel,
         out_shape=[shape((piece, width), F32)] * PIECES + [shape((total, width), BF16)],
-        in_specs=[VMEM] * 15,
+        in_specs=[VMEM] * 14,
         out_specs=[VMEM] * (PIECES + 1),
         scratch_shapes=scratch,
         compiler_params=params(24),
-    )(dfar, dnear, far_rows, early, pack, start, lagged, take, gather, *factors)
+    )(dfar, dnear, early, pack, start, lagged, take, gather, *factors)
 
     near_rows = route(brief, (1, 0, near, 0))
     far_rows = route(brief, (1, 0, far, 0), (0, 1, same, 0))

time: 25.4 us -> 25.4 us (level)
  no operation moved by 1% of the time
where the time goes in v9:
time: 25.4 us; the launch traced here: 25.2 us
  starting transfers between devices  14 us (55%)
  waiting for transfers between devices  6.01 us (24%)
  Pallas kernels  4.99 us (20%)
    ppermute x11, starting transfers between devices, route(): return lax.ppermute(array, AXES, table)  14 us
    ppermute x11, waiting for transfers between devices, route(): return lax.ppermute(array, AXES, table)  6.01 us
    pallas_call x1, Pallas kernels, shards(): pl.pallas_call(last_kernel, out_shape=shape(mine.shape, F32), in_specs=[V...  1.23 us
    pallas_call x1, Pallas kernels, shards(): pl.pallas_call(prepare_kernel, out_shape=[shape((7 * width, width), BF16)...  1.2 us
    pallas_call x1, Pallas kernels, shards(): lax.cond(lax.axis_index('sec') == 0, pl.pallas_call(shorten_kernel, out_s...  1.08 us
    pallas_call x2, Pallas kernels, ready(): pl.pallas_call(kernel, out_shape=[chunk] * 5 + [shape((6, SUB, width), F3...  1.08 us
  transfers between devices with their start and end apart: 11, of which 6 were waited for; matrix products, arithmetic and copies ran while one was open for 0% of the time, Pallas kernels for 15%

profile of v9, /device:TPU:0, one launch (start us, length us, event | category | flops | bytes accessed | tf_op | source)
XLA Modules:
  0.0 25.2 jit_solution(312343923705690438)
XLA Ops:
  0.0 0.5 %collective-permute-start.4 = (f32[1080,128]{1,0:T(8,128)}, f32[1080,128]{1,0:T(8,128)S(1)}, u32[]{:S(2)}, u32[]{:S(2)}) collective-permute-start(f32[1080,128]{1,0:T(8,128)} %bitcast.2), channel_id=1, source_target_pairs={{0,16},{1,17},{2,18},{3,19},{4,20},{5,21},{6,22},{7,23},{8,24},{9,... | collective-permute-start | bytes 1658888 | tf_op jit(solution)/shard_map/ppermute | solution.py:41
  0.5 0.0 copy-start
  0.5 1.1 %conditional.1 = ((bf16[540,256]{1,0:T(8,128)(2,1)S(1)}, bf16[90,256]{1,0:T(8,128)(2,1)S(1)})) conditional(s32[]{:T(128)} %convert_element_type.3, () %tuple.11, f32[1080,128]{1,0:T(8,128)} %bitcast.3), branch_computations={%region_0.0_spmd, %region_1.0_spmd} | conditional | flops 3000000000 | bytes 8 | solution.py:487
  0.5 1.1 %branch_1_fun.1 = (bf16[540,256]{1,0:T(8,128)(2,1)S(1)}, bf16[90,256]{1,0:T(8,128)(2,1)S(1)}) custom-call(f32[1080,128]{1,0:T(8,128)} %mine_ref), custom_call_target="tpu_custom_call" | custom-call | flops 3000000000 | tf_op jit(solution)/shard_map/cond/branch_1_fun/pallas_call | solution.py:487
  1.5 0.0 copy-start.6
  1.6 1.6 %collective-permute-start.3 = (bf16[540,256]{1,0:T(8,128)(2,1)S(1)}, bf16[540,256]{1,0:T(8,128)(2,1)S(1)}, u32[]{:S(2)}, u32[]{:S(2)}) collective-permute-start(bf16[540,256]{1,0:T(8,128)(2,1)S(1)} %get-tuple-element.32.short_ref), channel_id=1, source_target_pairs={{0,18},{1,19},{2,16},{3,17},{4,22},{5,23},{6,20},{7,21},{8,26},{9,... | collective-permute-start | bytes 829448 | tf_op jit(solution)/shard_map/ppermute | solution.py:41
  3.2 4.1 %collective-permute-start.2 = (bf16[540,256]{1,0:T(8,128)(2,1)S(1)}, bf16[540,256]{1,0:T(8,128)(2,1)S(1)}, u32[]{:S(2)}, u32[]{:S(2)}) collective-permute-start(bf16[540,256]{1,0:T(8,128)(2,1)S(1)} %get-tuple-element.32.short_ref), channel_id=1, source_target_pairs={{0,30},{1,31},{2,20},{3,21},{4,18},{5,19},{6,24},{7,25},{8,22},{9,... | collective-permute-start | bytes 829448 | tf_op jit(solution)/shard_map/ppermute | solution.py:41
  7.3 0.0 collective-permute-done.4.other_ref.state_ref
  7.3 0.0 copy-done
  7.3 0.0 copy-start.1
  7.3 0.0 copy-start.2
  7.3 0.0 copy-start.3
  7.3 0.0 copy-start.4
  7.3 0.0 copy-start.5
  7.4 0.1 collective-permute-start.5
  7.4 0.1 collective-permute-start.1
  7.5 2.1 %collective-permute-start = (bf16[90,256]{1,0:T(8,128)(2,1)S(1)}, bf16[90,256]{1,0:T(8,128)(2,1)S(1)}, u32[]{:S(2)}, u32[]{:S(2)}) collective-permute-start(bf16[90,256]{1,0:T(8,128)(2,1)S(1)} %get-tuple-element.31.head_ref), channel_id=1, source_target_pairs={{0,31},{1,30},{2,21},{3,20},{4,19},{5,18},{6,25},{7,24},{8,23},{9,... | collective-permute-start | bytes 138248 | tf_op jit(solution)/shard_map/ppermute | solution.py:41
  9.6 0.0 copy-done.6
  9.6 0.0 copy-done.1
  9.6 0.0 copy-done.2
  9.6 0.0 copy-done.3
  9.6 0.0 copy-done.4
  9.6 0.0 copy-done.5
  9.6 1.2 %shard_map.74 = (bf16[1792,256]{1,0:T(8,128)(2,1)S(1)}, bf16[540,256]{1,0:T(8,128)(2,1)S(1)}, f32[12,256]{1,0:T(8,128)S(1)}, f32[640,256]{1,0:T(8,128)S(1)}, f32[640,256]{1,0:T(8,128)S(1)}) custom-call(f32[1080,128]{1,0:T(8,128)S(1)} %bitcast.4, bf16[540,256]{1,0:T(8,128)(2,1)S(1)} %get-tuple-element.32.short_ref, s32[3,256]{1,0:T(4,128)S(1)} %copy-done.2, ...), custom_call_target="tpu_custom_call" | custom-call | flops 10000000 | tf_op jit(solution)/shard_map/pallas_call | solution.py:520
  10.8 0.0 collective-permute-done.5.pack_ref
  10.9 0.0 collective-permute-done.3.near_ref
  10.9 0.4 %collective-permute-done.2.far_ref = bf16[540,256]{1,0:T(8,128)(2,1)S(1)} collective-permute-done((bf16[540,256]{1,0:T(8,128)(2,1)S(1)}, bf16[540,256]{1,0:T(8,128)(2,1)S(1)}, u32[]{:S(2)}, u32[]{:S(2)}) %collective-permute-start.2) | collective-permute-done | bytes 276512 | tf_op jit(solution)/shard_map/ppermute | solution.py:41
  11.4 0.0 collective-permute-done.1.dnear_ref
  11.4 0.5 %collective-permute-done.dfar_ref = bf16[90,256]{1,0:T(8,128)(2,1)S(1)} collective-permute-done((bf16[90,256]{1,0:T(8,128)(2,1)S(1)}, bf16[90,256]{1,0:T(8,128)(2,1)S(1)}, u32[]{:S(2)}, u32[]{:S(2)}) %collective-permute-start) | collective-permute-done | bytes 46112 | tf_op jit(solution)/shard_map/ppermute | solution.py:41
  11.9 1.3 %collective-permute-start.7 = (bf16[640,256]{1,0:T(8,128)(2,1)S(1)}, bf16[640,256]{1,0:T(8,128)(2,1)S(1)}, u32[]{:S(2)}, u32[]{:S(2)}) collective-permute-start(bf16[640,256]{1,0:T(8,128)(2,1)S(1)} %get-tuple-element.44.brief_ref), channel_id=1, source_target_pairs={{16,2},{17,3},{18,0},{19,1},{20,6},{21,7},{22,4},{23,5},{24,10},{2... | collective-permute-start | bytes 983048 | tf_op jit(solution)/shard_map/ppermute | solution.py:41
  13.2 3.8 %collective-permute-start.6 = (bf16[640,256]{1,0:T(8,128)(2,1)S(1)}, bf16[640,256]{1,0:T(8,128)(2,1)S(1)}, u32[]{:S(2)}, u32[]{:S(2)}) collective-permute-start(bf16[640,256]{1,0:T(8,128)(2,1)S(1)} %get-tuple-element.44.brief_ref), channel_id=1, source_target_pairs={{16,14},{17,15},{18,4},{19,5},{20,2},{21,3},{22,8},{23,9},{24,6},{... | collective-permute-start | bytes 983048 | tf_op jit(solution)/shard_map/ppermute | solution.py:41
  16.9 0.1 collective-permute-start.8
  17.0 0.4 %collective-permute-start.9 = (f32[232,256]{1,0:T(8,128)S(1)}, f32[232,256]{1,0:T(8,128)S(1)}, u32[]{:S(2)}, u32[]{:S(2)}) collective-permute-start(f32[232,256]{1,0:T(8,128)S(1)} %get-tuple-element.46), channel_id=1, source_target_pairs={{16,0},{17,1},{18,2},{19,3},{20,4},{21,5},{22,6},{23,7},{24,8},{25... | collective-permute-start | bytes 712712 | tf_op jit(solution)/shard_map/ppermute | solution.py:41
  17.4 0.1 collective-permute-start.10
  17.5 1.0 %collective-permute-done.8.rest_0_ = f32[232,256]{1,0:T(8,128)S(1)} collective-permute-done((f32[232,256]{1,0:T(8,128)S(1)}, f32[232,256]{1,0:T(8,128)S(1)}, u32[]{:S(2)}, u32[]{:S(2)}) %collective-permute-start.8) | collective-permute-done | bytes 237600 | tf_op jit(solution)/shard_map/ppermute | solution.py:41
  18.5 0.3 %collective-permute-done.9.rest_1_ = f32[232,256]{1,0:T(8,128)S(1)} collective-permute-done((f32[232,256]{1,0:T(8,128)S(1)}, f32[232,256]{1,0:T(8,128)S(1)}, u32[]{:S(2)}, u32[]{:S(2)}) %collective-permute-start.9) | collective-permute-done | bytes 237600 | tf_op jit(solution)/shard_map/ppermute | solution.py:41
  18.9 0.3 %collective-permute-done.10.rest_2_ = f32[232,256]{1,0:T(8,128)S(1)} collective-permute-done((f32[232,256]{1,0:T(8,128)S(1)}, f32[232,256]{1,0:T(8,128)S(1)}, u32[]{:S(2)}, u32[]{:S(2)}) %collective-permute-start.10) | collective-permute-done | bytes 237600 | tf_op jit(solution)/shard_map/ppermute | solution.py:41
  19.2 1.1 %shard_map.79 = (f32[12,8,256]{2,1,0:T(8,128)S(1)}, f32[12,8,256]{2,1,0:T(8,128)S(1)}, f32[12,8,256]{2,1,0:T(8,128)S(1)}, f32[12,8,256]{2,1,0:T(8,128)S(1)}, f32...) custom-call(f32[45,256]{1,0:T(8,128)S(1)} %copy-done, ...), custom_call_target="tpu_custom_call" | custom-call | tf_op jit(solution)/shard_map/pallas_call | solution.py:539
  20.3 0.0 collective-permute-done.7.near_ref
  20.3 0.3 %shard_map.80.start_ref = f32[640,256]{1,0:T(8,128)S(1)} custom-call(bf16[640,256]{1,0:T(8,128)(2,1)S(1)} %collective-permute-done.7.near_ref, f32[640,256]{1,0:T(8,128)S(1)} %get-tuple-element.48.start_ref, f32[640,256]{1,0:T(8,128)S(1)} %get-tuple-element.35.take_ref, bf16[1792,256]{1,0:T(8,128)(2,1)S(1)} %get-tuple-element.36.gather_ref), custom_call_target="tpu_custom_call" | custom-call | tf_op jit(solution)/shard_map/pallas_call | solution.py:556
  20.6 3.3 %collective-permute-done.6.far_ref = bf16[640,256]{1,0:T(8,128)(2,1)S(1)} collective-permute-done((bf16[640,256]{1,0:T(8,128)(2,1)S(1)}, bf16[640,256]{1,0:T(8,128)(2,1)S(1)}, u32[]{:S(2)}, u32[]{:S(2)}) %collective-permute-start.6) | collective-permute-done | bytes 327712 | tf_op jit(solution)/shard_map/ppermute | solution.py:41
  24.0 1.2 %shard_map.81 = f32[1080,128]{1,0:T(8,128)} custom-call(bf16[640,256]{1,0:T(8,128)(2,1)S(1)} %collective-permute-done.6.far_ref, bf16[640,256]{1,0:T(8,128)(2,1)S(1)} %get-tuple-element.44.brief_ref, f32[640,256]{1,0:T(8,128)S(1)} %shard_map.80.start_ref, bf16[540,256]{1,0:T(8,128)(2,1)S(1)} %get-tuple-element.33.lagged_ref, s32[2,256]{1,0:T(2,128)S(1)} %copy-done.1, ...), custom_call_target="tpu_custom_call" | custom-call | tf_op jit(solution)/shard_map/pallas_call | solution.py:594
  (5 shorter events, 0.1 us)
Async XLA Ops:
  0.0 7.3 %collective-permute-start.4 = (f32[1080,128]{1,0:T(8,128)}, f32[1080,128]{1,0:T(8,128)S(1)}, u32[]{:S(2)}, u32[]{:S(2)}) collective-permute-start(f32[1080,128]{1,0:T(8,128)} %bitcast.2), channel_id=1, source_target_pairs={{0,16},{1,17},{2,18},{3,19},{4,20},{5,21},{6,22},{7,23},{8,24},{9,... | collective-permute-start | bytes 1658888 | tf_op jit(solution)/shard_map/ppermute | solution.py:41
  0.5 6.8 %copy-start = (f32[45,256]{1,0:T(8,128)S(1)}, f32[45,256]{1,0:T(8,128)}, u32[]{:S(2)}) copy-start(f32[45,256]{1,0:T(8,128)} %kappa_ref.5) | copy-start | bytes 138244
  1.5 8.1 %copy-start.6 = (f32[1,12,45,256]{3,0,2,1:T(1,128)S(1)}, f32[1,12,45,256]{3,0,2,1:T(1,128)}, u32[]{:S(2)}) copy-start(f32[1,12,45,256]{3,0,2,1:T(1,128)} %param.9) | copy-start | bytes 1658884
  1.6 9.3 %collective-permute-start.3 = (bf16[540,256]{1,0:T(8,128)(2,1)S(1)}, bf16[540,256]{1,0:T(8,128)(2,1)S(1)}, u32[]{:S(2)}, u32[]{:S(2)}) collective-permute-start(bf16[540,256]{1,0:T(8,128)(2,1)S(1)} %get-tuple-element.32.short_ref), channel_id=1, source_target_pairs={{0,18},{1,19},{2,16},{3,17},{4,22},{5,23},{6,20},{7,21},{8,26},{9,... | collective-permute-start | bytes 829448 | tf_op jit(solution)/shard_map/ppermute | solution.py:41
  3.2 8.2 %collective-permute-start.2 = (bf16[540,256]{1,0:T(8,128)(2,1)S(1)}, bf16[540,256]{1,0:T(8,128)(2,1)S(1)}, u32[]{:S(2)}, u32[]{:S(2)}) collective-permute-start(bf16[540,256]{1,0:T(8,128)(2,1)S(1)} %get-tuple-element.32.short_ref), channel_id=1, source_target_pairs={{0,30},{1,31},{2,20},{3,21},{4,18},{5,19},{6,24},{7,25},{8,22},{9,... | collective-permute-start | bytes 829448 | tf_op jit(solution)/shard_map/ppermute | solution.py:41
  7.3 2.3 %copy-start.1 = (s32[2,256]{1,0:T(2,128)S(1)}, s32[2,256]{1,0:T(2,128)}, u32[]{:S(2)}) copy-start(s32[2,256]{1,0:T(2,128)} %mask_ref.3) | copy-start | bytes 6148
  7.3 2.3 %copy-start.2 = (s32[3,256]{1,0:T(4,128)S(1)}, s32[3,256]{1,0:T(4,128)}, u32[]{:S(2)}) copy-start(s32[3,256]{1,0:T(4,128)} %nbr_ref.1) | copy-start | bytes 9220
  7.3 2.3 %copy-start.3 = (f32[3,256]{1,0:T(4,128)S(1)}, f32[3,256]{1,0:T(4,128)}, u32[]{:S(2)}) copy-start(f32[3,256]{1,0:T(4,128)} %weight_ref.1) | copy-start | bytes 9220
  7.3 2.3 %copy-start.4 = (f32[12]{0:T(128)S(1)}, f32[12]{0:T(128)}, u32[]{:S(2)}) copy-start(f32[12]{0:T(128)} %relax_ref.1) | copy-start | bytes 148
  7.3 2.3 %copy-start.5 = (f32[12]{0:T(128)S(1)}, f32[12]{0:T(128)}, u32[]{:S(2)}) copy-start(f32[12]{0:T(128)} %diff_ref.1) | copy-start | bytes 148
  7.4 3.5 %collective-permute-start.5 = (bf16[5,45,256]{2,1,0:T(8,128)(2,1)S(1)}, bf16[5,45,256]{2,1,0:T(8,128)(2,1)S(1)}, u32[]{:S(2)}, u32[]{:S(2)}) collective-permute-start(bf16[5,45,256]{2,1,0:T(8,128)(2,1)S(1)} %shard_map.73), channel_id=1, source_target_pairs={{0,17},{1,16},{2,19},{3,18},{4,21},{5,20},{6,23},{7,22},{8,25},{9,... | collective-permute-start | bytes 345608 | tf_op jit(solution)/shard_map/ppermute | solution.py:41
  7.4 3.9 %collective-permute-start.1 = (bf16[90,256]{1,0:T(8,128)(2,1)S(1)}, bf16[90,256]{1,0:T(8,128)(2,1)S(1)}, u32[]{:S(2)}, u32[]{:S(2)}) collective-permute-start(bf16[90,256]{1,0:T(8,128)(2,1)S(1)} %get-tuple-element.31.head_ref), channel_id=1, source_target_pairs={{0,19},{1,18},{2,17},{3,16},{4,23},{5,22},{6,21},{7,20},{8,27},{9,... | collective-permute-start | bytes 138248 | tf_op jit(solution)/shard_map/ppermute | solution.py:41
  7.5 4.4 %collective-permute-start = (bf16[90,256]{1,0:T(8,128)(2,1)S(1)}, bf16[90,256]{1,0:T(8,128)(2,1)S(1)}, u32[]{:S(2)}, u32[]{:S(2)}) collective-permute-start(bf16[90,256]{1,0:T(8,128)(2,1)S(1)} %get-tuple-element.31.head_ref), channel_id=1, source_target_pairs={{0,31},{1,30},{2,21},{3,20},{4,19},{5,18},{6,25},{7,24},{8,23},{9,... | collective-permute-start | bytes 138248 | tf_op jit(solution)/shard_map/ppermute | solution.py:41
  11.9 8.4 %collective-permute-start.7 = (bf16[640,256]{1,0:T(8,128)(2,1)S(1)}, bf16[640,256]{1,0:T(8,128)(2,1)S(1)}, u32[]{:S(2)}, u32[]{:S(2)}) collective-permute-start(bf16[640,256]{1,0:T(8,128)(2,1)S(1)} %get-tuple-element.44.brief_ref), channel_id=1, source_target_pairs={{16,2},{17,3},{18,0},{19,1},{20,6},{21,7},{22,4},{23,5},{24,10},{2... | collective-permute-start | bytes 983048 | tf_op jit(solution)/shard_map/ppermute | solution.py:41
  13.2 10.8 %collective-permute-start.6 = (bf16[640,256]{1,0:T(8,128)(2,1)S(1)}, bf16[640,256]{1,0:T(8,128)(2,1)S(1)}, u32[]{:S(2)}, u32[]{:S(2)}) collective-permute-start(bf16[640,256]{1,0:T(8,128)(2,1)S(1)} %get-tuple-element.44.brief_ref), channel_id=1, source_target_pairs={{16,14},{17,15},{18,4},{19,5},{20,2},{21,3},{22,8},{23,9},{24,6},{... | collective-permute-start | bytes 983048 | tf_op jit(solution)/shard_map/ppermute | solution.py:41
  16.9 1.6 %collective-permute-start.8 = (f32[232,256]{1,0:T(8,128)S(1)}, f32[232,256]{1,0:T(8,128)S(1)}, u32[]{:S(2)}, u32[]{:S(2)}) collective-permute-start(f32[232,256]{1,0:T(8,128)S(1)} %get-tuple-element.45), channel_id=1, source_target_pairs={{16,0},{17,1},{18,2},{19,3},{20,4},{21,5},{22,6},{23,7},{24,8},{25... | collective-permute-start | bytes 712712 | tf_op jit(solution)/shard_map/ppermute | solution.py:41
  17.0 1.9 %collective-permute-start.9 = (f32[232,256]{1,0:T(8,128)S(1)}, f32[232,256]{1,0:T(8,128)S(1)}, u32[]{:S(2)}, u32[]{:S(2)}) collective-permute-start(f32[232,256]{1,0:T(8,128)S(1)} %get-tuple-element.46), channel_id=1, source_target_pairs={{16,0},{17,1},{18,2},{19,3},{20,4},{21,5},{22,6},{23,7},{24,8},{25... | collective-permute-start | bytes 712712 | tf_op jit(solution)/shard_map/ppermute | solution.py:41
  17.4 1.8 %collective-permute-start.10 = (f32[232,256]{1,0:T(8,128)S(1)}, f32[232,256]{1,0:T(8,128)S(1)}, u32[]{:S(2)}, u32[]{:S(2)}) collective-permute-start(f32[232,256]{1,0:T(8,128)S(1)} %get-tuple-element.47), channel_id=1, source_target_pairs={{16,0},{17,1},{18,2},{19,3},{20,4},{21,5},{22,6},{23,7},{24,8},{25... | collective-permute-start | bytes 712712 | tf_op jit(solution)/shard_map/ppermute | solution.py:41

commit v10 on v9

--- a/solution.py
+++ b/solution.py
@@ -89,7 +89,7 @@
 def shorten_kernel(mine_ref, short_ref, head_ref, wide, sems):
     own, width = short_ref.shape
     parts = width // LANES
-    pieces = spans(0, own, up(-(-own // 2), TILE))
+    pieces = spans(0, own, up(own, TILE))
     copies = []
     for i, (low, high) in enumerate(pieces):
         rows = pl.ds(low * parts, (high - low) * parts)

time: 25.4 us -> 25.4 us (level)
  no operation moved by 1% of the time
where the time goes in v10:
time: 25.4 us; the launch traced here: 25.2 us
  starting transfers between devices  14 us (55%)
  waiting for transfers between devices  6.03 us (24%)
  Pallas kernels  5.02 us (20%)
    ppermute x11, starting transfers between devices, route(): return lax.ppermute(array, AXES, table)  14 us
    ppermute x11, waiting for transfers between devices, route(): return lax.ppermute(array, AXES, table)  6.03 us
    pallas_call x1, Pallas kernels, shards(): pl.pallas_call(last_kernel, out_shape=shape(mine.shape, F32), in_specs=[V...  1.23 us
    pallas_call x1, Pallas kernels, shards(): pl.pallas_call(prepare_kernel, out_shape=[shape((7 * width, width), BF16)...  1.2 us
    pallas_call x1, Pallas kernels, shards(): lax.cond(lax.axis_index('sec') == 0, pl.pallas_call(shorten_kernel, out_s...  1.11 us
    pallas_call x2, Pallas kernels, ready(): pl.pallas_call(kernel, out_shape=[chunk] * 5 + [shape((6, SUB, width), F3...  1.08 us
  transfers between devices with their start and end apart: 11, of which 6 were waited for; matrix products, arithmetic and copies ran while one was open for 0% of the time, Pallas kernels for 15%

profile of v10, /device:TPU:0, one launch (start us, length us, event | category | flops | bytes accessed | tf_op | source)
XLA Modules:
  0.0 25.2 jit_solution(13407581950826305787)
XLA Ops:
  0.0 0.5 %collective-permute-start.4 = (f32[1080,128]{1,0:T(8,128)}, f32[1080,128]{1,0:T(8,128)S(1)}, u32[]{:S(2)}, u32[]{:S(2)}) collective-permute-start(f32[1080,128]{1,0:T(8,128)} %bitcast.2), channel_id=1, source_target_pairs={{0,16},{1,17},{2,18},{3,19},{4,20},{5,21},{6,22},{7,23},{8,24},{9,... | collective-permute-start | bytes 1658888 | tf_op jit(solution)/shard_map/ppermute | solution.py:41
  0.5 0.0 copy-start
  0.5 1.1 %conditional.1 = ((bf16[540,256]{1,0:T(8,128)(2,1)S(1)}, bf16[90,256]{1,0:T(8,128)(2,1)S(1)})) conditional(s32[]{:T(128)} %convert_element_type.3, () %tuple.11, f32[1080,128]{1,0:T(8,128)} %bitcast.3), branch_computations={%region_0.0_spmd, %region_1.0_spmd} | conditional | flops 3000000000 | bytes 8 | solution.py:487
  0.5 1.1 %branch_1_fun.1 = (bf16[540,256]{1,0:T(8,128)(2,1)S(1)}, bf16[90,256]{1,0:T(8,128)(2,1)S(1)}) custom-call(f32[1080,128]{1,0:T(8,128)} %mine_ref), custom_call_target="tpu_custom_call" | custom-call | flops 3000000000 | tf_op jit(solution)/shard_map/cond/branch_1_fun/pallas_call | solution.py:487
  1.6 0.0 copy-start.6
  1.6 1.6 %collective-permute-start.3 = (bf16[540,256]{1,0:T(8,128)(2,1)S(1)}, bf16[540,256]{1,0:T(8,128)(2,1)S(1)}, u32[]{:S(2)}, u32[]{:S(2)}) collective-permute-start(bf16[540,256]{1,0:T(8,128)(2,1)S(1)} %get-tuple-element.32.short_ref), channel_id=1, source_target_pairs={{0,18},{1,19},{2,16},{3,17},{4,22},{5,23},{6,20},{7,21},{8,26},{9,... | collective-permute-start | bytes 829448 | tf_op jit(solution)/shard_map/ppermute | solution.py:41
  3.2 4.2 %collective-permute-start.2 = (bf16[540,256]{1,0:T(8,128)(2,1)S(1)}, bf16[540,256]{1,0:T(8,128)(2,1)S(1)}, u32[]{:S(2)}, u32[]{:S(2)}) collective-permute-start(bf16[540,256]{1,0:T(8,128)(2,1)S(1)} %get-tuple-element.32.short_ref), channel_id=1, source_target_pairs={{0,30},{1,31},{2,20},{3,21},{4,18},{5,19},{6,24},{7,25},{8,22},{9,... | collective-permute-start | bytes 829448 | tf_op jit(solution)/shard_map/ppermute | solution.py:41
  7.3 0.0 collective-permute-done.4.other_ref.state_ref
  7.3 0.0 copy-done
  7.3 0.0 copy-start.1
  7.3 0.0 copy-start.2
  7.3 0.0 copy-start.3
  7.4 0.0 copy-start.4
  7.4 0.0 copy-start.5
  7.4 0.1 collective-permute-start.5
  7.5 0.1 collective-permute-start.1
  7.5 2.1 %collective-permute-start = (bf16[90,256]{1,0:T(8,128)(2,1)S(1)}, bf16[90,256]{1,0:T(8,128)(2,1)S(1)}, u32[]{:S(2)}, u32[]{:S(2)}) collective-permute-start(bf16[90,256]{1,0:T(8,128)(2,1)S(1)} %get-tuple-element.31.head_ref), channel_id=1, source_target_pairs={{0,31},{1,30},{2,21},{3,20},{4,19},{5,18},{6,25},{7,24},{8,23},{9,... | collective-permute-start | bytes 138248 | tf_op jit(solution)/shard_map/ppermute | solution.py:41
  9.6 0.0 copy-done.6
  9.6 0.0 copy-done.1
  9.6 0.0 copy-done.2
  9.6 0.0 copy-done.3
  9.6 0.0 copy-done.4
  9.6 0.0 copy-done.5
  9.6 1.2 %shard_map.74 = (bf16[1792,256]{1,0:T(8,128)(2,1)S(1)}, bf16[540,256]{1,0:T(8,128)(2,1)S(1)}, f32[12,256]{1,0:T(8,128)S(1)}, f32[640,256]{1,0:T(8,128)S(1)}, f32[640,256]{1,0:T(8,128)S(1)}) custom-call(f32[1080,128]{1,0:T(8,128)S(1)} %bitcast.4, bf16[540,256]{1,0:T(8,128)(2,1)S(1)} %get-tuple-element.32.short_ref, s32[3,256]{1,0:T(4,128)S(1)} %copy-done.2, ...), custom_call_target="tpu_custom_call" | custom-call | flops 10000000 | tf_op jit(solution)/shard_map/pallas_call | solution.py:520
  10.8 0.0 collective-permute-done.5.pack_ref
  10.9 0.0 collective-permute-done.3.near_ref
  10.9 0.5 %collective-permute-done.2.far_ref = bf16[540,256]{1,0:T(8,128)(2,1)S(1)} collective-permute-done((bf16[540,256]{1,0:T(8,128)(2,1)S(1)}, bf16[540,256]{1,0:T(8,128)(2,1)S(1)}, u32[]{:S(2)}, u32[]{:S(2)}) %collective-permute-start.2) | collective-permute-done | bytes 276512 | tf_op jit(solution)/shard_map/ppermute | solution.py:41
  11.4 0.0 collective-permute-done.1.dnear_ref
  11.4 0.5 %collective-permute-done.dfar_ref = bf16[90,256]{1,0:T(8,128)(2,1)S(1)} collective-permute-done((bf16[90,256]{1,0:T(8,128)(2,1)S(1)}, bf16[90,256]{1,0:T(8,128)(2,1)S(1)}, u32[]{:S(2)}, u32[]{:S(2)}) %collective-permute-start) | collective-permute-done | bytes 46112 | tf_op jit(solution)/shard_map/ppermute | solution.py:41
  11.9 1.3 %collective-permute-start.7 = (bf16[640,256]{1,0:T(8,128)(2,1)S(1)}, bf16[640,256]{1,0:T(8,128)(2,1)S(1)}, u32[]{:S(2)}, u32[]{:S(2)}) collective-permute-start(bf16[640,256]{1,0:T(8,128)(2,1)S(1)} %get-tuple-element.44.brief_ref), channel_id=1, source_target_pairs={{16,2},{17,3},{18,0},{19,1},{20,6},{21,7},{22,4},{23,5},{24,10},{2... | collective-permute-start | bytes 983048 | tf_op jit(solution)/shard_map/ppermute | solution.py:41
  13.2 3.8 %collective-permute-start.6 = (bf16[640,256]{1,0:T(8,128)(2,1)S(1)}, bf16[640,256]{1,0:T(8,128)(2,1)S(1)}, u32[]{:S(2)}, u32[]{:S(2)}) collective-permute-start(bf16[640,256]{1,0:T(8,128)(2,1)S(1)} %get-tuple-element.44.brief_ref), channel_id=1, source_target_pairs={{16,14},{17,15},{18,4},{19,5},{20,2},{21,3},{22,8},{23,9},{24,6},{... | collective-permute-start | bytes 983048 | tf_op jit(solution)/shard_map/ppermute | solution.py:41
  17.0 0.1 collective-permute-start.8
  17.0 0.4 %collective-permute-start.9 = (f32[232,256]{1,0:T(8,128)S(1)}, f32[232,256]{1,0:T(8,128)S(1)}, u32[]{:S(2)}, u32[]{:S(2)}) collective-permute-start(f32[232,256]{1,0:T(8,128)S(1)} %get-tuple-element.46), channel_id=1, source_target_pairs={{16,0},{17,1},{18,2},{19,3},{20,4},{21,5},{22,6},{23,7},{24,8},{25... | collective-permute-start | bytes 712712 | tf_op jit(solution)/shard_map/ppermute | solution.py:41
  17.5 0.1 collective-permute-start.10
  17.6 1.0 %collective-permute-done.8.rest_0_ = f32[232,256]{1,0:T(8,128)S(1)} collective-permute-done((f32[232,256]{1,0:T(8,128)S(1)}, f32[232,256]{1,0:T(8,128)S(1)}, u32[]{:S(2)}, u32[]{:S(2)}) %collective-permute-start.8) | collective-permute-done | bytes 237600 | tf_op jit(solution)/shard_map/ppermute | solution.py:41
  18.6 0.3 %collective-permute-done.9.rest_1_ = f32[232,256]{1,0:T(8,128)S(1)} collective-permute-done((f32[232,256]{1,0:T(8,128)S(1)}, f32[232,256]{1,0:T(8,128)S(1)}, u32[]{:S(2)}, u32[]{:S(2)}) %collective-permute-start.9) | collective-permute-done | bytes 237600 | tf_op jit(solution)/shard_map/ppermute | solution.py:41
  18.9 0.3 %collective-permute-done.10.rest_2_ = f32[232,256]{1,0:T(8,128)S(1)} collective-permute-done((f32[232,256]{1,0:T(8,128)S(1)}, f32[232,256]{1,0:T(8,128)S(1)}, u32[]{:S(2)}, u32[]{:S(2)}) %collective-permute-start.10) | collective-permute-done | bytes 237600 | tf_op jit(solution)/shard_map/ppermute | solution.py:41
  19.2 1.1 %shard_map.79 = (f32[12,8,256]{2,1,0:T(8,128)S(1)}, f32[12,8,256]{2,1,0:T(8,128)S(1)}, f32[12,8,256]{2,1,0:T(8,128)S(1)}, f32[12,8,256]{2,1,0:T(8,128)S(1)}, f32...) custom-call(f32[45,256]{1,0:T(8,128)S(1)} %copy-done, ...), custom_call_target="tpu_custom_call" | custom-call | tf_op jit(solution)/shard_map/pallas_call | solution.py:539
  20.3 0.0 collective-permute-done.7.near_ref
  20.3 0.4 %shard_map.80.start_ref = f32[640,256]{1,0:T(8,128)S(1)} custom-call(bf16[640,256]{1,0:T(8,128)(2,1)S(1)} %collective-permute-done.7.near_ref, f32[640,256]{1,0:T(8,128)S(1)} %get-tuple-element.48.start_ref, f32[640,256]{1,0:T(8,128)S(1)} %get-tuple-element.35.take_ref, bf16[1792,256]{1,0:T(8,128)(2,1)S(1)} %get-tuple-element.36.gather_ref), custom_call_target="tpu_custom_call" | custom-call | tf_op jit(solution)/shard_map/pallas_call | solution.py:556
  20.7 3.3 %collective-permute-done.6.far_ref = bf16[640,256]{1,0:T(8,128)(2,1)S(1)} collective-permute-done((bf16[640,256]{1,0:T(8,128)(2,1)S(1)}, bf16[640,256]{1,0:T(8,128)(2,1)S(1)}, u32[]{:S(2)}, u32[]{:S(2)}) %collective-permute-start.6) | collective-permute-done | bytes 327712 | tf_op jit(solution)/shard_map/ppermute | solution.py:41
  24.0 1.2 %shard_map.81 = f32[1080,128]{1,0:T(8,128)} custom-call(bf16[640,256]{1,0:T(8,128)(2,1)S(1)} %collective-permute-done.6.far_ref, bf16[640,256]{1,0:T(8,128)(2,1)S(1)} %get-tuple-element.44.brief_ref, f32[640,256]{1,0:T(8,128)S(1)} %shard_map.80.start_ref, bf16[540,256]{1,0:T(8,128)(2,1)S(1)} %get-tuple-element.33.lagged_ref, s32[2,256]{1,0:T(2,128)S(1)} %copy-done.1, ...), custom_call_target="tpu_custom_call" | custom-call | tf_op jit(solution)/shard_map/pallas_call | solution.py:594
  (5 shorter events, 0.1 us)
Async XLA Ops:
  0.0 7.3 %collective-permute-start.4 = (f32[1080,128]{1,0:T(8,128)}, f32[1080,128]{1,0:T(8,128)S(1)}, u32[]{:S(2)}, u32[]{:S(2)}) collective-permute-start(f32[1080,128]{1,0:T(8,128)} %bitcast.2), channel_id=1, source_target_pairs={{0,16},{1,17},{2,18},{3,19},{4,20},{5,21},{6,22},{7,23},{8,24},{9,... | collective-permute-start | bytes 1658888 | tf_op jit(solution)/shard_map/ppermute | solution.py:41
  0.5 6.9 %copy-start = (f32[45,256]{1,0:T(8,128)S(1)}, f32[45,256]{1,0:T(8,128)}, u32[]{:S(2)}) copy-start(f32[45,256]{1,0:T(8,128)} %kappa_ref.5) | copy-start | bytes 138244
  1.6 8.0 %copy-start.6 = (f32[1,12,45,256]{3,0,2,1:T(1,128)S(1)}, f32[1,12,45,256]{3,0,2,1:T(1,128)}, u32[]{:S(2)}) copy-start(f32[1,12,45,256]{3,0,2,1:T(1,128)} %param.9) | copy-start | bytes 1658884
  1.6 9.3 %collective-permute-start.3 = (bf16[540,256]{1,0:T(8,128)(2,1)S(1)}, bf16[540,256]{1,0:T(8,128)(2,1)S(1)}, u32[]{:S(2)}, u32[]{:S(2)}) collective-permute-start(bf16[540,256]{1,0:T(8,128)(2,1)S(1)} %get-tuple-element.32.short_ref), channel_id=1, source_target_pairs={{0,18},{1,19},{2,16},{3,17},{4,22},{5,23},{6,20},{7,21},{8,26},{9,... | collective-permute-start | bytes 829448 | tf_op jit(solution)/shard_map/ppermute | solution.py:41
  3.2 8.2 %collective-permute-start.2 = (bf16[540,256]{1,0:T(8,128)(2,1)S(1)}, bf16[540,256]{1,0:T(8,128)(2,1)S(1)}, u32[]{:S(2)}, u32[]{:S(2)}) collective-permute-start(bf16[540,256]{1,0:T(8,128)(2,1)S(1)} %get-tuple-element.32.short_ref), channel_id=1, source_target_pairs={{0,30},{1,31},{2,20},{3,21},{4,18},{5,19},{6,24},{7,25},{8,22},{9,... | collective-permute-start | bytes 829448 | tf_op jit(solution)/shard_map/ppermute | solution.py:41
  7.3 2.3 %copy-start.1 = (s32[2,256]{1,0:T(2,128)S(1)}, s32[2,256]{1,0:T(2,128)}, u32[]{:S(2)}) copy-start(s32[2,256]{1,0:T(2,128)} %mask_ref.3) | copy-start | bytes 6148
  7.3 2.3 %copy-start.2 = (s32[3,256]{1,0:T(4,128)S(1)}, s32[3,256]{1,0:T(4,128)}, u32[]{:S(2)}) copy-start(s32[3,256]{1,0:T(4,128)} %nbr_ref.1) | copy-start | bytes 9220
  7.3 2.3 %copy-start.3 = (f32[3,256]{1,0:T(4,128)S(1)}, f32[3,256]{1,0:T(4,128)}, u32[]{:S(2)}) copy-start(f32[3,256]{1,0:T(4,128)} %weight_ref.1) | copy-start | bytes 9220
  7.4 2.3 %copy-start.4 = (f32[12]{0:T(128)S(1)}, f32[12]{0:T(128)}, u32[]{:S(2)}) copy-start(f32[12]{0:T(128)} %relax_ref.1) | copy-start | bytes 148
  7.4 2.3 %copy-start.5 = (f32[12]{0:T(128)S(1)}, f32[12]{0:T(128)}, u32[]{:S(2)}) copy-start(f32[12]{0:T(128)} %diff_ref.1) | copy-start | bytes 148
  7.4 3.4 %collective-permute-start.5 = (bf16[5,45,256]{2,1,0:T(8,128)(2,1)S(1)}, bf16[5,45,256]{2,1,0:T(8,128)(2,1)S(1)}, u32[]{:S(2)}, u32[]{:S(2)}) collective-permute-start(bf16[5,45,256]{2,1,0:T(8,128)(2,1)S(1)} %shard_map.73), channel_id=1, source_target_pairs={{0,17},{1,16},{2,19},{3,18},{4,21},{5,20},{6,23},{7,22},{8,25},{9,... | collective-permute-start | bytes 345608 | tf_op jit(solution)/shard_map/ppermute | solution.py:41
  7.5 3.9 %collective-permute-start.1 = (bf16[90,256]{1,0:T(8,128)(2,1)S(1)}, bf16[90,256]{1,0:T(8,128)(2,1)S(1)}, u32[]{:S(2)}, u32[]{:S(2)}) collective-permute-start(bf16[90,256]{1,0:T(8,128)(2,1)S(1)} %get-tuple-element.31.head_ref), channel_id=1, source_target_pairs={{0,19},{1,18},{2,17},{3,16},{4,23},{5,22},{6,21},{7,20},{8,27},{9,... | collective-permute-start | bytes 138248 | tf_op jit(solution)/shard_map/ppermute | solution.py:41
  7.5 4.4 %collective-permute-start = (bf16[90,256]{1,0:T(8,128)(2,1)S(1)}, bf16[90,256]{1,0:T(8,128)(2,1)S(1)}, u32[]{:S(2)}, u32[]{:S(2)}) collective-permute-start(bf16[90,256]{1,0:T(8,128)(2,1)S(1)} %get-tuple-element.31.head_ref), channel_id=1, source_target_pairs={{0,31},{1,30},{2,21},{3,20},{4,19},{5,18},{6,25},{7,24},{8,23},{9,... | collective-permute-start | bytes 138248 | tf_op jit(solution)/shard_map/ppermute | solution.py:41
  11.9 8.4 %collective-permute-start.7 = (bf16[640,256]{1,0:T(8,128)(2,1)S(1)}, bf16[640,256]{1,0:T(8,128)(2,1)S(1)}, u32[]{:S(2)}, u32[]{:S(2)}) collective-permute-start(bf16[640,256]{1,0:T(8,128)(2,1)S(1)} %get-tuple-element.44.brief_ref), channel_id=1, source_target_pairs={{16,2},{17,3},{18,0},{19,1},{20,6},{21,7},{22,4},{23,5},{24,10},{2... | collective-permute-start | bytes 983048 | tf_op jit(solution)/shard_map/ppermute | solution.py:41
  13.2 10.8 %collective-permute-start.6 = (bf16[640,256]{1,0:T(8,128)(2,1)S(1)}, bf16[640,256]{1,0:T(8,128)(2,1)S(1)}, u32[]{:S(2)}, u32[]{:S(2)}) collective-permute-start(bf16[640,256]{1,0:T(8,128)(2,1)S(1)} %get-tuple-element.44.brief_ref), channel_id=1, source_target_pairs={{16,14},{17,15},{18,4},{19,5},{20,2},{21,3},{22,8},{23,9},{24,6},{... | collective-permute-start | bytes 983048 | tf_op jit(solution)/shard_map/ppermute | solution.py:41
  17.0 1.6 %collective-permute-start.8 = (f32[232,256]{1,0:T(8,128)S(1)}, f32[232,256]{1,0:T(8,128)S(1)}, u32[]{:S(2)}, u32[]{:S(2)}) collective-permute-start(f32[232,256]{1,0:T(8,128)S(1)} %get-tuple-element.45), channel_id=1, source_target_pairs={{16,0},{17,1},{18,2},{19,3},{20,4},{21,5},{22,6},{23,7},{24,8},{25... | collective-permute-start | bytes 712712 | tf_op jit(solution)/shard_map/ppermute | solution.py:41
  17.0 1.9 %collective-permute-start.9 = (f32[232,256]{1,0:T(8,128)S(1)}, f32[232,256]{1,0:T(8,128)S(1)}, u32[]{:S(2)}, u32[]{:S(2)}) collective-permute-start(f32[232,256]{1,0:T(8,128)S(1)} %get-tuple-element.46), channel_id=1, source_target_pairs={{16,0},{17,1},{18,2},{19,3},{20,4},{21,5},{22,6},{23,7},{24,8},{25... | collective-permute-start | bytes 712712 | tf_op jit(solution)/shard_map/ppermute | solution.py:41
  17.5 1.8 %collective-permute-start.10 = (f32[232,256]{1,0:T(8,128)S(1)}, f32[232,256]{1,0:T(8,128)S(1)}, u32[]{:S(2)}, u32[]{:S(2)}) collective-permute-start(f32[232,256]{1,0:T(8,128)S(1)} %get-tuple-element.47), channel_id=1, source_target_pairs={{16,0},{17,1},{18,2},{19,3},{20,4},{21,5},{22,6},{23,7},{24,8},{25... | collective-permute-start | bytes 712712 | tf_op jit(solution)/shard_map/ppermute | solution.py:41
